TPU v7x, 32 devices: a whole 2x2x4 slice. The times are simulated.
32 devices in a mesh: grp: 2 (over x), rp: 8 (over z, y), re: 2 (over core).
Axes of the slice: x: 2, y: 2, z: 4, core: 2. Of those that a mesh axis runs over, the one named last changes fastest.
Arguments:
- weights: bfloat16 [2, 256, 8, 48, 256], P(None, 'rp', 're'), may hold values from -0.125 to 0.125
- rp_vectors: int32 [3, 256], P(None, 'rp'), may hold values from -6 to 6, as said below
- re_vectors: int32 [3, 8], replicated, may hold values from -6 to 6, as said below
- q_points: int32 [3, 16], P(None, 'grp'), parts along dimension 1, may hold values from 0 to 47
- k_points: int32 [3, 4], P(None, 'grp'), parts along dimension 1, may hold values from 0 to 47
- eigvecs: float32 [16, 2, 48, 48], P(('grp', 'rp')), parts along dimension 0, may hold values from -0.625 to 0.625
Outputs:
- bloch_out: bfloat16 [16, 2, 2, 48, 256], P(('grp', 'rp'), None, 're'), parts along dimension 0
There are 2 independent parts, one for each index of `grp`. A program takes and returns all parts, laid end to end along the dimension named above; an argument that names none is the same for every part. Nothing has to cross between parts.
Inputs may be any that keep to these rules, and one draw needn't show every extreme that they name: `rp_vectors`: distinct integer lattice vectors, no two columns equal. `re_vectors`: distinct integer lattice vectors, no two columns equal.
All inputs are finite; a program needn't handle non-finite values.
Results may differ from a plain program's by a relative error of at most 0.0038.
Values may be sent and summed in bfloat16 or wider, within the bound.
No kernel may reach another device: no remote copies, remote signals or barrier semaphores. Data moves between devices by JAX's collectives and lax.ppermute only.
A program may use at most 128 MiB of HBM per device.

v0:
```python
import math

import jax
import jax.numpy as jnp
from jax import lax
from jax.sharding import PartitionSpec as P

NFINE = 48


def phase_pair(points, vectors):
    products = jnp.sum(points[:, :, None] * vectors[:, None, :], axis=0)
    wrapped = jnp.mod(products, NFINE)
    angles = wrapped.astype(jnp.float32) * (2.0 * math.pi / NFINE)
    return (jnp.cos(angles), jnp.sin(angles))


def rp_product(cosine_rows, sine_rows, flat_rows):
    cos_half = cosine_rows.astype(jnp.bfloat16)
    sin_half = sine_rows.astype(jnp.bfloat16)
    upper_rows = jnp.concatenate([cos_half, -sin_half], axis=1)
    lower_rows = jnp.concatenate([sin_half, cos_half], axis=1)
    stacked = jnp.stack([upper_rows, lower_rows], axis=1).reshape(-1, upper_rows.shape[1])
    return jnp.dot(stacked, flat_rows, preferred_element_type=jnp.float32)


def mix_modes(operand, rotation):
    return jnp.einsum("qenm,qnv->qevm", operand, rotation, precision=lax.Precision.HIGHEST)


def rotate(source, vectors):
    real_part = mix_modes(source[:, 0], vectors[:, 0]) - mix_modes(source[:, 1], vectors[:, 1])
    imag_part = mix_modes(source[:, 0], vectors[:, 1]) + mix_modes(source[:, 1], vectors[:, 0])
    return jnp.stack([real_part, imag_part], axis=1)


def contract(matrix, values):
    return jnp.einsum("ke,qenm->qknm", matrix, values, precision=lax.Precision.HIGHEST)


def k_sum(phase_cos, phase_sin, source):
    real_part = contract(phase_cos, source[:, 0]) - contract(phase_sin, source[:, 1])
    imag_part = contract(phase_sin, source[:, 0]) + contract(phase_cos, source[:, 1])
    return jnp.stack([real_part, imag_part], axis=1)


def shards(weights, rp_vectors, re_vectors, q_points, k_points, eigvecs):
    local_rows = eigvecs.shape[0]
    slab_size = weights.shape[2]
    mode_count = weights.shape[3]
    pair_count = weights.shape[4]
    flat_rows = weights.reshape(2 * weights.shape[1], slab_size * mode_count * pair_count)
    own_start = lax.axis_index("re") * slab_size
    own_vectors = lax.dynamic_slice_in_dim(re_vectors, own_start, slab_size, 1)
    slab_cos, slab_sin = phase_pair(k_points, own_vectors)
    rp_cosine, rp_sine = phase_pair(q_points, rp_vectors)
    product = rp_product(rp_cosine, rp_sine, flat_rows)
    summed = lax.psum_scatter(
        product.reshape(local_rows * lax.axis_size("rp"), 2, slab_size, mode_count, pair_count),
        "rp",
        scatter_dimension=0,
        tiled=True,
    )
    rotated = rotate(summed, eigvecs)
    partial_value = k_sum(slab_cos, slab_sin, rotated)
    bloch_sum = lax.psum_scatter(partial_value, "re", scatter_dimension=2, tiled=True)
    return bloch_sum.astype(jnp.bfloat16)


def solution(mesh):
    return jax.shard_map(
        shards,
        mesh=mesh,
        in_specs=(
            P(None, "rp", "re", None, None),
            P(None, "rp"),
            P(),
            P(None, "grp"),
            P(None, "grp"),
            P(("grp", "rp"), None, None, None),
        ),
        out_specs=P(("grp", "rp"), None, "re", None, None),
        check_vma=False,
    )
```

profile of v0, /device:TPU:0, one launch (start us, length us, event | category | flops | bytes accessed | tf_op | source)
XLA Modules:
  0.0 128.2 jit_solution(1723295692915078214)
XLA Ops:
  6.5 0.8 multiply_reduce_fusion
  7.3 0.1 fusion.40
  7.4 0.1 cosine_convert_fusion
  7.4 9.0 %reshape.56 = bf16[64,49152]{1,0:T(8,128)(2,1)} reshape(bf16[2,32,4,48,256]{4,3,2,1,0:T(8,128)(2,1)} %param.6) | data formatting | bytes 12582912 | tf_op jit(solution)/shard_map/reshape | solution.py:52
  16.4 4.5 %copy.49 = bf16[8,8,192,256]{3,2,1,0:T(8,128)(2,1)S(1)} copy(bf16[8,8,192,256]{3,1,2,0:T(8,128)(2,1)} %bitcast.87) | data formatting | bytes 12582912
  20.9 0.1 maximum_bitcast_fusion.2
  21.0 3.5 %fusion = f32[8,2,4,48,256]{4,0,3,2,1:T(8,128)S(1)} fusion(bf16[4,48,256,64]{2,1,0,3:T(8,128)(2,1)S(1)} %bitcast.86, bf16[8,1,64]{2,0,1:T(8,128)(2,1)S(1)} %get-tuple-element.8, bf16[8,1,64]{2,0,1:T(8,128)(2,1)S(1)} %get-tuple-element.7), kind=kOutput, calls=%fused_computation | convolution fusion | flops 100667392 | bytes 9439232 | tf_op jit(solution)/shard_map/dot_general | solution.py:24
  24.5 2.6 %copy.36 = f32[8,2,4,48,256]{4,3,2,1,0:T(8,128)} copy(f32[8,2,4,48,256]{4,0,3,2,1:T(8,128)S(1)} %fusion) | data formatting | bytes 6291456 | tf_op jit(solution)/shard_map/dot_general | solution.py:24
  27.2 0.1 copy.39
  27.3 0.1 constant_dynamic-slice_fusion
  27.4 0.1 multiply_reduce_fusion.1
  27.4 77.0 %reduce-scatter.3.cloned.1.call-done = f32[1,2,4,48,256]{4,3,2,1,0:T(8,128)} async-done(((f32[8,2,4,48,256]{4,3,2,1,0:T(8,128)}), f32[1,2,4,48,256]{4,3,2,1,0:T(8,128)}) %reduce-scatter.3.cloned.1.call-update) | async-done | bytes 393232 | tf_op jit(solution)/shard_map/reduce_scatter | solution.py:58
  104.4 1.3 fusion.8
  105.7 1.3 %fusion.4 = f32[4,48,256]{2,1,0:T(8,128)S(1)} fusion(f32[4,256,48]{1,2,0:T(8,128)S(1)} %fusion.8, f32[1,2,4,48,256]{4,3,2,1,0:T(8,128)} %reduce-scatter.3.cloned.1.call-done, f32[1,2,48,48]{3,2,1,0:T(8,128)S(1)} %copy-done.1), kind=kOutput, calls=%fused_computation.6 | convolution fusion | flops 28360704 | bytes 614400 | tf_op jit(solution)/shard_map/qenm,qnv->qevm/dot_general | solution.py:28
  107.0 0.6 fusion.11
  107.6 0.6 fusion.13
  108.2 1.3 fusion.7
  109.4 1.3 %fusion.3 = f32[4,48,256]{2,1,0:T(8,128)S(1)} fusion(f32[4,256,48]{1,2,0:T(8,128)S(1)} %fusion.7, f32[1,2,4,48,256]{4,3,2,1,0:T(8,128)} %reduce-scatter.3.cloned.1.call-done, f32[1,2,48,48]{3,2,1,0:T(8,128)S(1)} %copy-done.1), kind=kOutput, calls=%fused_computation.4 | convolution fusion | flops 28360704 | bytes 614400 | tf_op jit(solution)/shard_map/qenm,qnv->qevm/dot_general | solution.py:28
  110.7 0.6 fusion.5
  111.3 0.6 fusion.6
  111.9 0.1 pad_maximum_fusion
  112.0 0.7 copy.44
  112.7 7.1 %reduce-scatter.5.cloned.1.call-done = f32[1,2,1,48,256]{4,3,1,0,2:T(8,128)} async-done(((f32[1,2,2,48,256]{4,3,1,0,2:T(8,128)}), f32[1,2,1,48,256]{4,3,1,0,2:T(8,128)}) %reduce-scatter.5.cloned.1.call-update) | async-done | bytes 98320 | tf_op jit(solution)/shard_map/reduce_scatter | solution.py:66
  119.8 1.5 %convert_bitcast_fusion = bf16[1,2,1,48,256]{4,3,2,1,0:T(8,128)(2,1)} fusion(f32[1,2,1,48,256]{4,3,1,0,2:T(8,128)} %reduce-scatter.5.cloned.1.call-done), kind=kLoop, calls=%fused_computation.22 | loop fusion | flops 24576 | bytes 147456 | tf_op jit(solution)/shard_map/convert_element_type | solution.py:67
  (10 shorter events, 0.1 us)
Async XLA Ops:
  6.5 20.7 %copy-start = (s32[3,8]{1,0:T(4,128)S(1)}, s32[3,8]{1,0:T(4,128)}, u32[]{:S(2)}) copy-start(s32[3,8]{1,0:T(4,128)} %param.8) | copy-start | bytes 292
  6.5 97.9 %reduce-scatter.3.cloned.1.call-start = ((), (), s32[]{:S(2)}) async-start(), calls=%async_computation.2 | async-start | bytes 3538944 | tf_op jit(solution)/shard_map/reduce_scatter | solution.py:58
  24.5 2.7 %copy-start.2 = (s32[3,2]{0,1:T(2,128)S(1)}, s32[3,2]{0,1:T(2,128)}, u32[]{:S(2)}) copy-start(s32[3,2]{0,1:T(2,128)} %param.10) | copy-start | bytes 76
  24.5 79.9 %copy-start.1 = (f32[1,2,48,48]{3,2,1,0:T(8,128)S(1)}, f32[1,2,48,48]{3,2,1,0:T(8,128)}, u32[]{:S(2)}) copy-start(f32[1,2,48,48]{3,2,1,0:T(8,128)} %param.11) | copy-start | bytes 55300
  27.1 92.7 %reduce-scatter.5.cloned.1.call-start = ((), (), s32[]{:S(2)}) async-start(), calls=%async_computation.3 | async-start | bytes 294912 | tf_op jit(solution)/shard_map/reduce_scatter | solution.py:66
Sparse Core Ops, SparseCore 0:
  27.2 77.1 reduce-scatter.2
  112.9 6.8 reduce-scatter.4
where the time goes:
time: 129 us; the launch traced here: 128 us
  waiting for transfers between devices  84 us (65%)
  local copies, waits for them, and re-layouts  16.9 us (13%)
  between operations  13.5 us (10%)
  matrix products  11 us (9%)
  other arithmetic  2.66 us (2%)
    reduce_scatter x1, waiting for transfers between devices, shards(): lax.psum_scatter(product.reshape(local_rows * lax.axis_size('rp'), 2, sla...  77 us
    reshape x1, local copies, waits for them, and re-layouts, shards(): weights.reshape(2 * weights.shape[1], slab_size * mode_count * pair_count)  9 us
    reduce_scatter x1, waiting for transfers between devices, shards(): lax.psum_scatter(partial_value, 're', scatter_dimension=2, tiled=True)  7.06 us
    dot_general x4, matrix products, mix_modes(): jnp.einsum('qenm,qnv->qevm', operand, rotation, precision=lax.Precision.H...  5.12 us
    unnamed x8, local copies, waits for them, and re-layouts  4.56 us
    dot_general x1, matrix products, rp_product(): return jnp.dot(stacked, flat_rows, preferred_element_type=jnp.float32)  3.49 us
    dot_general x1, local copies, waits for them, and re-layouts, rp_product(): return jnp.dot(stacked, flat_rows, preferred_element_type=jnp.float32)  2.63 us
  transfers between devices with their start and end apart: 2, of which 2 were waited for; matrix products, arithmetic and copies ran while one was open for 0% of the time, Pallas kernels for 0%

commit v1 on v0

v1 whole, which is shorter than its diff:
```python
import math

import jax
import jax.numpy as jnp
from jax import lax
from jax.experimental import pallas as pl
from jax.experimental.pallas import tpu as pltpu
from jax.sharding import PartitionSpec as P

NFINE = 48
ROWS = 16


def bit_order(bits, core):
    order = list(range(bits))
    if bits > 1 and core == 1:
        order[0], order[1] = order[1], order[0]
    return order


def swap_slot(slot, bits):
    if bits < 2:
        return slot
    high, low = (slot >> (bits - 1)) & 1, (slot >> (bits - 2)) & 1
    rest = slot & ((1 << (bits - 2)) - 1)
    return (low << (bits - 1)) | (high << (bits - 2)) | rest


def wrapped_angle(products):
    turns = jnp.floor((products + 0.5) * (1.0 / NFINE))
    return (products - NFINE * turns) * (2.0 * math.pi / NFINE)


def phase_kernel(bits, rp_name, re_name, q_ref, k_ref, ev_ref, rpv_ref, w_ref, keep_ref, send_ref, slabs, lhs, prod, sems):
    parts, points, slab, modes, pairs = w_ref.shape
    slots = keep_ref.shape[0]
    per_core = keep_ref.shape[1]
    chunks = modes // ROWS

    def fetch(c, e):
        return pltpu.make_async_copy(
            w_ref.at[:, :, e, pl.ds(c * ROWS, ROWS), :], slabs.at[c, e], sems.at[c, e]
        )

    for c in range(chunks):
        for e in range(slab):
            fetch(c, e).start()

    me = lax.axis_index(rp_name)
    core = lax.axis_index(re_name)
    width = points * ROWS
    spread = (
        lax.broadcasted_iota(jnp.int32, (points, width), 1) // ROWS
        == lax.broadcasted_iota(jnp.int32, (points, width), 0)
    ).astype(jnp.bfloat16)
    vectors = jnp.dot(rpv_ref[...].astype(jnp.bfloat16), spread, preferred_element_type=jnp.float32)
    rows = []
    for slot in range(slots):
        offset = 0
        for at, (one, other) in enumerate(zip(bit_order(bits, 0), bit_order(bits, 1))):
            if (slot >> (bits - 1 - at)) & 1:
                offset = offset + jnp.where(core == 0, 1 << one, 1 << other)
        q = me ^ offset
        row = 0.0
        for axis in range(3):
            row = row + q_ref[axis, q].astype(jnp.float32) * vectors[axis : axis + 1, :]
        rows.append(row)
    angles = wrapped_angle(jnp.concatenate(rows, axis=0))
    cosine, sine = jnp.cos(angles), jnp.sin(angles)
    diagonal = (
        lax.broadcasted_iota(jnp.int32, (ROWS, width), 1) % ROWS
        == lax.broadcasted_iota(jnp.int32, (ROWS, width), 0)
    ).astype(jnp.float32)
    for slot in range(slots):
        cos_block = (cosine[slot : slot + 1] * diagonal).astype(jnp.bfloat16)
        sin_block = (sine[slot : slot + 1] * diagonal).astype(jnp.bfloat16)
        top, bottom = pl.ds(2 * slot * ROWS, ROWS), pl.ds((2 * slot + 1) * ROWS, ROWS)
        lhs[top, :width] = cos_block
        lhs[top, width:] = -sin_block
        lhs[bottom, :width] = sin_block
        lhs[bottom, width:] = cos_block

    places = (2 * per_core, slab)
    at_row = lax.broadcasted_iota(jnp.int32, places, 0)
    at_lane = lax.broadcasted_iota(jnp.int32, places, 1)
    products = jnp.zeros(places, jnp.float32)
    for side in range(2):
        for i in range(per_core):
            k = (core ^ side) * per_core + i
            for e in range(slab):
                total = 0
                for axis in range(3):
                    total = total + k_ref[axis, k] * ev_ref[axis, core * slab + e]
                here = (at_row == side * per_core + i) & (at_lane == e)
                products = jnp.where(here, total.astype(jnp.float32), products)
    k_angles = wrapped_angle(products)
    k_cos, k_sin = jnp.cos(k_angles), jnp.sin(k_angles)

    for c in range(chunks):
        for e in range(slab):
            fetch(c, e).wait()
            block = slabs[c, e].reshape(parts * width, pairs)
            prod[e] = jnp.dot(lhs[...], block, preferred_element_type=jnp.float32)
        for side in range(2):
            for i in range(per_core):
                line = side * per_core + i
                for slot in range(slots):
                    real = imag = None
                    for e in range(slab):
                        cos_e = jnp.broadcast_to(k_cos[line : line + 1, e : e + 1], (ROWS, pairs))
                        sin_e = jnp.broadcast_to(k_sin[line : line + 1, e : e + 1], (ROWS, pairs))
                        p_real = prod[e, pl.ds(2 * slot * ROWS, ROWS), :]
                        p_imag = prod[e, pl.ds((2 * slot + 1) * ROWS, ROWS), :]
                        r_term = cos_e * p_real - sin_e * p_imag
                        i_term = sin_e * p_real + cos_e * p_imag
                        real = r_term if real is None else real + r_term
                        imag = i_term if imag is None else imag + i_term
                    where = pl.ds(c * ROWS, ROWS)
                    if side == 0:
                        keep_ref[slot, i, 0, where, :] = real
                        keep_ref[slot, i, 1, where, :] = imag
                    else:
                        there = swap_slot(slot, bits)
                        send_ref[there, i, 0, where, :] = real.astype(send_ref.dtype)
                        send_ref[there, i, 1, where, :] = imag.astype(send_ref.dtype)


def rotate_kernel(mine_ref, got_ref, eig_ref, out_ref):
    real_vec, imag_vec = eig_ref[0, 0], eig_ref[0, 1]

    def mix(vec, source):
        return lax.dot_general(
            vec, source, (((0,), (0,)), ((), ())),
            precision=lax.Precision.HIGHEST, preferred_element_type=jnp.float32,
        )

    for i in range(mine_ref.shape[1]):
        real = mine_ref[0, i, 0] + got_ref[0, i, 0].astype(jnp.float32)
        imag = mine_ref[0, i, 1] + got_ref[0, i, 1].astype(jnp.float32)
        out_ref[0, 0, i] = (mix(real_vec, real) - mix(imag_vec, imag)).astype(out_ref.dtype)
        out_ref[0, 1, i] = (mix(imag_vec, real) + mix(real_vec, imag)).astype(out_ref.dtype)


def make_shards(mesh):
    ranks, cores = mesh.shape["rp"], mesh.shape["re"]
    bits = ranks.bit_length() - 1
    vmem = pl.BlockSpec(memory_space=pltpu.VMEM)
    smem = pl.BlockSpec(memory_space=pltpu.SMEM)

    def shards(weights, rp_vectors, re_vectors, q_points, k_points, eigvecs):
        parts, points, slab, modes, pairs = weights.shape
        slots = q_points.shape[1]
        per_core = k_points.shape[1] // cores
        chunks = modes // ROWS
        shape = (slots, per_core, 2, modes, pairs)
        keep, send = pl.pallas_call(
            lambda *refs: phase_kernel(bits, "rp", "re", *refs),
            out_shape=(jax.ShapeDtypeStruct(shape, jnp.float32), jax.ShapeDtypeStruct(shape, jnp.bfloat16)),
            in_specs=[smem, smem, smem, vmem, pl.BlockSpec(memory_space=pl.ANY)],
            out_specs=(vmem, vmem),
            scratch_shapes=[
                pltpu.VMEM((chunks, slab, parts, points, ROWS, pairs), jnp.bfloat16),
                pltpu.VMEM((2 * slots * ROWS, parts * points * ROWS), jnp.bfloat16),
                pltpu.VMEM((slab, 2 * slots * ROWS, pairs), jnp.float32),
                pltpu.SemaphoreType.DMA((chunks, slab)),
            ],
            compiler_params=pltpu.CompilerParams(vmem_limit_bytes=40 * 2**20),
            name="phase_sums",
        )(q_points, k_points, re_vectors, rp_vectors, weights)
        got = lax.ppermute(send, "re", [(c, c ^ 1) for c in range(cores)])
        mine = keep
        for step in range(bits):
            half = mine.shape[0] // 2
            total = mine + got.astype(jnp.float32)
            mine, away = total[:half], total[half:].astype(jnp.bfloat16)
            pairs_of = [
                (r * cores + c, (r ^ (1 << bit_order(bits, c)[step])) * cores + c)
                for r in range(ranks)
                for c in range(cores)
            ]
            got = lax.ppermute(away, ("rp", "re"), pairs_of)
        return pl.pallas_call(
            rotate_kernel,
            out_shape=jax.ShapeDtypeStruct((1, 2, per_core, modes, pairs), jnp.bfloat16),
            in_specs=[vmem, vmem, vmem],
            out_specs=vmem,
            name="rotate_modes",
        )(mine, got, eigvecs)

    return shards


def solution(mesh):
    return jax.shard_map(
        make_shards(mesh),
        mesh=mesh,
        in_specs=(
            P(None, "rp", "re", None, None),
            P(None, "rp"),
            P(),
            P(None, "grp"),
            P(None, "grp"),
            P(("grp", "rp"), None, None, None),
        ),
        out_specs=P(("grp", "rp"), None, "re", None, None),
        check_vma=False,
    )
```

time: 129 us -> 34.5 us (0.27)
  waiting for transfers between devices: 84 us -> 9.02 us
  between operations: 13.5 us -> 0.06 us
  matrix products: 11 us -> 0 us
  local copies, waits for them, and re-layouts: 16.9 us -> 6.9 us
  Pallas kernels: 0 us -> 9.35 us
  starting transfers between devices: 0.04 us -> 8.71 us
  other arithmetic: 2.66 us -> 0.16 us
    reduce_scatter x2 -> x0, waiting for transfers between devices: 84 us -> none  [the longest x1 77 us: shards(): lax.psum_scatter(product.reshape(local_rows * lax.axis_size('rp'), 2, sla...]
    dot_general x9 -> x0, matrix products: 11 us -> none  [the longest x4 5.12 us: mix_modes(): jnp.einsum('qenm,qnv->qevm', operand, rotation, precision=lax.Precision.H...]
    pallas_call x0 -> x2, Pallas kernels: none -> 9.35 us  [the longest x1 7.45 us: shards(): pl.pallas_call(lambda *refs: phase_kernel(bits, 'rp', 're', *refs), out_s...]
    ppermute x0 -> x4, waiting for transfers between devices: none -> 9.02 us  [the longest x3 7.67 us: shards(): got = lax.ppermute(away, ('rp', 're'), pairs_of)]
    reshape x1 -> x0, local copies, waits for them, and re-layouts: 9 us -> none  [shards(): weights.reshape(2 * weights.shape[1], slab_size * mode_count * pair_count)]
    ppermute x0 -> x4, starting transfers between devices: none -> 8.71 us  [the longest x3 8.19 us: shards(): got = lax.ppermute(away, ('rp', 're'), pairs_of)]
    dot_general x1 -> x0, local copies, waits for them, and re-layouts: 2.63 us -> none  [rp_product(): return jnp.dot(stacked, flat_rows, preferred_element_type=jnp.float32)]
    unnamed x8 -> x11, local copies, waits for them, and re-layouts: 4.56 us -> 6.21 us
  transfers between devices with their start and end apart: 2 -> 4, of which waited for: 2 -> 4; matrix products, arithmetic and copies ran while one was open for 0% -> 2% of each run, Pallas kernels for 0% -> 0%
where the time goes in v1:
time: 34.5 us; the launch traced here: 34.2 us
  Pallas kernels  9.35 us (27%)
  waiting for transfers between devices  9.02 us (26%)
  starting transfers between devices  8.71 us (25%)
  local copies, waits for them, and re-layouts  6.9 us (20%)
    ppermute x3, starting transfers between devices, shards(): got = lax.ppermute(away, ('rp', 're'), pairs_of)  8.19 us
    ppermute x3, waiting for transfers between devices, shards(): got = lax.ppermute(away, ('rp', 're'), pairs_of)  7.67 us
    pallas_call x1, Pallas kernels, shards(): pl.pallas_call(lambda *refs: phase_kernel(bits, 'rp', 're', *refs), out_s...  7.45 us
    unnamed x11, local copies, waits for them, and re-layouts  6.21 us
    pallas_call x1, Pallas kernels, shards(): pl.pallas_call(rotate_kernel, out_shape=jax.ShapeDtypeStruct((1, 2, per_c...  1.9 us
    ppermute x1, waiting for transfers between devices, shards(): got = lax.ppermute(send, 're', [(c, c ^ 1) for c in range(cores)])  1.35 us
  transfers between devices with their start and end apart: 4, of which 4 were waited for; matrix products, arithmetic and copies ran while one was open for 2% of the time, Pallas kernels for 0%

profile of v1, /device:TPU:0, one launch (start us, length us, event | category | flops | bytes accessed | tf_op | source)
XLA Modules:
  0.0 34.2 jit_solution(3634009348889334408)
XLA Ops:
  0.0 0.8 %copy.7.refs_1_ = s32[3,2]{1,0:T(4,128)S(1)} copy(s32[3,2]{0,1:T(2,128)} %param.10) | data formatting | bytes 48 | tf_op args[4]
  0.8 0.0 copy-start
  0.8 2.8 %copy-done = bf16[2,32,4,48,256]{4,3,2,1,0:T(8,128)(2,1)S(1)} copy-done((bf16[2,32,4,48,256]{4,3,2,1,0:T(8,128)(2,1)S(1)}, bf16[2,32,4,48,256]{4,3,2,1,0:T(8,128)(2,1)}, u32[]{:S(2)}) %copy-start) | copy-done | bytes 6291480
  3.6 0.0 copy-start.1
  3.6 0.7 %copy-done.1 = s32[3,8]{1,0:T(4,128)S(1)} copy-done((s32[3,8]{1,0:T(4,128)S(1)}, s32[3,8]{1,0:T(4,128)}, u32[]{:S(2)}) %copy-start.1) | copy-done | bytes 120
  4.2 0.0 copy-start.2
  4.2 0.7 %copy-done.2 = s32[3,8]{1,0:T(4,128)S(1)} copy-done((s32[3,8]{1,0:T(4,128)S(1)}, s32[3,8]{1,0:T(4,128)}, u32[]{:S(2)}) %copy-start.2) | copy-done | bytes 120
  4.9 0.0 copy-start.3
  4.9 0.7 %copy-done.3 = s32[3,32]{1,0:T(4,128)S(1)} copy-done((s32[3,32]{1,0:T(4,128)S(1)}, s32[3,32]{1,0:T(4,128)}, u32[]{:S(2)}) %copy-start.3) | copy-done | bytes 408
  5.6 7.5 %phase_sums.1 = (f32[8,1,2,48,256]{4,3,2,1,0:T(8,128)S(1)}, bf16[8,1,2,48,256]{4,3,2,1,0:T(8,128)(2,1)S(1)}) custom-call(s32[3,8]{1,0:T(4,128)S(1)} %copy-done.1, s32[3,2]{1,0:T(4,128)S(1)} %copy.7.refs_1_, s32[3,8]{1,0:T(4,128)S(1)} %copy-done.2, s32[3,32]{1,0:T(4,128)S(1)} %copy-done.3, bf16[2,32,4,48,256]{4,3,2,1,0:T(8,128)(2,1)S(1)} %copy-done), custom_call_target="tpu_custom_call" | custom-call | tf_op jit(solution)/shard_map/phase_sums/pallas_call | solution.py:156
  13.1 0.5 %collective-permute-start = (bf16[8,1,2,48,256]{4,3,2,1,0:T(8,128)(2,1)S(1)}, bf16[8,1,2,48,256]{4,3,2,1,0:T(8,128)(2,1)S(1)}, u32[]{:S(2)}, u32[]{:S(2)}) collective-permute-start(bf16[8,1,2,48,256]{4,3,2,1,0:T(8,128)(2,1)S(1)} %get-tuple-element.8), channel_id=1, source_target_pairs={{0,1},{1,0},{2,3},{3,2},{4,5},{5,4},{6,7},{7,6},{8,9},{9,8},{10,11... | collective-permute-start | bytes 1179656 | tf_op jit(solution)/shard_map/ppermute | solution.py:170
  13.6 1.3 %collective-permute-done = bf16[8,1,2,48,256]{4,3,2,1,0:T(8,128)(2,1)S(1)} collective-permute-done((bf16[8,1,2,48,256]{4,3,2,1,0:T(8,128)(2,1)S(1)}, bf16[8,1,2,48,256]{4,3,2,1,0:T(8,128)(2,1)S(1)}, u32[]{:S(2)}, u32[]{:S(2)}) %collective-permute-start) | collective-permute-done | bytes 393248 | tf_op jit(solution)/shard_map/ppermute | solution.py:170
  14.9 0.1 convert_add_fusion
  15.1 3.0 %collective-permute-start.1 = (bf16[4,1,2,48,256]{4,3,2,1,0:T(8,128)(2,1)S(1)}, bf16[4,1,2,48,256]{4,3,2,1,0:T(8,128)(2,1)S(1)}, u32[]{:S(2)}, u32[]{:S(2)}) collective-permute-start(bf16[4,1,2,48,256]{4,3,2,1,0:T(8,128)(2,1)S(1)} %slice.38), channel_id=1, source_target_pairs={{0,2},{1,5},{2,0},{3,7},{4,6},{5,1},{6,4},{7,3},{8,10},{9,13},{10,... | collective-permute-start | bytes 589832 | tf_op jit(solution)/shard_map/ppermute | solution.py:181
  18.0 3.6 %collective-permute-done.1 = bf16[4,1,2,48,256]{4,3,2,1,0:T(8,128)(2,1)S(1)} collective-permute-done((bf16[4,1,2,48,256]{4,3,2,1,0:T(8,128)(2,1)S(1)}, bf16[4,1,2,48,256]{4,3,2,1,0:T(8,128)(2,1)S(1)}, u32[]{:S(2)}, u32[]{:S(2)}) %collective-permute-start.1) | collective-permute-done | bytes 196640 | tf_op jit(solution)/shard_map/ppermute | solution.py:181
  21.7 2.1 %collective-permute-start.2 = (bf16[2,1,2,48,256]{4,3,2,1,0:T(8,128)(2,1)S(1)}, bf16[2,1,2,48,256]{4,3,2,1,0:T(8,128)(2,1)S(1)}, u32[]{:S(2)}, u32[]{:S(2)}) collective-permute-start(bf16[2,1,2,48,256]{4,3,2,1,0:T(8,128)(2,1)S(1)} %slice.39), channel_id=1, source_target_pairs={{0,4},{1,3},{2,6},{3,1},{4,0},{5,7},{6,2},{7,5},{8,12},{9,11},{10,... | collective-permute-start | bytes 294920 | tf_op jit(solution)/shard_map/ppermute | solution.py:181
  23.9 2.6 %collective-permute-done.2 = bf16[2,1,2,48,256]{4,3,2,1,0:T(8,128)(2,1)S(1)} collective-permute-done((bf16[2,1,2,48,256]{4,3,2,1,0:T(8,128)(2,1)S(1)}, bf16[2,1,2,48,256]{4,3,2,1,0:T(8,128)(2,1)S(1)}, u32[]{:S(2)}, u32[]{:S(2)}) %collective-permute-start.2) | collective-permute-done | bytes 98336 | tf_op jit(solution)/shard_map/ppermute | solution.py:181
  26.5 3.1 %collective-permute-start.3 = (bf16[1,1,2,48,256]{4,3,2,1,0:T(8,128)(2,1)S(1)}, bf16[1,1,2,48,256]{4,3,2,1,0:T(8,128)(2,1)S(1)}, u32[]{:S(2)}, u32[]{:S(2)}) collective-permute-start(bf16[1,1,2,48,256]{4,3,2,1,0:T(8,128)(2,1)S(1)} %slice.40), channel_id=1, source_target_pairs={{0,8},{1,9},{2,10},{3,11},{4,12},{5,13},{6,14},{7,15},{8,0},{9,1},... | collective-permute-start | bytes 147464 | tf_op jit(solution)/shard_map/ppermute | solution.py:181
  29.6 0.6 %slice.31.mine_ref = f32[1,1,2,48,256]{4,3,2,1,0:T(8,128)} slice(f32[2,1,2,48,256]{4,3,2,1,0:T(8,128)S(1)} %slice_add_fusion.1), slice={[0:1], [0:1], [0:2], [0:48], [0:256]} | slice | bytes 196608 | tf_op jit(solution)/shard_map/slice | solution.py:175
  30.3 1.4 %collective-permute-done.3.got_ref = bf16[1,1,2,48,256]{4,3,2,1,0:T(8,128)(2,1)S(1)} collective-permute-done((bf16[1,1,2,48,256]{4,3,2,1,0:T(8,128)(2,1)S(1)}, bf16[1,1,2,48,256]{4,3,2,1,0:T(8,128)(2,1)S(1)}, u32[]{:S(2)}, u32[]{:S(2)}) %collective-permute-start.3) | collective-permute-done | bytes 49184 | tf_op jit(solution)/shard_map/ppermute | solution.py:181
  31.7 0.0 copy-start.4
  31.7 0.6 %copy-done.4 = bf16[1,1,2,48,256]{4,3,2,1,0:T(8,128)(2,1)} copy-done((bf16[1,1,2,48,256]{4,3,2,1,0:T(8,128)(2,1)}, bf16[1,1,2,48,256]{4,3,2,1,0:T(8,128)(2,1)S(1)}, u32[]{:S(2)}) %copy-start.4) | copy-done | bytes 49176
  32.3 1.9 %rotate_modes.1 = bf16[1,2,1,48,256]{4,3,2,1,0:T(8,128)(2,1)} custom-call(f32[1,1,2,48,256]{4,3,2,1,0:T(8,128)} %slice.31.mine_ref, bf16[1,1,2,48,256]{4,3,2,1,0:T(8,128)(2,1)} %copy-done.4, f32[1,2,48,48]{3,2,1,0:T(8,128)} %eig_ref.1), custom_call_target="tpu_custom_call" | custom-call | tf_op jit(solution)/shard_map/rotate_modes/pallas_call | solution.py:182
  (5 shorter events, 0.1 us)
Async XLA Ops:
  0.8 2.8 %copy-start = (bf16[2,32,4,48,256]{4,3,2,1,0:T(8,128)(2,1)S(1)}, bf16[2,32,4,48,256]{4,3,2,1,0:T(8,128)(2,1)}, u32[]{:S(2)}) copy-start(bf16[2,32,4,48,256]{4,3,2,1,0:T(8,128)(2,1)} %refs_4_.1) | copy-start | bytes 18874372
  3.6 0.7 %copy-start.1 = (s32[3,8]{1,0:T(4,128)S(1)}, s32[3,8]{1,0:T(4,128)}, u32[]{:S(2)}) copy-start(s32[3,8]{1,0:T(4,128)} %refs_0_.1) | copy-start | bytes 292
  4.2 0.7 %copy-start.2 = (s32[3,8]{1,0:T(4,128)S(1)}, s32[3,8]{1,0:T(4,128)}, u32[]{:S(2)}) copy-start(s32[3,8]{1,0:T(4,128)} %refs_2_.1) | copy-start | bytes 292
  4.9 0.7 %copy-start.3 = (s32[3,32]{1,0:T(4,128)S(1)}, s32[3,32]{1,0:T(4,128)}, u32[]{:S(2)}) copy-start(s32[3,32]{1,0:T(4,128)} %refs_3_.1) | copy-start | bytes 1156
  13.1 1.9 %collective-permute-start = (bf16[8,1,2,48,256]{4,3,2,1,0:T(8,128)(2,1)S(1)}, bf16[8,1,2,48,256]{4,3,2,1,0:T(8,128)(2,1)S(1)}, u32[]{:S(2)}, u32[]{:S(2)}) collective-permute-start(bf16[8,1,2,48,256]{4,3,2,1,0:T(8,128)(2,1)S(1)} %get-tuple-element.8), channel_id=1, source_target_pairs={{0,1},{1,0},{2,3},{3,2},{4,5},{5,4},{6,7},{7,6},{8,9},{9,8},{10,11... | collective-permute-start | bytes 1179656 | tf_op jit(solution)/shard_map/ppermute | solution.py:170
  15.1 6.6 %collective-permute-start.1 = (bf16[4,1,2,48,256]{4,3,2,1,0:T(8,128)(2,1)S(1)}, bf16[4,1,2,48,256]{4,3,2,1,0:T(8,128)(2,1)S(1)}, u32[]{:S(2)}, u32[]{:S(2)}) collective-permute-start(bf16[4,1,2,48,256]{4,3,2,1,0:T(8,128)(2,1)S(1)} %slice.38), channel_id=1, source_target_pairs={{0,2},{1,5},{2,0},{3,7},{4,6},{5,1},{6,4},{7,3},{8,10},{9,13},{10,... | collective-permute-start | bytes 589832 | tf_op jit(solution)/shard_map/ppermute | solution.py:181
  21.7 4.7 %collective-permute-start.2 = (bf16[2,1,2,48,256]{4,3,2,1,0:T(8,128)(2,1)S(1)}, bf16[2,1,2,48,256]{4,3,2,1,0:T(8,128)(2,1)S(1)}, u32[]{:S(2)}, u32[]{:S(2)}) collective-permute-start(bf16[2,1,2,48,256]{4,3,2,1,0:T(8,128)(2,1)S(1)} %slice.39), channel_id=1, source_target_pairs={{0,4},{1,3},{2,6},{3,1},{4,0},{5,7},{6,2},{7,5},{8,12},{9,11},{10,... | collective-permute-start | bytes 294920 | tf_op jit(solution)/shard_map/ppermute | solution.py:181
  26.5 5.2 %collective-permute-start.3 = (bf16[1,1,2,48,256]{4,3,2,1,0:T(8,128)(2,1)S(1)}, bf16[1,1,2,48,256]{4,3,2,1,0:T(8,128)(2,1)S(1)}, u32[]{:S(2)}, u32[]{:S(2)}) collective-permute-start(bf16[1,1,2,48,256]{4,3,2,1,0:T(8,128)(2,1)S(1)} %slice.40), channel_id=1, source_target_pairs={{0,8},{1,9},{2,10},{3,11},{4,12},{5,13},{6,14},{7,15},{8,0},{9,1},... | collective-permute-start | bytes 147464 | tf_op jit(solution)/shard_map/ppermute | solution.py:181
  31.7 0.6 %copy-start.4 = (bf16[1,1,2,48,256]{4,3,2,1,0:T(8,128)(2,1)}, bf16[1,1,2,48,256]{4,3,2,1,0:T(8,128)(2,1)S(1)}, u32[]{:S(2)}) copy-start(bf16[1,1,2,48,256]{4,3,2,1,0:T(8,128)(2,1)S(1)} %collective-permute-done.3.got_ref) | copy-start | bytes 147460

commit v2 on v1

v2 whole, which is shorter than its diff:
```python
import math

import jax
import jax.numpy as jnp
from jax import lax
from jax.experimental import pallas as pl
from jax.experimental.pallas import tpu as pltpu
from jax.sharding import PartitionSpec as P

NFINE = 48
ROWS = 16


def bit_order(bits, core):
    order = list(range(bits))
    if bits > 1 and core == 1:
        order[0], order[1] = order[1], order[0]
    return order


def swap_slot(slot, bits):
    if bits < 2:
        return slot
    high, low = (slot >> (bits - 1)) & 1, (slot >> (bits - 2)) & 1
    rest = slot & ((1 << (bits - 2)) - 1)
    return (low << (bits - 1)) | (high << (bits - 2)) | rest


def wrapped_angle(products):
    turns = jnp.floor((products + 0.5) * (1.0 / NFINE))
    return (products - NFINE * turns) * (2.0 * math.pi / NFINE)


def phase_kernel(bits, q_hbm, k_hbm, ev_hbm, rpv_hbm, eig_hbm, w_ref, keep_ref, send_ref, mixer_ref,
                 slabs, lhs, prod, rpv_ref, eig_ref, q_ref, k_ref, ev_ref, sems, small_sems):
    parts, points, slab, modes, pairs = w_ref.shape
    slots, per_core = keep_ref.shape[:2]
    chunks = modes // ROWS

    small = [
        pltpu.make_async_copy(source, target, small_sems.at[at])
        for at, (source, target) in enumerate(
            [(rpv_hbm, rpv_ref), (q_hbm, q_ref), (k_hbm, k_ref), (ev_hbm, ev_ref), (eig_hbm, eig_ref)]
        )
    ]
    for copy in small:
        copy.start()

    def fetch(c, e):
        return pltpu.make_async_copy(
            w_ref.at[:, :, e, pl.ds(c * ROWS, ROWS), :], slabs.at[c, e], sems.at[c, e]
        )

    for c in range(chunks):
        for e in range(slab):
            fetch(c, e).start()
    for copy in small:
        copy.wait()

    me = lax.axis_index("rp")
    core = lax.axis_index("re")
    width = points * ROWS
    spread = (
        lax.broadcasted_iota(jnp.int32, (points, width), 1) // ROWS
        == lax.broadcasted_iota(jnp.int32, (points, width), 0)
    ).astype(jnp.bfloat16)
    vectors = jnp.dot(rpv_ref[...].astype(jnp.bfloat16), spread, preferred_element_type=jnp.float32)
    rows = []
    for slot in range(slots):
        offset = 0
        for at, (one, other) in enumerate(zip(bit_order(bits, 0), bit_order(bits, 1))):
            if (slot >> (bits - 1 - at)) & 1:
                offset = offset + jnp.where(core == 0, 1 << one, 1 << other)
        q = me ^ offset
        row = 0.0
        for axis in range(3):
            row = row + q_ref[axis, q].astype(jnp.float32) * vectors[axis : axis + 1, :]
        rows.append(row)
    angles = wrapped_angle(jnp.concatenate(rows, axis=0))
    cosine, sine = jnp.cos(angles), jnp.sin(angles)
    diagonal = (
        lax.broadcasted_iota(jnp.int32, (ROWS, width), 1) % ROWS
        == lax.broadcasted_iota(jnp.int32, (ROWS, width), 0)
    ).astype(jnp.float32)
    for slot in range(slots):
        cos_block = (cosine[slot : slot + 1] * diagonal).astype(jnp.bfloat16)
        sin_block = (sine[slot : slot + 1] * diagonal).astype(jnp.bfloat16)
        top, bottom = pl.ds(2 * slot * ROWS, ROWS), pl.ds((2 * slot + 1) * ROWS, ROWS)
        lhs[top, :width] = cos_block
        lhs[top, width:] = -sin_block
        lhs[bottom, :width] = sin_block
        lhs[bottom, width:] = cos_block

    places = (2 * per_core, slab)
    at_row = lax.broadcasted_iota(jnp.int32, places, 0)
    at_lane = lax.broadcasted_iota(jnp.int32, places, 1)
    products = jnp.zeros(places, jnp.float32)
    for side in range(2):
        for i in range(per_core):
            k = (core ^ side) * per_core + i
            for e in range(slab):
                total = 0
                for axis in range(3):
                    total = total + k_ref[k, axis] * ev_ref[axis, core * slab + e]
                here = (at_row == side * per_core + i) & (at_lane == e)
                products = jnp.where(here, total.astype(jnp.float32), products)
    k_angles = wrapped_angle(products)
    k_cos, k_sin = jnp.cos(k_angles), jnp.sin(k_angles)

    real_vec, imag_vec = eig_ref[0, 0], eig_ref[0, 1]
    rotation = jnp.concatenate(
        [jnp.concatenate([real_vec, imag_vec], axis=1), jnp.concatenate([-imag_vec, real_vec], axis=1)], axis=0
    )
    high = rotation.astype(jnp.bfloat16)
    mixer_ref[0] = high
    mixer_ref[1] = high
    mixer_ref[2] = (rotation - high.astype(jnp.float32)).astype(jnp.bfloat16)

    def k_sum(c):
        where = pl.ds(c * ROWS, ROWS)
        for slot in range(slots):
            sums = {}
            for e in range(slab):
                p_real = prod[c % 2, e, pl.ds(2 * slot * ROWS, ROWS), :]
                p_imag = prod[c % 2, e, pl.ds((2 * slot + 1) * ROWS, ROWS), :]
                for line in range(2 * per_core):
                    cos_e = jnp.broadcast_to(k_cos[line : line + 1, e : e + 1], (ROWS, pairs))
                    sin_e = jnp.broadcast_to(k_sin[line : line + 1, e : e + 1], (ROWS, pairs))
                    r_term = cos_e * p_real - sin_e * p_imag
                    i_term = sin_e * p_real + cos_e * p_imag
                    if e:
                        r_term, i_term = r_term + sums[line][0], i_term + sums[line][1]
                    sums[line] = r_term, i_term
            for i in range(per_core):
                for part in range(2):
                    keep_ref[slot, i, part, where, :] = sums[i][part]
                    send_ref[swap_slot(slot, bits), i, part, where, :] = sums[per_core + i][part].astype(send_ref.dtype)

    for c in range(chunks):
        for e in range(slab):
            fetch(c, e).wait()
        for e in range(slab):
            prod[c % 2, e] = jnp.dot(
                lhs[...], slabs[c, e].reshape(parts * width, pairs), preferred_element_type=jnp.float32
            )
        if c:
            k_sum(c - 1)
    k_sum(chunks - 1)


def rotate_kernel(mine_ref, got_ref, mixer_ref, out_ref):
    modes, pairs = mine_ref.shape[-2:]
    mixer = mixer_ref[...].reshape(-1, 2 * modes)
    for i in range(mine_ref.shape[1]):
        source = (mine_ref[0, i] + got_ref[0, i].astype(jnp.float32)).reshape(2 * modes, pairs)
        high = source.astype(jnp.bfloat16)
        low = (source - high.astype(jnp.float32)).astype(jnp.bfloat16)
        stacked = jnp.concatenate([high, low, high], axis=0)
        turned = lax.dot_general(
            mixer, stacked, (((0,), (0,)), ((), ())), preferred_element_type=jnp.float32
        ).astype(out_ref.dtype)
        out_ref[0, 0, i] = turned[:modes]
        out_ref[0, 1, i] = turned[modes:]


def make_shards(mesh):
    ranks, cores = mesh.shape["rp"], mesh.shape["re"]
    bits = ranks.bit_length() - 1
    vmem = pl.BlockSpec(memory_space=pltpu.VMEM)
    smem = pl.BlockSpec(memory_space=pltpu.SMEM)

    def shards(weights, rp_vectors, re_vectors, q_points, k_points, eigvecs):
        parts, points, slab, modes, pairs = weights.shape
        slots = q_points.shape[1]
        per_core = k_points.shape[1] // cores
        chunks = modes // ROWS
        shape = (slots, per_core, 2, modes, pairs)
        hbm = pl.BlockSpec(memory_space=pltpu.HBM)
        keep, send, mixer = pl.pallas_call(
            lambda *refs: phase_kernel(bits, *refs),
            out_shape=(
                jax.ShapeDtypeStruct(shape, jnp.float32),
                jax.ShapeDtypeStruct(shape, jnp.bfloat16),
                jax.ShapeDtypeStruct((3, 2 * modes, 2 * modes), jnp.bfloat16),
            ),
            in_specs=[hbm] * 6,
            out_specs=(vmem, vmem, vmem),
            scratch_shapes=[
                pltpu.VMEM((chunks, slab, parts, points, ROWS, pairs), jnp.bfloat16),
                pltpu.VMEM((2 * slots * ROWS, parts * points * ROWS), jnp.bfloat16),
                pltpu.VMEM((2, slab, 2 * slots * ROWS, pairs), jnp.float32),
                pltpu.VMEM(rp_vectors.shape, jnp.int32),
                pltpu.VMEM(eigvecs.shape, jnp.float32),
                pltpu.SMEM(q_points.shape, jnp.int32),
                pltpu.SMEM(k_points.shape[::-1], jnp.int32),
                pltpu.SMEM(re_vectors.shape, jnp.int32),
                pltpu.SemaphoreType.DMA((chunks, slab)),
                pltpu.SemaphoreType.DMA((5,)),
            ],
            compiler_params=pltpu.CompilerParams(vmem_limit_bytes=32 * 2**20),
            name="phase_sums",
        )(*[pltpu.with_memory_space_constraint(x, pltpu.HBM) for x in (q_points, k_points.T, re_vectors, rp_vectors, eigvecs, weights)])
        got = lax.ppermute(send, "re", [(c, c ^ 1) for c in range(cores)])
        mine = keep
        for step in range(bits):
            half = slots >> (step + 1)
            mine = mine[: 2 * half] + got.astype(jnp.float32)
            away = mine[half:].astype(jnp.bfloat16)
            pairs_of = [
                (r * cores + c, (r ^ (1 << bit_order(bits, c)[step])) * cores + c)
                for r in range(ranks)
                for c in range(cores)
            ]
            got = lax.ppermute(away, ("rp", "re"), pairs_of)
        return pl.pallas_call(
            rotate_kernel,
            out_shape=jax.ShapeDtypeStruct((1, 2, per_core, modes, pairs), jnp.bfloat16),
            in_specs=[vmem, vmem, vmem],
            out_specs=vmem,
            compiler_params=pltpu.CompilerParams(vmem_limit_bytes=4 * 2**20),
            name="rotate_modes",
        )(mine, got, mixer)

    return shards


def solution(mesh):
    return jax.shard_map(
        make_shards(mesh),
        mesh=mesh,
        in_specs=(
            P(None, "rp", "re", None, None),
            P(None, "rp"),
            P(),
            P(None, "grp"),
            P(None, "grp"),
            P(("grp", "rp"), None, None, None),
        ),
        out_specs=P(("grp", "rp"), None, "re", None, None),
        check_vma=False,
    )
```

time: 34.5 us -> 25.2 us (0.73)
  local copies, waits for them, and re-layouts: 6.9 us -> 0.05 us
  Pallas kernels: 9.35 us -> 6.43 us
  waiting for transfers between devices: 9.02 us -> 9.66 us
    unnamed x11 -> x0, local copies, waits for them, and re-layouts: 6.21 us -> none
    pallas_call x1, Pallas kernels: 7.45 us -> 5.59 us  [shards(): pl.pallas_call(lambda *refs: phase_kernel(bits, *refs), out_shape=(jax.Sh...]
    pallas_call x1, Pallas kernels: 1.9 us -> 0.84 us  [shards(): pl.pallas_call(rotate_kernel, out_shape=jax.ShapeDtypeStruct((1, 2, per_c...]
    ppermute x3, waiting for transfers between devices: 7.67 us -> 8.32 us  [shards(): got = lax.ppermute(away, ('rp', 're'), pairs_of)]
    slice x4 -> x3, local copies, waits for them, and re-layouts: 0.69 us -> 0.05 us  [shards(): away = mine[half:].astype(jnp.bfloat16)]
  transfers between devices with their start and end apart: 4 -> 4, of which waited for: 4 -> 4; matrix products, arithmetic and copies ran while one was open for 2% -> 0% of each run, Pallas kernels for 0% -> 0%
where the time goes in v2:
time: 25.2 us; the launch traced here: 25.1 us
  waiting for transfers between devices  9.66 us (38%)
  starting transfers between devices  8.71 us (35%)
  Pallas kernels  6.43 us (26%)
    ppermute x3, waiting for transfers between devices, shards(): got = lax.ppermute(away, ('rp', 're'), pairs_of)  8.32 us
    ppermute x3, starting transfers between devices, shards(): got = lax.ppermute(away, ('rp', 're'), pairs_of)  8.19 us
    pallas_call x1, Pallas kernels, shards(): pl.pallas_call(lambda *refs: phase_kernel(bits, *refs), out_shape=(jax.Sh...  5.59 us
    ppermute x1, waiting for transfers between devices, shards(): got = lax.ppermute(send, 're', [(c, c ^ 1) for c in range(cores)])  1.35 us
    pallas_call x1, Pallas kernels, shards(): pl.pallas_call(rotate_kernel, out_shape=jax.ShapeDtypeStruct((1, 2, per_c...  0.84 us
    ppermute x1, starting transfers between devices, shards(): got = lax.ppermute(send, 're', [(c, c ^ 1) for c in range(cores)])  0.52 us
  transfers between devices with their start and end apart: 4, of which 4 were waited for; matrix products, arithmetic and copies ran while one was open for 0% of the time, Pallas kernels for 0%

profile of v2, /device:TPU:0, one launch (start us, length us, event | category | flops | bytes accessed | tf_op | source)
XLA Modules:
  0.0 25.1 jit_solution(6112491735853779421)
XLA Ops:
  0.0 5.6 %phase_sums.1 = (f32[8,1,2,48,256]{4,3,2,1,0:T(8,128)S(1)}, bf16[8,1,2,48,256]{4,3,2,1,0:T(8,128)(2,1)S(1)}, bf16[3,96,96]{2,1,0:T(8,128)(2,1)S(1)}) custom-call(s32[3,8]{1,0:T(4,128)} %refs_0_.1, s32[2,3]{1,0:T(2,128)} %bitcast.1, s32[3,8]{1,0:T(4,128)} %refs_2_.1, s32[3,32]{1,0:T(4,128)} %refs_3_.1, f32[1,2,48,48]{3,2,1,0:T(8,128)} %refs_4_.1, ...), custom_call_target="tpu_custom_call" | custom-call | tf_op jit(solution)/shard_map/phase_sums/pallas_call | solution.py:179
  5.6 0.5 %collective-permute-start = (bf16[8,1,2,48,256]{4,3,2,1,0:T(8,128)(2,1)S(1)}, bf16[8,1,2,48,256]{4,3,2,1,0:T(8,128)(2,1)S(1)}, u32[]{:S(2)}, u32[]{:S(2)}) collective-permute-start(bf16[8,1,2,48,256]{4,3,2,1,0:T(8,128)(2,1)S(1)} %get-tuple-element.9), channel_id=1, source_target_pairs={{0,1},{1,0},{2,3},{3,2},{4,5},{5,4},{6,7},{7,6},{8,9},{9,8},{10,11... | collective-permute-start | bytes 1179656 | tf_op jit(solution)/shard_map/ppermute | solution.py:203
  6.1 1.3 %collective-permute-done = bf16[8,1,2,48,256]{4,3,2,1,0:T(8,128)(2,1)S(1)} collective-permute-done((bf16[8,1,2,48,256]{4,3,2,1,0:T(8,128)(2,1)S(1)}, bf16[8,1,2,48,256]{4,3,2,1,0:T(8,128)(2,1)S(1)}, u32[]{:S(2)}, u32[]{:S(2)}) %collective-permute-start) | collective-permute-done | bytes 393248 | tf_op jit(solution)/shard_map/ppermute | solution.py:203
  7.5 0.1 convert_add_fusion
  7.6 3.0 %collective-permute-start.1 = (bf16[4,1,2,48,256]{4,3,2,1,0:T(8,128)(2,1)S(1)}, bf16[4,1,2,48,256]{4,3,2,1,0:T(8,128)(2,1)S(1)}, u32[]{:S(2)}, u32[]{:S(2)}) collective-permute-start(bf16[4,1,2,48,256]{4,3,2,1,0:T(8,128)(2,1)S(1)} %slice.33), channel_id=1, source_target_pairs={{0,2},{1,5},{2,0},{3,7},{4,6},{5,1},{6,4},{7,3},{8,10},{9,13},{10,... | collective-permute-start | bytes 589832 | tf_op jit(solution)/shard_map/ppermute | solution.py:214
  10.5 3.6 %collective-permute-done.1 = bf16[4,1,2,48,256]{4,3,2,1,0:T(8,128)(2,1)S(1)} collective-permute-done((bf16[4,1,2,48,256]{4,3,2,1,0:T(8,128)(2,1)S(1)}, bf16[4,1,2,48,256]{4,3,2,1,0:T(8,128)(2,1)S(1)}, u32[]{:S(2)}, u32[]{:S(2)}) %collective-permute-start.1) | collective-permute-done | bytes 196640 | tf_op jit(solution)/shard_map/ppermute | solution.py:214
  14.3 2.1 %collective-permute-start.2 = (bf16[2,1,2,48,256]{4,3,2,1,0:T(8,128)(2,1)S(1)}, bf16[2,1,2,48,256]{4,3,2,1,0:T(8,128)(2,1)S(1)}, u32[]{:S(2)}, u32[]{:S(2)}) collective-permute-start(bf16[2,1,2,48,256]{4,3,2,1,0:T(8,128)(2,1)S(1)} %slice.34), channel_id=1, source_target_pairs={{0,4},{1,3},{2,6},{3,1},{4,0},{5,7},{6,2},{7,5},{8,12},{9,11},{10,... | collective-permute-start | bytes 294920 | tf_op jit(solution)/shard_map/ppermute | solution.py:214
  16.4 2.6 %collective-permute-done.2 = bf16[2,1,2,48,256]{4,3,2,1,0:T(8,128)(2,1)S(1)} collective-permute-done((bf16[2,1,2,48,256]{4,3,2,1,0:T(8,128)(2,1)S(1)}, bf16[2,1,2,48,256]{4,3,2,1,0:T(8,128)(2,1)S(1)}, u32[]{:S(2)}, u32[]{:S(2)}) %collective-permute-start.2) | collective-permute-done | bytes 98336 | tf_op jit(solution)/shard_map/ppermute | solution.py:214
  19.0 3.1 %collective-permute-start.3 = (bf16[1,1,2,48,256]{4,3,2,1,0:T(8,128)(2,1)S(1)}, bf16[1,1,2,48,256]{4,3,2,1,0:T(8,128)(2,1)S(1)}, u32[]{:S(2)}, u32[]{:S(2)}) collective-permute-start(bf16[1,1,2,48,256]{4,3,2,1,0:T(8,128)(2,1)S(1)} %slice.35), channel_id=1, source_target_pairs={{0,8},{1,9},{2,10},{3,11},{4,12},{5,13},{6,14},{7,15},{8,0},{9,1},... | collective-permute-start | bytes 147464 | tf_op jit(solution)/shard_map/ppermute | solution.py:214
  22.1 2.1 %collective-permute-done.3.got_ref = bf16[1,1,2,48,256]{4,3,2,1,0:T(8,128)(2,1)S(1)} collective-permute-done((bf16[1,1,2,48,256]{4,3,2,1,0:T(8,128)(2,1)S(1)}, bf16[1,1,2,48,256]{4,3,2,1,0:T(8,128)(2,1)S(1)}, u32[]{:S(2)}, u32[]{:S(2)}) %collective-permute-start.3) | collective-permute-done | bytes 49184 | tf_op jit(solution)/shard_map/ppermute | solution.py:214
  24.2 0.8 %rotate_modes.1 = bf16[1,2,1,48,256]{4,3,2,1,0:T(8,128)(2,1)} custom-call(f32[2,1,2,48,256]{4,3,2,1,0:T(8,128)S(1)} %slice_add_fusion.1.mine_ref, bf16[1,1,2,48,256]{4,3,2,1,0:T(8,128)(2,1)S(1)} %collective-permute-done.3.got_ref, bf16[3,96,96]{2,1,0:T(8,128)(2,1)S(1)} %get-tuple-element.10.mixer_ref), custom_call_target="tpu_custom_call" | custom-call | tf_op jit(solution)/shard_map/rotate_modes/pallas_call | solution.py:215
  (5 shorter events, 0.1 us)
Async XLA Ops:
  5.6 1.9 %collective-permute-start = (bf16[8,1,2,48,256]{4,3,2,1,0:T(8,128)(2,1)S(1)}, bf16[8,1,2,48,256]{4,3,2,1,0:T(8,128)(2,1)S(1)}, u32[]{:S(2)}, u32[]{:S(2)}) collective-permute-start(bf16[8,1,2,48,256]{4,3,2,1,0:T(8,128)(2,1)S(1)} %get-tuple-element.9), channel_id=1, source_target_pairs={{0,1},{1,0},{2,3},{3,2},{4,5},{5,4},{6,7},{7,6},{8,9},{9,8},{10,11... | collective-permute-start | bytes 1179656 | tf_op jit(solution)/shard_map/ppermute | solution.py:203
  7.6 6.6 %collective-permute-start.1 = (bf16[4,1,2,48,256]{4,3,2,1,0:T(8,128)(2,1)S(1)}, bf16[4,1,2,48,256]{4,3,2,1,0:T(8,128)(2,1)S(1)}, u32[]{:S(2)}, u32[]{:S(2)}) collective-permute-start(bf16[4,1,2,48,256]{4,3,2,1,0:T(8,128)(2,1)S(1)} %slice.33), channel_id=1, source_target_pairs={{0,2},{1,5},{2,0},{3,7},{4,6},{5,1},{6,4},{7,3},{8,10},{9,13},{10,... | collective-permute-start | bytes 589832 | tf_op jit(solution)/shard_map/ppermute | solution.py:214
  14.3 4.7 %collective-permute-start.2 = (bf16[2,1,2,48,256]{4,3,2,1,0:T(8,128)(2,1)S(1)}, bf16[2,1,2,48,256]{4,3,2,1,0:T(8,128)(2,1)S(1)}, u32[]{:S(2)}, u32[]{:S(2)}) collective-permute-start(bf16[2,1,2,48,256]{4,3,2,1,0:T(8,128)(2,1)S(1)} %slice.34), channel_id=1, source_target_pairs={{0,4},{1,3},{2,6},{3,1},{4,0},{5,7},{6,2},{7,5},{8,12},{9,11},{10,... | collective-permute-start | bytes 294920 | tf_op jit(solution)/shard_map/ppermute | solution.py:214
  19.0 5.2 %collective-permute-start.3 = (bf16[1,1,2,48,256]{4,3,2,1,0:T(8,128)(2,1)S(1)}, bf16[1,1,2,48,256]{4,3,2,1,0:T(8,128)(2,1)S(1)}, u32[]{:S(2)}, u32[]{:S(2)}) collective-permute-start(bf16[1,1,2,48,256]{4,3,2,1,0:T(8,128)(2,1)S(1)} %slice.35), channel_id=1, source_target_pairs={{0,8},{1,9},{2,10},{3,11},{4,12},{5,13},{6,14},{7,15},{8,0},{9,1},... | collective-permute-start | bytes 147464 | tf_op jit(solution)/shard_map/ppermute | solution.py:214

commit v3 on v2

v3 whole, which is shorter than its diff:
```python
import math

import jax
import jax.numpy as jnp
from jax import lax
from jax.experimental import pallas as pl
from jax.experimental.pallas import tpu as pltpu
from jax.sharding import PartitionSpec as P

NFINE = 48
NEAR = 2
PIECES = 2
ROWS = 16


def slot_offset(slot, bits):
    near = min(NEAR, bits - 1)
    return (slot >> (bits - near)) | ((slot & ((1 << (bits - near)) - 1)) << near)


def wrapped_angle(products):
    turns = jnp.floor((products + 0.5) * (1.0 / NFINE))
    return (products - NFINE * turns) * (2.0 * math.pi / NFINE)


def k_phases(core, per_core, slab, k_ref, ev_ref):
    places = (2 * per_core, slab)
    at_row = lax.broadcasted_iota(jnp.int32, places, 0)
    at_lane = lax.broadcasted_iota(jnp.int32, places, 1)
    products = jnp.zeros(places, jnp.float32)
    for line in range(2 * per_core):
        k = (core ^ (line // per_core)) * per_core + line % per_core
        for e in range(slab):
            total = 0
            for axis in range(3):
                total = total + k_ref[k, axis] * ev_ref[axis, core * slab + e]
            products = jnp.where((at_row == line) & (at_lane == e), total.astype(jnp.float32), products)
    angles = wrapped_angle(products)
    return jnp.cos(angles), jnp.sin(angles)


def k_sum(prod_ref, c, slot, k_cos, k_sin, line):
    slab, _, pairs = prod_ref.shape[1:]
    real = imag = None
    for e in range(slab):
        p_real = prod_ref[c, e, pl.ds(2 * slot * ROWS, ROWS), :]
        p_imag = prod_ref[c, e, pl.ds((2 * slot + 1) * ROWS, ROWS), :]
        cos_e = jnp.broadcast_to(k_cos[line : line + 1, e : e + 1], (ROWS, pairs))
        sin_e = jnp.broadcast_to(k_sin[line : line + 1, e : e + 1], (ROWS, pairs))
        r_term = cos_e * p_real - sin_e * p_imag
        i_term = sin_e * p_real + cos_e * p_imag
        real = r_term if e == 0 else real + r_term
        imag = i_term if e == 0 else imag + i_term
    return real, imag


def phase_kernel(bits, q_hbm, k_hbm, ev_hbm, rpv_hbm, w_ref, prod_ref, send_ref, turn_ref,
                 slabs, lhs, rpv_ref, q_ref, k_ref, ev_ref, sems, small_sems):
    parts, points, slab, modes, pairs = w_ref.shape
    slots, per_core = send_ref.shape[:2]
    chunks = modes // ROWS
    pieces = sems.shape[1]

    small = [
        pltpu.make_async_copy(source, target, small_sems.at[at])
        for at, (source, target) in enumerate(
            [(rpv_hbm, rpv_ref), (q_hbm, q_ref), (k_hbm, k_ref), (ev_hbm, ev_ref)]
        )
    ]
    for copy in small:
        copy.start()

    def fetch(c, piece):
        some = pl.ds(piece * (points // pieces), points // pieces)
        return pltpu.make_async_copy(
            w_ref.at[:, some, :, pl.ds(c * ROWS, ROWS), :], slabs.at[c, :, some], sems.at[c, piece]
        )

    for c in range(chunks):
        for piece in range(pieces):
            fetch(c, piece).start()
    for copy in small:
        copy.wait()

    me = lax.axis_index("rp")
    core = lax.axis_index("re")
    width = points * ROWS
    spread = (
        lax.broadcasted_iota(jnp.int32, (points, width), 1) // ROWS
        == lax.broadcasted_iota(jnp.int32, (points, width), 0)
    ).astype(jnp.bfloat16)
    vectors = jnp.dot(rpv_ref[...].astype(jnp.bfloat16), spread, preferred_element_type=jnp.float32)
    rows = []
    for slot in range(slots):
        q = me ^ slot_offset(slot, bits)
        row = 0.0
        for axis in range(3):
            row = row + q_ref[axis, q].astype(jnp.float32) * vectors[axis : axis + 1, :]
        rows.append(row)
    angles = wrapped_angle(jnp.concatenate(rows, axis=0))
    cosine, sine = jnp.cos(angles), jnp.sin(angles)
    diagonal = (
        lax.broadcasted_iota(jnp.int32, (ROWS, width), 1) % ROWS
        == lax.broadcasted_iota(jnp.int32, (ROWS, width), 0)
    ).astype(jnp.float32)
    for slot in range(slots):
        cos_block = (cosine[slot : slot + 1] * diagonal).astype(jnp.bfloat16)
        sin_block = (sine[slot : slot + 1] * diagonal).astype(jnp.bfloat16)
        top, bottom = pl.ds(2 * slot * ROWS, ROWS), pl.ds((2 * slot + 1) * ROWS, ROWS)
        lhs[top, :width] = cos_block
        lhs[top, width:] = -sin_block
        lhs[bottom, :width] = sin_block
        lhs[bottom, width:] = cos_block

    k_cos, k_sin = k_phases(core, per_core, slab, k_ref, ev_ref)
    turn_ref[0] = k_cos
    turn_ref[1] = k_sin

    def send_sum(c):
        for slot in range(slots):
            for i in range(per_core):
                sums = k_sum(prod_ref, c, slot, k_cos, k_sin, per_core + i)
                for part in range(2):
                    send_ref[slot, i, part, pl.ds(c * ROWS, ROWS), :] = sums[part].astype(send_ref.dtype)

    for c in range(chunks):
        for piece in range(pieces):
            fetch(c, piece).wait()
        for e in range(slab):
            block = slabs[c, :, :, e].reshape(parts * width, pairs)
            prod_ref[c, e] = jnp.dot(lhs[...], block, preferred_element_type=jnp.float32)
        if c:
            send_sum(c - 1)
    send_sum(chunks - 1)


def keep_kernel(prod_ref, turn_ref, eig_hbm, keep_ref, mixer_ref, eig_ref, sem):
    fetch = pltpu.make_async_copy(eig_hbm, eig_ref, sem)
    fetch.start()
    slots, per_core = keep_ref.shape[:2]
    k_cos, k_sin = turn_ref[0], turn_ref[1]
    for c in range(prod_ref.shape[0]):
        for slot in range(slots):
            for i in range(per_core):
                sums = k_sum(prod_ref, c, slot, k_cos, k_sin, i)
                for part in range(2):
                    keep_ref[slot, i, part, pl.ds(c * ROWS, ROWS), :] = sums[part]

    fetch.wait()
    real_vec, imag_vec = eig_ref[0, 0], eig_ref[0, 1]
    rotation = jnp.concatenate(
        [jnp.concatenate([real_vec, imag_vec], axis=1), jnp.concatenate([-imag_vec, real_vec], axis=1)], axis=0
    )
    high = rotation.astype(jnp.bfloat16)
    mixer_ref[0] = high
    mixer_ref[1] = high
    mixer_ref[2] = (rotation - high.astype(jnp.float32)).astype(jnp.bfloat16)


def rotate_kernel(mine_ref, got_ref, mixer_ref, out_ref):
    modes, pairs = mine_ref.shape[-2:]
    mixer = mixer_ref[...].reshape(-1, 2 * modes)
    for i in range(mine_ref.shape[1]):
        source = (mine_ref[0, i] + got_ref[0, i].astype(jnp.float32)).reshape(2 * modes, pairs)
        high = source.astype(jnp.bfloat16)
        low = (source - high.astype(jnp.float32)).astype(jnp.bfloat16)
        stacked = jnp.concatenate([high, low, high], axis=0)
        turned = lax.dot_general(
            mixer, stacked, (((0,), (0,)), ((), ())), preferred_element_type=jnp.float32
        ).astype(out_ref.dtype)
        out_ref[0, 0, i] = turned[:modes]
        out_ref[0, 1, i] = turned[modes:]


def make_shards(mesh):
    ranks, cores = mesh.shape["rp"], mesh.shape["re"]
    bits = ranks.bit_length() - 1
    vmem = pl.BlockSpec(memory_space=pltpu.VMEM)
    hbm = pl.BlockSpec(memory_space=pltpu.HBM)

    def in_hbm(x):
        return pltpu.with_memory_space_constraint(x, pltpu.HBM)

    def shards(weights, rp_vectors, re_vectors, q_points, k_points, eigvecs):
        parts, points, slab, modes, pairs = weights.shape
        slots = q_points.shape[1]
        per_core = k_points.shape[1] // cores
        chunks = modes // ROWS
        shape = (slots, per_core, 2, modes, pairs)
        pieces = math.gcd(points, PIECES)
        lines = 2 * slots * ROWS
        prod, send, turn = pl.pallas_call(
            lambda *refs: phase_kernel(bits, *refs),
            out_shape=(
                jax.ShapeDtypeStruct((chunks, slab, lines, pairs), jnp.float32),
                jax.ShapeDtypeStruct(shape, jnp.bfloat16),
                jax.ShapeDtypeStruct((2, 2 * per_core, slab), jnp.float32),
            ),
            in_specs=[hbm] * 5,
            out_specs=(vmem, vmem, vmem),
            scratch_shapes=[
                pltpu.VMEM((chunks, parts, points, slab, ROWS, pairs), jnp.bfloat16),
                pltpu.VMEM((lines, parts * points * ROWS), jnp.bfloat16),
                pltpu.VMEM(rp_vectors.shape, jnp.int32),
                pltpu.SMEM(q_points.shape, jnp.int32),
                pltpu.SMEM(k_points.shape[::-1], jnp.int32),
                pltpu.SMEM(re_vectors.shape, jnp.int32),
                pltpu.SemaphoreType.DMA((chunks, pieces)),
                pltpu.SemaphoreType.DMA((4,)),
            ],
            compiler_params=pltpu.CompilerParams(vmem_limit_bytes=32 * 2**20),
            name="phase_sums",
        )(*[in_hbm(x) for x in (q_points, k_points.T, re_vectors, rp_vectors, weights)])
        keep, mixer = pl.pallas_call(
            keep_kernel,
            out_shape=(
                jax.ShapeDtypeStruct(shape, jnp.float32),
                jax.ShapeDtypeStruct((3, 2 * modes, 2 * modes), jnp.bfloat16),
            ),
            in_specs=[vmem, vmem, hbm],
            out_specs=(vmem, vmem),
            scratch_shapes=[pltpu.VMEM(eigvecs.shape, jnp.float32), pltpu.SemaphoreType.DMA],
            compiler_params=pltpu.CompilerParams(vmem_limit_bytes=4 * 2**20),
            cost_estimate=pl.CostEstimate(flops=8 * prod.size, bytes_accessed=4 * prod.size, transcendentals=0),
            name="own_k_sums",
        )(prod, turn, in_hbm(eigvecs))
        got = lax.ppermute(send, "re", [(c, c ^ 1) for c in range(cores)])
        mine = keep + got.astype(jnp.float32)

        def swap(block, offset):
            return lax.ppermute(block, "rp", [(r, r ^ offset) for r in range(ranks)]).astype(jnp.float32)

        near = min(NEAR, bits - 1)
        far = bits - near
        half = slots >> near
        parcels = {d: mine[d * half : (d + 1) * half].astype(jnp.bfloat16) for d in range(1, 1 << near)}
        total = mine[:half]
        for d in sorted(parcels, key=lambda d: -d):
            total = total + swap(parcels[d], d)
        for step in range(far - 1):
            half = half // 2
            total = total[:half] + swap(total[half : 2 * half].astype(jnp.bfloat16), 1 << (bits - 1 - step))
        got = lax.ppermute(total[half // 2 :].astype(jnp.bfloat16), "rp", [(r, r ^ (1 << near)) for r in range(ranks)])
        return pl.pallas_call(
            rotate_kernel,
            out_shape=jax.ShapeDtypeStruct((1, 2, per_core, modes, pairs), jnp.bfloat16),
            in_specs=[vmem, vmem, vmem],
            out_specs=vmem,
            compiler_params=pltpu.CompilerParams(vmem_limit_bytes=4 * 2**20),
            name="rotate_modes",
        )(total, got, mixer)

    return shards


def solution(mesh):
    return jax.shard_map(
        make_shards(mesh),
        mesh=mesh,
        in_specs=(
            P(None, "rp", "re", None, None),
            P(None, "rp"),
            P(),
            P(None, "grp"),
            P(None, "grp"),
            P(("grp", "rp"), None, None, None),
        ),
        out_specs=P(("grp", "rp"), None, "re", None, None),
        check_vma=False,
    )
```

time: 25.2 us -> 22 us (0.87)
  waiting for transfers between devices: 9.66 us -> 8.1 us
  starting transfers between devices: 8.71 us -> 7.78 us
  Pallas kernels: 6.43 us -> 5.74 us
    pallas_call x1, Pallas kernels: 5.59 us -> 4.01 us  [shards(): pl.pallas_call(lambda *refs: phase_kernel(bits, *refs), out_shape=(jax.Sh...]
    ppermute x3 -> x4, starting transfers between devices: 8.19 us -> 7.26 us  [the longest x3 4.61 us: swap(): lax.ppermute(block, 'rp', [(r, r ^ offset) for r in range(ranks)])]
    ppermute x1, waiting for transfers between devices: 1.35 us -> 0.45 us  [shards(): got = lax.ppermute(send, 're', [(c, c ^ 1) for c in range(cores)])]
    pallas_call x0 -> x1, Pallas kernels: none -> 0.89 us  [shards(): pl.pallas_call(keep_kernel, out_shape=(jax.ShapeDtypeStruct(shape, jnp.fl...]
    ppermute x3 -> x4, waiting for transfers between devices: 8.32 us -> 7.65 us  [the longest x3 4.72 us: swap(): lax.ppermute(block, 'rp', [(r, r ^ offset) for r in range(ranks)])]
  transfers between devices with their start and end apart: 4 -> 5, of which waited for: 4 -> 5; matrix products, arithmetic and copies ran while one was open for 0% -> 0% of each run, Pallas kernels for 0% -> 4%
where the time goes in v3:
time: 22 us; the launch traced here: 21.9 us
  waiting for transfers between devices  8.1 us (37%)
  starting transfers between devices  7.78 us (35%)
  Pallas kernels  5.74 us (26%)
    ppermute x3, waiting for transfers between devices, swap(): lax.ppermute(block, 'rp', [(r, r ^ offset) for r in range(ranks)])  4.72 us
    ppermute x3, starting transfers between devices, swap(): lax.ppermute(block, 'rp', [(r, r ^ offset) for r in range(ranks)])  4.61 us
    pallas_call x1, Pallas kernels, shards(): pl.pallas_call(lambda *refs: phase_kernel(bits, *refs), out_shape=(jax.Sh...  4.01 us
    ppermute x1, waiting for transfers between devices, shards(): lax.ppermute(total[half // 2:].astype(jnp.bfloat16), 'rp', [(r, r ^ 1 <<...  2.93 us
    ppermute x1, starting transfers between devices, shards(): lax.ppermute(total[half // 2:].astype(jnp.bfloat16), 'rp', [(r, r ^ 1 <<...  2.65 us
    pallas_call x1, Pallas kernels, shards(): pl.pallas_call(keep_kernel, out_shape=(jax.ShapeDtypeStruct(shape, jnp.fl...  0.89 us
    pallas_call x1, Pallas kernels, shards(): pl.pallas_call(rotate_kernel, out_shape=jax.ShapeDtypeStruct((1, 2, per_c...  0.84 us
    ppermute x1, starting transfers between devices, shards(): got = lax.ppermute(send, 're', [(c, c ^ 1) for c in range(cores)])  0.52 us
  transfers between devices with their start and end apart: 5, of which 5 were waited for; matrix products, arithmetic and copies ran while one was open for 0% of the time, Pallas kernels for 4%

profile of v3, /device:TPU:0, one launch (start us, length us, event | category | flops | bytes accessed | tf_op | source)
XLA Modules:
  0.0 21.9 jit_solution(5060533313029739697)
XLA Ops:
  0.0 4.0 %phase_sums.1 = (f32[3,4,256,256]{3,2,1,0:T(8,128)S(1)}, bf16[8,1,2,48,256]{4,3,2,1,0:T(8,128)(2,1)S(1)}, f32[2,2,4]{2,1,0:T(2,128)S(1)}) custom-call(s32[3,8]{1,0:T(4,128)} %refs_0_.1, s32[2,3]{1,0:T(2,128)} %bitcast.1, s32[3,8]{1,0:T(4,128)} %refs_2_.1, s32[3,32]{1,0:T(4,128)} %refs_3_.1, bf16[2,32,4,48,256]{4,3,2,1,0:T(8,128)(2,1)} %refs_4_.1), custom_call_target="tpu_custom_call" | custom-call | tf_op jit(solution)/shard_map/phase_sums/pallas_call | solution.py:192
  4.0 0.5 %collective-permute-start = (bf16[8,1,2,48,256]{4,3,2,1,0:T(8,128)(2,1)S(1)}, bf16[8,1,2,48,256]{4,3,2,1,0:T(8,128)(2,1)S(1)}, u32[]{:S(2)}, u32[]{:S(2)}) collective-permute-start(bf16[8,1,2,48,256]{4,3,2,1,0:T(8,128)(2,1)S(1)} %get-tuple-element.13), channel_id=1, source_target_pairs={{0,1},{1,0},{2,3},{3,2},{4,5},{5,4},{6,7},{7,6},{8,9},{9,8},{10,11... | collective-permute-start | bytes 1179656 | tf_op jit(solution)/shard_map/ppermute | solution.py:227
  4.5 0.9 %own_k_sums.1 = (f32[8,1,2,48,256]{4,3,2,1,0:T(8,128)S(1)}, bf16[3,96,96]{2,1,0:T(8,128)(2,1)S(1)}) custom-call(f32[3,4,256,256]{3,2,1,0:T(8,128)S(1)} %get-tuple-element.10.prod_ref, f32[2,2,4]{2,1,0:T(2,128)S(1)} %get-tuple-element.11.turn_ref, f32[1,2,48,48]{3,2,1,0:T(8,128)} %eig_hbm.1), custom_call_target="tpu_custom_call" | custom-call | flops 6291456 | bytes 3145728 | tf_op jit(solution)/shard_map/own_k_sums/pallas_call | solution.py:214
  5.4 0.5 %collective-permute-done = bf16[8,1,2,48,256]{4,3,2,1,0:T(8,128)(2,1)S(1)} collective-permute-done((bf16[8,1,2,48,256]{4,3,2,1,0:T(8,128)(2,1)S(1)}, bf16[8,1,2,48,256]{4,3,2,1,0:T(8,128)(2,1)S(1)}, u32[]{:S(2)}, u32[]{:S(2)}) %collective-permute-start) | collective-permute-done | bytes 393248 | tf_op jit(solution)/shard_map/ppermute | solution.py:227
  5.9 0.1 fusion.2
  6.0 4.0 %collective-permute-start.1 = (bf16[2,1,2,48,256]{4,3,2,1,0:T(8,128)(2,1)S(1)}, bf16[2,1,2,48,256]{4,3,2,1,0:T(8,128)(2,1)S(1)}, u32[]{:S(2)}, u32[]{:S(2)}) collective-permute-start(bf16[2,1,2,48,256]{4,3,2,1,0:T(8,128)(2,1)S(1)} %get-tuple-element.17), channel_id=1, source_target_pairs={{0,6},{2,4},{4,2},{6,0},{8,14},{10,12},{12,10},{14,8},{1,7},{3,5},... | collective-permute-start | bytes 294920 | tf_op jit(solution)/shard_map/ppermute | solution.py:231
  10.0 0.5 %collective-permute-start.3 = (bf16[2,1,2,48,256]{4,3,2,1,0:T(8,128)(2,1)S(1)}, bf16[2,1,2,48,256]{4,3,2,1,0:T(8,128)(2,1)S(1)}, u32[]{:S(2)}, u32[]{:S(2)}) collective-permute-start(bf16[2,1,2,48,256]{4,3,2,1,0:T(8,128)(2,1)S(1)} %get-tuple-element.18), channel_id=1, source_target_pairs={{0,2},{2,0},{4,6},{6,4},{8,10},{10,8},{12,14},{14,12},{1,3},{3,1},... | collective-permute-start | bytes 294920 | tf_op jit(solution)/shard_map/ppermute | solution.py:231
  10.5 0.1 collective-permute-start.2
  10.7 2.6 %collective-permute-done.1 = bf16[2,1,2,48,256]{4,3,2,1,0:T(8,128)(2,1)S(1)} collective-permute-done((bf16[2,1,2,48,256]{4,3,2,1,0:T(8,128)(2,1)S(1)}, bf16[2,1,2,48,256]{4,3,2,1,0:T(8,128)(2,1)S(1)}, u32[]{:S(2)}, u32[]{:S(2)}) %collective-permute-start.1) | collective-permute-done | bytes 98336 | tf_op jit(solution)/shard_map/ppermute | solution.py:231
  13.2 2.0 %collective-permute-done.3 = bf16[2,1,2,48,256]{4,3,2,1,0:T(8,128)(2,1)S(1)} collective-permute-done((bf16[2,1,2,48,256]{4,3,2,1,0:T(8,128)(2,1)S(1)}, bf16[2,1,2,48,256]{4,3,2,1,0:T(8,128)(2,1)S(1)}, u32[]{:S(2)}, u32[]{:S(2)}) %collective-permute-start.3) | collective-permute-done | bytes 98336 | tf_op jit(solution)/shard_map/ppermute | solution.py:231
  15.2 0.2 collective-permute-done.2
  15.4 0.1 fusion.1.mine_ref
  15.4 2.7 %collective-permute-start.4 = (bf16[1,1,2,48,256]{4,3,2,1,0:T(8,128)(2,1)S(1)}, bf16[1,1,2,48,256]{4,3,2,1,0:T(8,128)(2,1)S(1)}, u32[]{:S(2)}, u32[]{:S(2)}) collective-permute-start(bf16[1,1,2,48,256]{4,3,2,1,0:T(8,128)(2,1)S(1)} %slice.35), channel_id=1, source_target_pairs={{0,8},{2,10},{4,12},{6,14},{8,0},{10,2},{12,4},{14,6},{1,9},{3,11}... | collective-permute-start | bytes 147464 | tf_op jit(solution)/shard_map/ppermute | solution.py:243
  18.1 2.9 %collective-permute-done.4.got_ref = bf16[1,1,2,48,256]{4,3,2,1,0:T(8,128)(2,1)S(1)} collective-permute-done((bf16[1,1,2,48,256]{4,3,2,1,0:T(8,128)(2,1)S(1)}, bf16[1,1,2,48,256]{4,3,2,1,0:T(8,128)(2,1)S(1)}, u32[]{:S(2)}, u32[]{:S(2)}) %collective-permute-start.4) | collective-permute-done | bytes 49184 | tf_op jit(solution)/shard_map/ppermute | solution.py:243
  21.0 0.8 %rotate_modes.1 = bf16[1,2,1,48,256]{4,3,2,1,0:T(8,128)(2,1)} custom-call(f32[2,1,2,48,256]{4,3,2,1,0:T(8,128)S(1)} %fusion.1.mine_ref, bf16[1,1,2,48,256]{4,3,2,1,0:T(8,128)(2,1)S(1)} %collective-permute-done.4.got_ref, bf16[3,96,96]{2,1,0:T(8,128)(2,1)S(1)} %get-tuple-element.14.mixer_ref), custom_call_target="tpu_custom_call" | custom-call | tf_op jit(solution)/shard_map/rotate_modes/pallas_call | solution.py:244
  (2 shorter events, 0.0 us)
Async XLA Ops:
  4.0 1.9 %collective-permute-start = (bf16[8,1,2,48,256]{4,3,2,1,0:T(8,128)(2,1)S(1)}, bf16[8,1,2,48,256]{4,3,2,1,0:T(8,128)(2,1)S(1)}, u32[]{:S(2)}, u32[]{:S(2)}) collective-permute-start(bf16[8,1,2,48,256]{4,3,2,1,0:T(8,128)(2,1)S(1)} %get-tuple-element.13), channel_id=1, source_target_pairs={{0,1},{1,0},{2,3},{3,2},{4,5},{5,4},{6,7},{7,6},{8,9},{9,8},{10,11... | collective-permute-start | bytes 1179656 | tf_op jit(solution)/shard_map/ppermute | solution.py:227
  6.0 7.2 %collective-permute-start.1 = (bf16[2,1,2,48,256]{4,3,2,1,0:T(8,128)(2,1)S(1)}, bf16[2,1,2,48,256]{4,3,2,1,0:T(8,128)(2,1)S(1)}, u32[]{:S(2)}, u32[]{:S(2)}) collective-permute-start(bf16[2,1,2,48,256]{4,3,2,1,0:T(8,128)(2,1)S(1)} %get-tuple-element.17), channel_id=1, source_target_pairs={{0,6},{2,4},{4,2},{6,0},{8,14},{10,12},{12,10},{14,8},{1,7},{3,5},... | collective-permute-start | bytes 294920 | tf_op jit(solution)/shard_map/ppermute | solution.py:231
  10.0 5.2 %collective-permute-start.3 = (bf16[2,1,2,48,256]{4,3,2,1,0:T(8,128)(2,1)S(1)}, bf16[2,1,2,48,256]{4,3,2,1,0:T(8,128)(2,1)S(1)}, u32[]{:S(2)}, u32[]{:S(2)}) collective-permute-start(bf16[2,1,2,48,256]{4,3,2,1,0:T(8,128)(2,1)S(1)} %get-tuple-element.18), channel_id=1, source_target_pairs={{0,2},{2,0},{4,6},{6,4},{8,10},{10,8},{12,14},{14,12},{1,3},{3,1},... | collective-permute-start | bytes 294920 | tf_op jit(solution)/shard_map/ppermute | solution.py:231
  10.5 4.9 %collective-permute-start.2 = (bf16[2,1,2,48,256]{4,3,2,1,0:T(8,128)(2,1)S(1)}, bf16[2,1,2,48,256]{4,3,2,1,0:T(8,128)(2,1)S(1)}, u32[]{:S(2)}, u32[]{:S(2)}) collective-permute-start(bf16[2,1,2,48,256]{4,3,2,1,0:T(8,128)(2,1)S(1)} %get-tuple-element.19), channel_id=1, source_target_pairs={{0,4},{2,6},{4,0},{6,2},{8,12},{10,14},{12,8},{14,10},{1,5},{3,7},... | collective-permute-start | bytes 294920 | tf_op jit(solution)/shard_map/ppermute | solution.py:231
  15.4 5.6 %collective-permute-start.4 = (bf16[1,1,2,48,256]{4,3,2,1,0:T(8,128)(2,1)S(1)}, bf16[1,1,2,48,256]{4,3,2,1,0:T(8,128)(2,1)S(1)}, u32[]{:S(2)}, u32[]{:S(2)}) collective-permute-start(bf16[1,1,2,48,256]{4,3,2,1,0:T(8,128)(2,1)S(1)} %slice.35), channel_id=1, source_target_pairs={{0,8},{2,10},{4,12},{6,14},{8,0},{10,2},{12,4},{14,6},{1,9},{3,11}... | collective-permute-start | bytes 147464 | tf_op jit(solution)/shard_map/ppermute | solution.py:243

commit v4 on v3

--- a/solution.py
+++ b/solution.py
@@ -13,9 +13,15 @@
 ROWS = 16
 
 
-def slot_offset(slot, bits):
-    near = min(NEAR, bits - 1)
-    return (slot >> (bits - near)) | ((slot & ((1 << (bits - near)) - 1)) << near)
+def near_bits(bits):
+    return min(NEAR, bits - 1)
+
+
+def slot_offsets(bits):
+    near = near_bits(bits)
+    last = (1 << near) - 1
+    beyond = [f << near for f in range(1, 1 << (bits - near))]
+    return [last | far for far in (*beyond, 0)], [d | far for d in range(last) for far in beyond] + list(range(last))
 
 
 def wrapped_angle(products):
@@ -54,10 +60,11 @@
     return real, imag
 
 
-def phase_kernel(bits, q_hbm, k_hbm, ev_hbm, rpv_hbm, w_ref, prod_ref, send_ref, turn_ref,
+def phase_kernel(bits, q_hbm, k_hbm, ev_hbm, rpv_hbm, w_ref, prod_ref, first_ref, rest_ref, turn_ref,
                  slabs, lhs, rpv_ref, q_ref, k_ref, ev_ref, sems, small_sems):
     parts, points, slab, modes, pairs = w_ref.shape
-    slots, per_core = send_ref.shape[:2]
+    first_slots, per_core = first_ref.shape[:2]
+    slots = first_slots + rest_ref.shape[0]
     chunks = modes // ROWS
     pieces = sems.shape[1]
 
@@ -91,8 +98,8 @@
     ).astype(jnp.bfloat16)
     vectors = jnp.dot(rpv_ref[...].astype(jnp.bfloat16), spread, preferred_element_type=jnp.float32)
     rows = []
-    for slot in range(slots):
-        q = me ^ slot_offset(slot, bits)
+    for offset in sum(slot_offsets(bits), []):
+        q = me ^ offset
         row = 0.0
         for axis in range(3):
             row = row + q_ref[axis, q].astype(jnp.float32) * vectors[axis : axis + 1, :]
@@ -121,7 +128,11 @@
             for i in range(per_core):
                 sums = k_sum(prod_ref, c, slot, k_cos, k_sin, per_core + i)
                 for part in range(2):
-                    send_ref[slot, i, part, pl.ds(c * ROWS, ROWS), :] = sums[part].astype(send_ref.dtype)
+                    place = (i, part, pl.ds(c * ROWS, ROWS), slice(None))
+                    if slot < first_slots:
+                        first_ref[(slot, *place)] = sums[part].astype(first_ref.dtype)
+                    else:
+                        rest_ref[(slot - first_slots, *place)] = sums[part].astype(rest_ref.dtype)
 
     for c in range(chunks):
         for piece in range(pieces):
@@ -134,17 +145,22 @@
     send_sum(chunks - 1)
 
 
-def keep_kernel(prod_ref, turn_ref, eig_hbm, keep_ref, mixer_ref, eig_ref, sem):
+def keep_kernel(prod_ref, turn_ref, eig_hbm, first_ref, rest_ref, mixer_ref, eig_ref, sem):
     fetch = pltpu.make_async_copy(eig_hbm, eig_ref, sem)
     fetch.start()
-    slots, per_core = keep_ref.shape[:2]
+    first_slots, per_core = first_ref.shape[:2]
+    slots = first_slots + rest_ref.shape[0]
     k_cos, k_sin = turn_ref[0], turn_ref[1]
     for c in range(prod_ref.shape[0]):
         for slot in range(slots):
             for i in range(per_core):
                 sums = k_sum(prod_ref, c, slot, k_cos, k_sin, i)
                 for part in range(2):
-                    keep_ref[slot, i, part, pl.ds(c * ROWS, ROWS), :] = sums[part]
+                    place = (i, part, pl.ds(c * ROWS, ROWS), slice(None))
+                    if slot < first_slots:
+                        first_ref[(slot, *place)] = sums[part]
+                    else:
+                        rest_ref[(slot - first_slots, *place)] = sums[part]
 
     fetch.wait()
     real_vec, imag_vec = eig_ref[0, 0], eig_ref[0, 1]
@@ -157,11 +173,15 @@
     mixer_ref[2] = (rotation - high.astype(jnp.float32)).astype(jnp.bfloat16)
 
 
-def rotate_kernel(mine_ref, got_ref, mixer_ref, out_ref):
+def rotate_kernel(mixer_ref, mine_ref, *refs):
+    *got_refs, out_ref = refs
     modes, pairs = mine_ref.shape[-2:]
     mixer = mixer_ref[...].reshape(-1, 2 * modes)
     for i in range(mine_ref.shape[1]):
-        source = (mine_ref[0, i] + got_ref[0, i].astype(jnp.float32)).reshape(2 * modes, pairs)
+        source = mine_ref[0, i]
+        for got_ref in got_refs:
+            source = source + got_ref[0, i].astype(jnp.float32)
+        source = source.reshape(2 * modes, pairs)
         high = source.astype(jnp.bfloat16)
         low = (source - high.astype(jnp.float32)).astype(jnp.bfloat16)
         stacked = jnp.concatenate([high, low, high], axis=0)
@@ -186,18 +206,21 @@
         slots = q_points.shape[1]
         per_core = k_points.shape[1] // cores
         chunks = modes // ROWS
-        shape = (slots, per_core, 2, modes, pairs)
+        near = near_bits(bits)
+        groups, spans = 1 << near, 1 << (bits - near)
+        block = (per_core, 2, modes, pairs)
+        shapes = [(spans, *block), (slots - spans, *block)]
         pieces = math.gcd(points, PIECES)
         lines = 2 * slots * ROWS
-        prod, send, turn = pl.pallas_call(
+        prod, first_away, rest_away, turn = pl.pallas_call(
             lambda *refs: phase_kernel(bits, *refs),
             out_shape=(
                 jax.ShapeDtypeStruct((chunks, slab, lines, pairs), jnp.float32),
-                jax.ShapeDtypeStruct(shape, jnp.bfloat16),
+                *[jax.ShapeDtypeStruct(shape, jnp.bfloat16) for shape in shapes],
                 jax.ShapeDtypeStruct((2, 2 * per_core, slab), jnp.float32),
             ),
             in_specs=[hbm] * 5,
-            out_specs=(vmem, vmem, vmem),
+            out_specs=(vmem,) * 4,
             scratch_shapes=[
                 pltpu.VMEM((chunks, parts, points, slab, ROWS, pairs), jnp.bfloat16),
                 pltpu.VMEM((lines, parts * points * ROWS), jnp.bfloat16),
@@ -211,44 +234,56 @@
             compiler_params=pltpu.CompilerParams(vmem_limit_bytes=32 * 2**20),
             name="phase_sums",
         )(*[in_hbm(x) for x in (q_points, k_points.T, re_vectors, rp_vectors, weights)])
-        keep, mixer = pl.pallas_call(
+        first_sums, rest_sums, mixer = pl.pallas_call(
             keep_kernel,
             out_shape=(
-                jax.ShapeDtypeStruct(shape, jnp.float32),
+                *[jax.ShapeDtypeStruct(shape, jnp.float32) for shape in shapes],
                 jax.ShapeDtypeStruct((3, 2 * modes, 2 * modes), jnp.bfloat16),
             ),
             in_specs=[vmem, vmem, hbm],
-            out_specs=(vmem, vmem),
+            out_specs=(vmem,) * 3,
             scratch_shapes=[pltpu.VMEM(eigvecs.shape, jnp.float32), pltpu.SemaphoreType.DMA],
             compiler_params=pltpu.CompilerParams(vmem_limit_bytes=4 * 2**20),
             cost_estimate=pl.CostEstimate(flops=8 * prod.size, bytes_accessed=4 * prod.size, transcendentals=0),
             name="own_k_sums",
         )(prod, turn, in_hbm(eigvecs))
-        got = lax.ppermute(send, "re", [(c, c ^ 1) for c in range(cores)])
-        mine = keep + got.astype(jnp.float32)
-
-        def swap(block, offset):
-            return lax.ppermute(block, "rp", [(r, r ^ offset) for r in range(ranks)]).astype(jnp.float32)
-
-        near = min(NEAR, bits - 1)
-        far = bits - near
-        half = slots >> near
-        parcels = {d: mine[d * half : (d + 1) * half].astype(jnp.bfloat16) for d in range(1, 1 << near)}
-        total = mine[:half]
-        for d in sorted(parcels, key=lambda d: -d):
-            total = total + swap(parcels[d], d)
-        for step in range(far - 1):
+
+        def swap(blocks, offset, axis="rp"):
+            size = mesh.shape[axis]
+            ends = [(r, r ^ offset) for r in range(size)]
+            return lax.ppermute(blocks.astype(jnp.bfloat16), axis, ends)
+
+        def wide(blocks):
+            return blocks.astype(jnp.float32)
+
+        first_other = swap(first_away, 1, "re")
+        rest_other = swap(rest_away, 1, "re")
+        last = groups - 1
+        first_sums = first_sums + wide(first_other)
+        rest_sums = rest_sums + wide(rest_other)
+        first_got = swap(first_sums, last)
+        width = spans - 1
+        beyond = [swap(rest_sums[d * width : (d + 1) * width], d) for d in range(1, last)]
+        among = [swap(rest_sums[last * width + d :][:1], d) for d in range(1, last)]
+        total = rest_sums[:width] + wide(first_got[:width])
+        for got in beyond:
+            total = total + wide(got)
+        own = rest_sums[last * width :][:1] + wide(first_got[width:])
+        half = spans // 2
+        while half > 1:
+            got = swap(total[half - 1 :], half << near)
+            total = total[: half - 1] + wide(got[1:])
+            among.append(got[:1])
             half = half // 2
-            total = total[:half] + swap(total[half : 2 * half].astype(jnp.bfloat16), 1 << (bits - 1 - step))
-        got = lax.ppermute(total[half // 2 :].astype(jnp.bfloat16), "rp", [(r, r ^ (1 << near)) for r in range(ranks)])
+        among.append(swap(total, 1 << near))
         return pl.pallas_call(
             rotate_kernel,
             out_shape=jax.ShapeDtypeStruct((1, 2, per_core, modes, pairs), jnp.bfloat16),
-            in_specs=[vmem, vmem, vmem],
+            in_specs=[vmem] * (2 + len(among)),
             out_specs=vmem,
             compiler_params=pltpu.CompilerParams(vmem_limit_bytes=4 * 2**20),
             name="rotate_modes",
-        )(total, got, mixer)
+        )(mixer, own, *among)
 
     return shards
 

time: 22 us -> 20.5 us (0.932)
  waiting for transfers between devices: 8.1 us -> 2.95 us
  starting transfers between devices: 7.78 us -> 11.4 us
    ppermute x5 -> x8, waiting for transfers between devices: 8.1 us -> 2.95 us  [swap(): return lax.ppermute(blocks.astype(jnp.bfloat16), axis, ends)]
    ppermute x5 -> x8, starting transfers between devices: 7.78 us -> 11.4 us  [swap(): return lax.ppermute(blocks.astype(jnp.bfloat16), axis, ends)]
  transfers between devices with their start and end apart: 5 -> 8, of which waited for: 5 -> 2; matrix products, arithmetic and copies ran while one was open for 0% -> 1% of each run, Pallas kernels for 4% -> 4%
where the time goes in v4:
time: 20.5 us; the launch traced here: 20.3 us
  starting transfers between devices  11.4 us (56%)
  Pallas kernels  5.74 us (28%)
  waiting for transfers between devices  2.95 us (14%)
    ppermute x8, starting transfers between devices, swap(): return lax.ppermute(blocks.astype(jnp.bfloat16), axis, ends)  11.4 us
    pallas_call x1, Pallas kernels, shards(): pl.pallas_call(lambda *refs: phase_kernel(bits, *refs), out_shape=(jax.Sh...  4.01 us
    ppermute x8, waiting for transfers between devices, swap(): return lax.ppermute(blocks.astype(jnp.bfloat16), axis, ends)  2.95 us
    pallas_call x1, Pallas kernels, shards(): pl.pallas_call(keep_kernel, out_shape=(*[jax.ShapeDtypeStruct(shape, jnp....  0.89 us
    pallas_call x1, Pallas kernels, shards(): pl.pallas_call(rotate_kernel, out_shape=jax.ShapeDtypeStruct((1, 2, per_c...  0.84 us
  transfers between devices with their start and end apart: 8, of which 2 were waited for; matrix products, arithmetic and copies ran while one was open for 1% of the time, Pallas kernels for 4%

profile of v4, /device:TPU:0, one launch (start us, length us, event | category | flops | bytes accessed | tf_op | source)
XLA Modules:
  0.0 20.3 jit_solution(14160178211717740948)
XLA Ops:
  0.0 4.0 %phase_sums.1 = (f32[3,4,256,256]{3,2,1,0:T(8,128)S(1)}, bf16[2,1,2,48,256]{4,3,2,1,0:T(8,128)(2,1)S(1)}, bf16[6,1,2,48,256]{4,3,2,1,0:T(8,128)(2,1)S(1)}, f32[2,2,4]{2,1,0:T(2,128)S(1)}) custom-call(s32[3,8]{1,0:T(4,128)} %refs_0_.1, s32[2,3]{1,0:T(2,128)} %bitcast.1, s32[3,8]{1,0:T(4,128)} %refs_2_.1, s32[3,32]{1,0:T(4,128)} %refs_3_.1, ...), custom_call_target="tpu_custom_call" | custom-call | tf_op jit(solution)/shard_map/phase_sums/pallas_call | solution.py:215
  4.0 0.5 %collective-permute-start.1 = (bf16[2,1,2,48,256]{4,3,2,1,0:T(8,128)(2,1)S(1)}, bf16[2,1,2,48,256]{4,3,2,1,0:T(8,128)(2,1)S(1)}, u32[]{:S(2)}, u32[]{:S(2)}) collective-permute-start(bf16[2,1,2,48,256]{4,3,2,1,0:T(8,128)(2,1)S(1)} %get-tuple-element.18), channel_id=1, source_target_pairs={{0,1},{1,0},{2,3},{3,2},{4,5},{5,4},{6,7},{7,6},{8,9},{9,8},{10,11... | collective-permute-start | bytes 294920 | tf_op jit(solution)/shard_map/ppermute | solution.py:254
  4.5 0.1 collective-permute-start
  4.6 0.9 %own_k_sums.1 = (f32[2,1,2,48,256]{4,3,2,1,0:T(8,128)S(1)}, f32[6,1,2,48,256]{4,3,2,1,0:T(8,128)S(1)}, bf16[3,96,96]{2,1,0:T(8,128)(2,1)S(1)}) custom-call(f32[3,4,256,256]{3,2,1,0:T(8,128)S(1)} %get-tuple-element.12.prod_ref, f32[2,2,4]{2,1,0:T(2,128)S(1)} %get-tuple-element.13.turn_ref, f32[1,2,48,48]{3,2,1,0:T(8,128)} %eig_hbm.1), custom_call_target="tpu_custom_call" | custom-call | flops 6291456 | bytes 3145728 | tf_op jit(solution)/shard_map/own_k_sums/pallas_call | solution.py:237
  5.5 0.0 collective-permute-done.1
  5.6 4.0 %collective-permute-start.2 = (bf16[2,1,2,48,256]{4,3,2,1,0:T(8,128)(2,1)S(1)}, bf16[2,1,2,48,256]{4,3,2,1,0:T(8,128)(2,1)S(1)}, u32[]{:S(2)}, u32[]{:S(2)}) collective-permute-start(bf16[2,1,2,48,256]{4,3,2,1,0:T(8,128)(2,1)S(1)} %add_convert_fusion), channel_id=1, source_target_pairs={{0,6},{2,4},{4,2},{6,0},{8,14},{10,12},{12,10},{14,8},{1,7},{3,5},... | collective-permute-start | bytes 294920 | tf_op jit(solution)/shard_map/ppermute | solution.py:254
  9.6 0.0 collective-permute-done
  9.6 0.1 fusion.3
  9.7 0.6 %collective-permute-start.5 = (bf16[1,1,2,48,256]{4,3,2,1,0:T(8,128)(2,1)S(1)}, bf16[1,1,2,48,256]{4,3,2,1,0:T(8,128)(2,1)S(1)}, u32[]{:S(2)}, u32[]{:S(2)}) collective-permute-start(bf16[1,1,2,48,256]{4,3,2,1,0:T(8,128)(2,1)S(1)} %get-tuple-element.23), channel_id=1, source_target_pairs={{0,2},{2,0},{4,6},{6,4},{8,10},{10,8},{12,14},{14,12},{1,3},{3,1},... | collective-permute-start | bytes 147464 | tf_op jit(solution)/shard_map/ppermute | solution.py:254
  10.3 0.3 %collective-permute-start.6 = (bf16[1,1,2,48,256]{4,3,2,1,0:T(8,128)(2,1)S(1)}, bf16[1,1,2,48,256]{4,3,2,1,0:T(8,128)(2,1)S(1)}, u32[]{:S(2)}, u32[]{:S(2)}) collective-permute-start(bf16[1,1,2,48,256]{4,3,2,1,0:T(8,128)(2,1)S(1)} %get-tuple-element.24), channel_id=1, source_target_pairs={{0,4},{2,6},{4,0},{6,2},{8,12},{10,14},{12,8},{14,10},{1,5},{3,7},... | collective-permute-start | bytes 147464 | tf_op jit(solution)/shard_map/ppermute | solution.py:254
  10.6 1.7 %collective-permute-start.4 = (bf16[1,1,2,48,256]{4,3,2,1,0:T(8,128)(2,1)S(1)}, bf16[1,1,2,48,256]{4,3,2,1,0:T(8,128)(2,1)S(1)}, u32[]{:S(2)}, u32[]{:S(2)}) collective-permute-start(bf16[1,1,2,48,256]{4,3,2,1,0:T(8,128)(2,1)S(1)} %get-tuple-element.25), channel_id=1, source_target_pairs={{0,4},{2,6},{4,0},{6,2},{8,12},{10,14},{12,8},{14,10},{1,5},{3,7},... | collective-permute-start | bytes 147464 | tf_op jit(solution)/shard_map/ppermute | solution.py:254
  12.3 1.5 %collective-permute-start.3 = (bf16[1,1,2,48,256]{4,3,2,1,0:T(8,128)(2,1)S(1)}, bf16[1,1,2,48,256]{4,3,2,1,0:T(8,128)(2,1)S(1)}, u32[]{:S(2)}, u32[]{:S(2)}) collective-permute-start(bf16[1,1,2,48,256]{4,3,2,1,0:T(8,128)(2,1)S(1)} %get-tuple-element.26), channel_id=1, source_target_pairs={{0,2},{2,0},{4,6},{6,4},{8,10},{10,8},{12,14},{14,12},{1,3},{3,1},... | collective-permute-start | bytes 147464 | tf_op jit(solution)/shard_map/ppermute | solution.py:254
  13.8 0.0 collective-permute-done.2
  13.8 0.0 collective-permute-done.5
  13.9 0.5 %collective-permute-done.6 = bf16[1,1,2,48,256]{4,3,2,1,0:T(8,128)(2,1)S(1)} collective-permute-done((bf16[1,1,2,48,256]{4,3,2,1,0:T(8,128)(2,1)S(1)}, bf16[1,1,2,48,256]{4,3,2,1,0:T(8,128)(2,1)S(1)}, u32[]{:S(2)}, u32[]{:S(2)}) %collective-permute-start.6) | collective-permute-done | bytes 49184 | tf_op jit(solution)/shard_map/ppermute | solution.py:254
  14.4 2.7 %collective-permute-start.7 = (bf16[1,1,2,48,256]{4,3,2,1,0:T(8,128)(2,1)S(1)}, bf16[1,1,2,48,256]{4,3,2,1,0:T(8,128)(2,1)S(1)}, u32[]{:S(2)}, u32[]{:S(2)}) collective-permute-start(bf16[1,1,2,48,256]{4,3,2,1,0:T(8,128)(2,1)S(1)} %get-tuple-element.21), channel_id=1, source_target_pairs={{0,8},{2,10},{4,12},{6,14},{8,0},{10,2},{12,4},{14,6},{1,9},{3,11}... | collective-permute-start | bytes 147464 | tf_op jit(solution)/shard_map/ppermute | solution.py:254
  17.1 0.0 collective-permute-done.4.refs_1_
  17.1 0.0 collective-permute-done.3.refs_0_
  17.1 2.4 %collective-permute-done.7.refs_2_ = bf16[1,1,2,48,256]{4,3,2,1,0:T(8,128)(2,1)S(1)} collective-permute-done((bf16[1,1,2,48,256]{4,3,2,1,0:T(8,128)(2,1)S(1)}, bf16[1,1,2,48,256]{4,3,2,1,0:T(8,128)(2,1)S(1)}, u32[]{:S(2)}, u32[]{:S(2)}) %collective-permute-start.7) | collective-permute-done | bytes 49184 | tf_op jit(solution)/shard_map/ppermute | solution.py:254
  19.5 0.8 %rotate_modes.1 = bf16[1,2,1,48,256]{4,3,2,1,0:T(8,128)(2,1)} custom-call(bf16[3,96,96]{2,1,0:T(8,128)(2,1)S(1)} %get-tuple-element.14.mixer_ref, f32[1,1,2,48,256]{4,3,2,1,0:T(8,128)S(1)} %get-tuple-element.22.mine_ref, bf16[1,1,2,48,256]{4,3,2,1,0:T(8,128)(2,1)S(1)} %collective-permute-done.3.refs_0_, ...), custom_call_target="tpu_custom_call" | custom-call | tf_op jit(solution)/shard_map/rotate_modes/pallas_call | solution.py:279
  (3 shorter events, 0.1 us)
Async XLA Ops:
  4.0 1.5 %collective-permute-start.1 = (bf16[2,1,2,48,256]{4,3,2,1,0:T(8,128)(2,1)S(1)}, bf16[2,1,2,48,256]{4,3,2,1,0:T(8,128)(2,1)S(1)}, u32[]{:S(2)}, u32[]{:S(2)}) collective-permute-start(bf16[2,1,2,48,256]{4,3,2,1,0:T(8,128)(2,1)S(1)} %get-tuple-element.18), channel_id=1, source_target_pairs={{0,1},{1,0},{2,3},{3,2},{4,5},{5,4},{6,7},{7,6},{8,9},{9,8},{10,11... | collective-permute-start | bytes 294920 | tf_op jit(solution)/shard_map/ppermute | solution.py:254
  4.5 5.0 %collective-permute-start = (bf16[6,1,2,48,256]{4,3,2,1,0:T(8,128)(2,1)S(1)}, bf16[6,1,2,48,256]{4,3,2,1,0:T(8,128)(2,1)S(1)}, u32[]{:S(2)}, u32[]{:S(2)}) collective-permute-start(bf16[6,1,2,48,256]{4,3,2,1,0:T(8,128)(2,1)S(1)} %get-tuple-element.16), channel_id=1, source_target_pairs={{0,1},{1,0},{2,3},{3,2},{4,5},{5,4},{6,7},{7,6},{8,9},{9,8},{10,11... | collective-permute-start | bytes 884744 | tf_op jit(solution)/shard_map/ppermute | solution.py:254
  5.6 8.3 %collective-permute-start.2 = (bf16[2,1,2,48,256]{4,3,2,1,0:T(8,128)(2,1)S(1)}, bf16[2,1,2,48,256]{4,3,2,1,0:T(8,128)(2,1)S(1)}, u32[]{:S(2)}, u32[]{:S(2)}) collective-permute-start(bf16[2,1,2,48,256]{4,3,2,1,0:T(8,128)(2,1)S(1)} %add_convert_fusion), channel_id=1, source_target_pairs={{0,6},{2,4},{4,2},{6,0},{8,14},{10,12},{12,10},{14,8},{1,7},{3,5},... | collective-permute-start | bytes 294920 | tf_op jit(solution)/shard_map/ppermute | solution.py:254
  9.7 4.2 %collective-permute-start.5 = (bf16[1,1,2,48,256]{4,3,2,1,0:T(8,128)(2,1)S(1)}, bf16[1,1,2,48,256]{4,3,2,1,0:T(8,128)(2,1)S(1)}, u32[]{:S(2)}, u32[]{:S(2)}) collective-permute-start(bf16[1,1,2,48,256]{4,3,2,1,0:T(8,128)(2,1)S(1)} %get-tuple-element.23), channel_id=1, source_target_pairs={{0,2},{2,0},{4,6},{6,4},{8,10},{10,8},{12,14},{14,12},{1,3},{3,1},... | collective-permute-start | bytes 147464 | tf_op jit(solution)/shard_map/ppermute | solution.py:254
  10.3 4.1 %collective-permute-start.6 = (bf16[1,1,2,48,256]{4,3,2,1,0:T(8,128)(2,1)S(1)}, bf16[1,1,2,48,256]{4,3,2,1,0:T(8,128)(2,1)S(1)}, u32[]{:S(2)}, u32[]{:S(2)}) collective-permute-start(bf16[1,1,2,48,256]{4,3,2,1,0:T(8,128)(2,1)S(1)} %get-tuple-element.24), channel_id=1, source_target_pairs={{0,4},{2,6},{4,0},{6,2},{8,12},{10,14},{12,8},{14,10},{1,5},{3,7},... | collective-permute-start | bytes 147464 | tf_op jit(solution)/shard_map/ppermute | solution.py:254
  10.6 6.5 %collective-permute-start.4 = (bf16[1,1,2,48,256]{4,3,2,1,0:T(8,128)(2,1)S(1)}, bf16[1,1,2,48,256]{4,3,2,1,0:T(8,128)(2,1)S(1)}, u32[]{:S(2)}, u32[]{:S(2)}) collective-permute-start(bf16[1,1,2,48,256]{4,3,2,1,0:T(8,128)(2,1)S(1)} %get-tuple-element.25), channel_id=1, source_target_pairs={{0,4},{2,6},{4,0},{6,2},{8,12},{10,14},{12,8},{14,10},{1,5},{3,7},... | collective-permute-start | bytes 147464 | tf_op jit(solution)/shard_map/ppermute | solution.py:254
  12.3 4.8 %collective-permute-start.3 = (bf16[1,1,2,48,256]{4,3,2,1,0:T(8,128)(2,1)S(1)}, bf16[1,1,2,48,256]{4,3,2,1,0:T(8,128)(2,1)S(1)}, u32[]{:S(2)}, u32[]{:S(2)}) collective-permute-start(bf16[1,1,2,48,256]{4,3,2,1,0:T(8,128)(2,1)S(1)} %get-tuple-element.26), channel_id=1, source_target_pairs={{0,2},{2,0},{4,6},{6,4},{8,10},{10,8},{12,14},{14,12},{1,3},{3,1},... | collective-permute-start | bytes 147464 | tf_op jit(solution)/shard_map/ppermute | solution.py:254
  14.4 5.1 %collective-permute-start.7 = (bf16[1,1,2,48,256]{4,3,2,1,0:T(8,128)(2,1)S(1)}, bf16[1,1,2,48,256]{4,3,2,1,0:T(8,128)(2,1)S(1)}, u32[]{:S(2)}, u32[]{:S(2)}) collective-permute-start(bf16[1,1,2,48,256]{4,3,2,1,0:T(8,128)(2,1)S(1)} %get-tuple-element.21), channel_id=1, source_target_pairs={{0,8},{2,10},{4,12},{6,14},{8,0},{10,2},{12,4},{14,6},{1,9},{3,11}... | collective-permute-start | bytes 147464 | tf_op jit(solution)/shard_map/ppermute | solution.py:254

commit v5 on v4

--- a/solution.py
+++ b/solution.py
@@ -60,8 +60,8 @@
     return real, imag
 
 
-def phase_kernel(bits, q_hbm, k_hbm, ev_hbm, rpv_hbm, w_ref, prod_ref, first_ref, rest_ref, turn_ref,
-                 slabs, lhs, rpv_ref, q_ref, k_ref, ev_ref, sems, small_sems):
+def phase_kernel(bits, q_hbm, k_hbm, ev_hbm, rpv_hbm, eig_hbm, w_ref, prod_ref, first_ref, rest_ref, turn_ref, mixer_ref,
+                 slabs, lhs, rpv_ref, eig_ref, q_ref, k_ref, ev_ref, sems, small_sems):
     parts, points, slab, modes, pairs = w_ref.shape
     first_slots, per_core = first_ref.shape[:2]
     slots = first_slots + rest_ref.shape[0]
@@ -71,7 +71,7 @@
     small = [
         pltpu.make_async_copy(source, target, small_sems.at[at])
         for at, (source, target) in enumerate(
-            [(rpv_hbm, rpv_ref), (q_hbm, q_ref), (k_hbm, k_ref), (ev_hbm, ev_ref)]
+            [(rpv_hbm, rpv_ref), (q_hbm, q_ref), (k_hbm, k_ref), (ev_hbm, ev_ref), (eig_hbm, eig_ref)]
         )
     ]
     for copy in small:
@@ -123,6 +123,15 @@
     turn_ref[0] = k_cos
     turn_ref[1] = k_sin
 
+    real_vec, imag_vec = eig_ref[0, 0], eig_ref[0, 1]
+    rotation = jnp.concatenate(
+        [jnp.concatenate([real_vec, imag_vec], axis=1), jnp.concatenate([-imag_vec, real_vec], axis=1)], axis=0
+    )
+    high = rotation.astype(jnp.bfloat16)
+    mixer_ref[0] = high
+    mixer_ref[1] = high
+    mixer_ref[2] = (rotation - high.astype(jnp.float32)).astype(jnp.bfloat16)
+
     def send_sum(c):
         for slot in range(slots):
             for i in range(per_core):
@@ -135,19 +144,17 @@
                         rest_ref[(slot - first_slots, *place)] = sums[part].astype(rest_ref.dtype)
 
     for c in range(chunks):
+        if c:
+            send_sum(c - 1)
         for piece in range(pieces):
             fetch(c, piece).wait()
         for e in range(slab):
             block = slabs[c, :, :, e].reshape(parts * width, pairs)
             prod_ref[c, e] = jnp.dot(lhs[...], block, preferred_element_type=jnp.float32)
-        if c:
-            send_sum(c - 1)
     send_sum(chunks - 1)
 
 
-def keep_kernel(prod_ref, turn_ref, eig_hbm, first_ref, rest_ref, mixer_ref, eig_ref, sem):
-    fetch = pltpu.make_async_copy(eig_hbm, eig_ref, sem)
-    fetch.start()
+def keep_kernel(prod_ref, turn_ref, first_ref, rest_ref):
     first_slots, per_core = first_ref.shape[:2]
     slots = first_slots + rest_ref.shape[0]
     k_cos, k_sin = turn_ref[0], turn_ref[1]
@@ -161,16 +168,6 @@
                         first_ref[(slot, *place)] = sums[part]
                     else:
                         rest_ref[(slot - first_slots, *place)] = sums[part]
-
-    fetch.wait()
-    real_vec, imag_vec = eig_ref[0, 0], eig_ref[0, 1]
-    rotation = jnp.concatenate(
-        [jnp.concatenate([real_vec, imag_vec], axis=1), jnp.concatenate([-imag_vec, real_vec], axis=1)], axis=0
-    )
-    high = rotation.astype(jnp.bfloat16)
-    mixer_ref[0] = high
-    mixer_ref[1] = high
-    mixer_ref[2] = (rotation - high.astype(jnp.float32)).astype(jnp.bfloat16)
 
 
 def rotate_kernel(mixer_ref, mine_ref, *refs):
@@ -212,41 +209,39 @@
         shapes = [(spans, *block), (slots - spans, *block)]
         pieces = math.gcd(points, PIECES)
         lines = 2 * slots * ROWS
-        prod, first_away, rest_away, turn = pl.pallas_call(
+        prod, first_away, rest_away, turn, mixer = pl.pallas_call(
             lambda *refs: phase_kernel(bits, *refs),
             out_shape=(
                 jax.ShapeDtypeStruct((chunks, slab, lines, pairs), jnp.float32),
                 *[jax.ShapeDtypeStruct(shape, jnp.bfloat16) for shape in shapes],
                 jax.ShapeDtypeStruct((2, 2 * per_core, slab), jnp.float32),
+                jax.ShapeDtypeStruct((3, 2 * modes, 2 * modes), jnp.bfloat16),
             ),
-            in_specs=[hbm] * 5,
-            out_specs=(vmem,) * 4,
+            in_specs=[hbm] * 6,
+            out_specs=(vmem,) * 5,
             scratch_shapes=[
                 pltpu.VMEM((chunks, parts, points, slab, ROWS, pairs), jnp.bfloat16),
                 pltpu.VMEM((lines, parts * points * ROWS), jnp.bfloat16),
                 pltpu.VMEM(rp_vectors.shape, jnp.int32),
+                pltpu.VMEM(eigvecs.shape, jnp.float32),
                 pltpu.SMEM(q_points.shape, jnp.int32),
                 pltpu.SMEM(k_points.shape[::-1], jnp.int32),
                 pltpu.SMEM(re_vectors.shape, jnp.int32),
                 pltpu.SemaphoreType.DMA((chunks, pieces)),
-                pltpu.SemaphoreType.DMA((4,)),
+                pltpu.SemaphoreType.DMA((5,)),
             ],
-            compiler_params=pltpu.CompilerParams(vmem_limit_bytes=32 * 2**20),
+            compiler_params=pltpu.CompilerParams(vmem_limit_bytes=16 * 2**20),
             name="phase_sums",
-        )(*[in_hbm(x) for x in (q_points, k_points.T, re_vectors, rp_vectors, weights)])
-        first_sums, rest_sums, mixer = pl.pallas_call(
+        )(*[in_hbm(x) for x in (q_points, k_points.T, re_vectors, rp_vectors, eigvecs, weights)])
+        first_sums, rest_sums = pl.pallas_call(
             keep_kernel,
-            out_shape=(
-                *[jax.ShapeDtypeStruct(shape, jnp.float32) for shape in shapes],
-                jax.ShapeDtypeStruct((3, 2 * modes, 2 * modes), jnp.bfloat16),
-            ),
-            in_specs=[vmem, vmem, hbm],
-            out_specs=(vmem,) * 3,
-            scratch_shapes=[pltpu.VMEM(eigvecs.shape, jnp.float32), pltpu.SemaphoreType.DMA],
+            out_shape=[jax.ShapeDtypeStruct(shape, jnp.float32) for shape in shapes],
+            in_specs=[vmem, vmem],
+            out_specs=[vmem, vmem],
             compiler_params=pltpu.CompilerParams(vmem_limit_bytes=4 * 2**20),
             cost_estimate=pl.CostEstimate(flops=8 * prod.size, bytes_accessed=4 * prod.size, transcendentals=0),
             name="own_k_sums",
-        )(prod, turn, in_hbm(eigvecs))
+        )(prod, turn)
 
         def swap(blocks, offset, axis="rp"):
             size = mesh.shape[axis]

time: 20.5 us -> 20.3 us (level)
  Pallas kernels: 5.74 us -> 5.24 us
  waiting for transfers between devices: 2.95 us -> 3.4 us
    ppermute x8, waiting for transfers between devices: 2.95 us -> 3.4 us  [swap(): return lax.ppermute(blocks.astype(jnp.bfloat16), axis, ends)]
    pallas_call x1, Pallas kernels: 0.89 us -> 0.48 us  [shards(): pl.pallas_call(keep_kernel, out_shape=[jax.ShapeDtypeStruct(shape, jnp.fl...]
  transfers between devices with their start and end apart: 8 -> 8, of which waited for: 2 -> 3; matrix products, arithmetic and copies ran while one was open for 1% -> 1% of each run, Pallas kernels for 4% -> 2%
where the time goes in v5:
time: 20.3 us; the launch traced here: 20.2 us
  starting transfers between devices  11.3 us (56%)
  Pallas kernels  5.24 us (26%)
  waiting for transfers between devices  3.4 us (17%)
    ppermute x8, starting transfers between devices, swap(): return lax.ppermute(blocks.astype(jnp.bfloat16), axis, ends)  11.3 us
    pallas_call x1, Pallas kernels, shards(): pl.pallas_call(lambda *refs: phase_kernel(bits, *refs), out_shape=(jax.Sh...  3.92 us
    ppermute x8, waiting for transfers between devices, swap(): return lax.ppermute(blocks.astype(jnp.bfloat16), axis, ends)  3.4 us
    pallas_call x1, Pallas kernels, shards(): pl.pallas_call(rotate_kernel, out_shape=jax.ShapeDtypeStruct((1, 2, per_c...  0.84 us
    pallas_call x1, Pallas kernels, shards(): pl.pallas_call(keep_kernel, out_shape=[jax.ShapeDtypeStruct(shape, jnp.fl...  0.48 us
  transfers between devices with their start and end apart: 8, of which 3 were waited for; matrix products, arithmetic and copies ran while one was open for 1% of the time, Pallas kernels for 2%

profile of v5, /device:TPU:0, one launch (start us, length us, event | category | flops | bytes accessed | tf_op | source)
XLA Modules:
  0.0 20.2 jit_solution(11320111270507347119)
XLA Ops:
  0.0 3.9 %phase_sums.1 = (f32[3,4,256,256]{3,2,1,0:T(8,128)S(1)}, bf16[2,1,2,48,256]{4,3,2,1,0:T(8,128)(2,1)S(1)}, bf16[6,1,2,48,256]{4,3,2,1,0:T(8,128)(2,1)S(1)}, f32[2,2,4]{2,1,0:T(2,128)S(1)}, bf16[3,96,96]{2,1,0:T(8,128)(2,1)S(1)}) custom-call(s32[3,8]{1,0:T(4,128)} %refs_0_.1, s32[2,3]{1,0:T(2,128)} %bitcast.1, s32[3,8]{1,0:T(4,128)} %refs_2_.1, ...), custom_call_target="tpu_custom_call" | custom-call | tf_op jit(solution)/shard_map/phase_sums/pallas_call | solution.py:212
  3.9 0.5 %collective-permute-start.1 = (bf16[2,1,2,48,256]{4,3,2,1,0:T(8,128)(2,1)S(1)}, bf16[2,1,2,48,256]{4,3,2,1,0:T(8,128)(2,1)S(1)}, u32[]{:S(2)}, u32[]{:S(2)}) collective-permute-start(bf16[2,1,2,48,256]{4,3,2,1,0:T(8,128)(2,1)S(1)} %get-tuple-element.18), channel_id=1, source_target_pairs={{0,1},{1,0},{2,3},{3,2},{4,5},{5,4},{6,7},{7,6},{8,9},{9,8},{10,11... | collective-permute-start | bytes 294920 | tf_op jit(solution)/shard_map/ppermute | solution.py:249
  4.4 0.1 collective-permute-start
  4.5 0.5 %own_k_sums.1 = (f32[2,1,2,48,256]{4,3,2,1,0:T(8,128)S(1)}, f32[6,1,2,48,256]{4,3,2,1,0:T(8,128)S(1)}) custom-call(f32[3,4,256,256]{3,2,1,0:T(8,128)S(1)} %get-tuple-element.13.prod_ref, f32[2,2,4]{2,1,0:T(2,128)S(1)} %get-tuple-element.14.turn_ref), custom_call_target="tpu_custom_call" | custom-call | flops 6291456 | bytes 3145728 | tf_op jit(solution)/shard_map/own_k_sums/pallas_call | solution.py:236
  5.0 0.4 %collective-permute-done.1 = bf16[2,1,2,48,256]{4,3,2,1,0:T(8,128)(2,1)S(1)} collective-permute-done((bf16[2,1,2,48,256]{4,3,2,1,0:T(8,128)(2,1)S(1)}, bf16[2,1,2,48,256]{4,3,2,1,0:T(8,128)(2,1)S(1)}, u32[]{:S(2)}, u32[]{:S(2)}) %collective-permute-start.1) | collective-permute-done | bytes 98336 | tf_op jit(solution)/shard_map/ppermute | solution.py:249
  5.4 3.9 %collective-permute-start.2 = (bf16[2,1,2,48,256]{4,3,2,1,0:T(8,128)(2,1)S(1)}, bf16[2,1,2,48,256]{4,3,2,1,0:T(8,128)(2,1)S(1)}, u32[]{:S(2)}, u32[]{:S(2)}) collective-permute-start(bf16[2,1,2,48,256]{4,3,2,1,0:T(8,128)(2,1)S(1)} %add_convert_fusion), channel_id=1, source_target_pairs={{0,6},{2,4},{4,2},{6,0},{8,14},{10,12},{12,10},{14,8},{1,7},{3,5},... | collective-permute-start | bytes 294920 | tf_op jit(solution)/shard_map/ppermute | solution.py:249
  9.4 0.0 collective-permute-done
  9.4 0.1 fusion.3
  9.5 0.6 %collective-permute-start.5 = (bf16[1,1,2,48,256]{4,3,2,1,0:T(8,128)(2,1)S(1)}, bf16[1,1,2,48,256]{4,3,2,1,0:T(8,128)(2,1)S(1)}, u32[]{:S(2)}, u32[]{:S(2)}) collective-permute-start(bf16[1,1,2,48,256]{4,3,2,1,0:T(8,128)(2,1)S(1)} %get-tuple-element.23), channel_id=1, source_target_pairs={{0,2},{2,0},{4,6},{6,4},{8,10},{10,8},{12,14},{14,12},{1,3},{3,1},... | collective-permute-start | bytes 147464 | tf_op jit(solution)/shard_map/ppermute | solution.py:249
  10.1 0.4 %collective-permute-start.6 = (bf16[1,1,2,48,256]{4,3,2,1,0:T(8,128)(2,1)S(1)}, bf16[1,1,2,48,256]{4,3,2,1,0:T(8,128)(2,1)S(1)}, u32[]{:S(2)}, u32[]{:S(2)}) collective-permute-start(bf16[1,1,2,48,256]{4,3,2,1,0:T(8,128)(2,1)S(1)} %get-tuple-element.24), channel_id=1, source_target_pairs={{0,4},{2,6},{4,0},{6,2},{8,12},{10,14},{12,8},{14,10},{1,5},{3,7},... | collective-permute-start | bytes 147464 | tf_op jit(solution)/shard_map/ppermute | solution.py:249
  10.5 1.6 %collective-permute-start.4 = (bf16[1,1,2,48,256]{4,3,2,1,0:T(8,128)(2,1)S(1)}, bf16[1,1,2,48,256]{4,3,2,1,0:T(8,128)(2,1)S(1)}, u32[]{:S(2)}, u32[]{:S(2)}) collective-permute-start(bf16[1,1,2,48,256]{4,3,2,1,0:T(8,128)(2,1)S(1)} %get-tuple-element.25), channel_id=1, source_target_pairs={{0,4},{2,6},{4,0},{6,2},{8,12},{10,14},{12,8},{14,10},{1,5},{3,7},... | collective-permute-start | bytes 147464 | tf_op jit(solution)/shard_map/ppermute | solution.py:249
  12.1 1.5 %collective-permute-start.3 = (bf16[1,1,2,48,256]{4,3,2,1,0:T(8,128)(2,1)S(1)}, bf16[1,1,2,48,256]{4,3,2,1,0:T(8,128)(2,1)S(1)}, u32[]{:S(2)}, u32[]{:S(2)}) collective-permute-start(bf16[1,1,2,48,256]{4,3,2,1,0:T(8,128)(2,1)S(1)} %get-tuple-element.26), channel_id=1, source_target_pairs={{0,2},{2,0},{4,6},{6,4},{8,10},{10,8},{12,14},{14,12},{1,3},{3,1},... | collective-permute-start | bytes 147464 | tf_op jit(solution)/shard_map/ppermute | solution.py:249
  13.6 0.0 collective-permute-done.2
  13.6 0.0 collective-permute-done.5
  13.6 0.6 %collective-permute-done.6 = bf16[1,1,2,48,256]{4,3,2,1,0:T(8,128)(2,1)S(1)} collective-permute-done((bf16[1,1,2,48,256]{4,3,2,1,0:T(8,128)(2,1)S(1)}, bf16[1,1,2,48,256]{4,3,2,1,0:T(8,128)(2,1)S(1)}, u32[]{:S(2)}, u32[]{:S(2)}) %collective-permute-start.6) | collective-permute-done | bytes 49184 | tf_op jit(solution)/shard_map/ppermute | solution.py:249
  14.3 2.7 %collective-permute-start.7 = (bf16[1,1,2,48,256]{4,3,2,1,0:T(8,128)(2,1)S(1)}, bf16[1,1,2,48,256]{4,3,2,1,0:T(8,128)(2,1)S(1)}, u32[]{:S(2)}, u32[]{:S(2)}) collective-permute-start(bf16[1,1,2,48,256]{4,3,2,1,0:T(8,128)(2,1)S(1)} %get-tuple-element.21), channel_id=1, source_target_pairs={{0,8},{2,10},{4,12},{6,14},{8,0},{10,2},{12,4},{14,6},{1,9},{3,11}... | collective-permute-start | bytes 147464 | tf_op jit(solution)/shard_map/ppermute | solution.py:249
  16.9 0.0 collective-permute-done.4.refs_1_
  16.9 0.0 collective-permute-done.3.refs_0_
  16.9 2.4 %collective-permute-done.7.refs_2_ = bf16[1,1,2,48,256]{4,3,2,1,0:T(8,128)(2,1)S(1)} collective-permute-done((bf16[1,1,2,48,256]{4,3,2,1,0:T(8,128)(2,1)S(1)}, bf16[1,1,2,48,256]{4,3,2,1,0:T(8,128)(2,1)S(1)}, u32[]{:S(2)}, u32[]{:S(2)}) %collective-permute-start.7) | collective-permute-done | bytes 49184 | tf_op jit(solution)/shard_map/ppermute | solution.py:249
  19.3 0.8 %rotate_modes.1 = bf16[1,2,1,48,256]{4,3,2,1,0:T(8,128)(2,1)} custom-call(bf16[3,96,96]{2,1,0:T(8,128)(2,1)S(1)} %get-tuple-element.12.mixer_ref, f32[1,1,2,48,256]{4,3,2,1,0:T(8,128)S(1)} %get-tuple-element.22.mine_ref, bf16[1,1,2,48,256]{4,3,2,1,0:T(8,128)(2,1)S(1)} %collective-permute-done.3.refs_0_, ...), custom_call_target="tpu_custom_call" | custom-call | tf_op jit(solution)/shard_map/rotate_modes/pallas_call | solution.py:274
  (3 shorter events, 0.1 us)
Async XLA Ops:
  3.9 1.5 %collective-permute-start.1 = (bf16[2,1,2,48,256]{4,3,2,1,0:T(8,128)(2,1)S(1)}, bf16[2,1,2,48,256]{4,3,2,1,0:T(8,128)(2,1)S(1)}, u32[]{:S(2)}, u32[]{:S(2)}) collective-permute-start(bf16[2,1,2,48,256]{4,3,2,1,0:T(8,128)(2,1)S(1)} %get-tuple-element.18), channel_id=1, source_target_pairs={{0,1},{1,0},{2,3},{3,2},{4,5},{5,4},{6,7},{7,6},{8,9},{9,8},{10,11... | collective-permute-start | bytes 294920 | tf_op jit(solution)/shard_map/ppermute | solution.py:249
  4.4 4.9 %collective-permute-start = (bf16[6,1,2,48,256]{4,3,2,1,0:T(8,128)(2,1)S(1)}, bf16[6,1,2,48,256]{4,3,2,1,0:T(8,128)(2,1)S(1)}, u32[]{:S(2)}, u32[]{:S(2)}) collective-permute-start(bf16[6,1,2,48,256]{4,3,2,1,0:T(8,128)(2,1)S(1)} %get-tuple-element.16), channel_id=1, source_target_pairs={{0,1},{1,0},{2,3},{3,2},{4,5},{5,4},{6,7},{7,6},{8,9},{9,8},{10,11... | collective-permute-start | bytes 884744 | tf_op jit(solution)/shard_map/ppermute | solution.py:249
  5.4 8.2 %collective-permute-start.2 = (bf16[2,1,2,48,256]{4,3,2,1,0:T(8,128)(2,1)S(1)}, bf16[2,1,2,48,256]{4,3,2,1,0:T(8,128)(2,1)S(1)}, u32[]{:S(2)}, u32[]{:S(2)}) collective-permute-start(bf16[2,1,2,48,256]{4,3,2,1,0:T(8,128)(2,1)S(1)} %add_convert_fusion), channel_id=1, source_target_pairs={{0,6},{2,4},{4,2},{6,0},{8,14},{10,12},{12,10},{14,8},{1,7},{3,5},... | collective-permute-start | bytes 294920 | tf_op jit(solution)/shard_map/ppermute | solution.py:249
  9.5 4.2 %collective-permute-start.5 = (bf16[1,1,2,48,256]{4,3,2,1,0:T(8,128)(2,1)S(1)}, bf16[1,1,2,48,256]{4,3,2,1,0:T(8,128)(2,1)S(1)}, u32[]{:S(2)}, u32[]{:S(2)}) collective-permute-start(bf16[1,1,2,48,256]{4,3,2,1,0:T(8,128)(2,1)S(1)} %get-tuple-element.23), channel_id=1, source_target_pairs={{0,2},{2,0},{4,6},{6,4},{8,10},{10,8},{12,14},{14,12},{1,3},{3,1},... | collective-permute-start | bytes 147464 | tf_op jit(solution)/shard_map/ppermute | solution.py:249
  10.1 4.2 %collective-permute-start.6 = (bf16[1,1,2,48,256]{4,3,2,1,0:T(8,128)(2,1)S(1)}, bf16[1,1,2,48,256]{4,3,2,1,0:T(8,128)(2,1)S(1)}, u32[]{:S(2)}, u32[]{:S(2)}) collective-permute-start(bf16[1,1,2,48,256]{4,3,2,1,0:T(8,128)(2,1)S(1)} %get-tuple-element.24), channel_id=1, source_target_pairs={{0,4},{2,6},{4,0},{6,2},{8,12},{10,14},{12,8},{14,10},{1,5},{3,7},... | collective-permute-start | bytes 147464 | tf_op jit(solution)/shard_map/ppermute | solution.py:249
  10.5 6.5 %collective-permute-start.4 = (bf16[1,1,2,48,256]{4,3,2,1,0:T(8,128)(2,1)S(1)}, bf16[1,1,2,48,256]{4,3,2,1,0:T(8,128)(2,1)S(1)}, u32[]{:S(2)}, u32[]{:S(2)}) collective-permute-start(bf16[1,1,2,48,256]{4,3,2,1,0:T(8,128)(2,1)S(1)} %get-tuple-element.25), channel_id=1, source_target_pairs={{0,4},{2,6},{4,0},{6,2},{8,12},{10,14},{12,8},{14,10},{1,5},{3,7},... | collective-permute-start | bytes 147464 | tf_op jit(solution)/shard_map/ppermute | solution.py:249
  12.1 4.8 %collective-permute-start.3 = (bf16[1,1,2,48,256]{4,3,2,1,0:T(8,128)(2,1)S(1)}, bf16[1,1,2,48,256]{4,3,2,1,0:T(8,128)(2,1)S(1)}, u32[]{:S(2)}, u32[]{:S(2)}) collective-permute-start(bf16[1,1,2,48,256]{4,3,2,1,0:T(8,128)(2,1)S(1)} %get-tuple-element.26), channel_id=1, source_target_pairs={{0,2},{2,0},{4,6},{6,4},{8,10},{10,8},{12,14},{14,12},{1,3},{3,1},... | collective-permute-start | bytes 147464 | tf_op jit(solution)/shard_map/ppermute | solution.py:249
  14.3 5.1 %collective-permute-start.7 = (bf16[1,1,2,48,256]{4,3,2,1,0:T(8,128)(2,1)S(1)}, bf16[1,1,2,48,256]{4,3,2,1,0:T(8,128)(2,1)S(1)}, u32[]{:S(2)}, u32[]{:S(2)}) collective-permute-start(bf16[1,1,2,48,256]{4,3,2,1,0:T(8,128)(2,1)S(1)} %get-tuple-element.21), channel_id=1, source_target_pairs={{0,8},{2,10},{4,12},{6,14},{8,0},{10,2},{12,4},{14,6},{1,9},{3,11}... | collective-permute-start | bytes 147464 | tf_op jit(solution)/shard_map/ppermute | solution.py:249

commit v6 on v5

--- a/solution.py
+++ b/solution.py
@@ -170,7 +170,11 @@
                         rest_ref[(slot - first_slots, *place)] = sums[part]
 
 
-def rotate_kernel(mixer_ref, mine_ref, *refs):
+def turn_by(mixer, source):
+    return lax.dot_general(mixer, source, (((0,), (0,)), ((), ())), preferred_element_type=jnp.float32)
+
+
+def early_kernel(mixer_ref, mine_ref, *refs):
     *got_refs, out_ref = refs
     modes, pairs = mine_ref.shape[-2:]
     mixer = mixer_ref[...].reshape(-1, 2 * modes)
@@ -181,10 +185,15 @@
         source = source.reshape(2 * modes, pairs)
         high = source.astype(jnp.bfloat16)
         low = (source - high.astype(jnp.float32)).astype(jnp.bfloat16)
-        stacked = jnp.concatenate([high, low, high], axis=0)
-        turned = lax.dot_general(
-            mixer, stacked, (((0,), (0,)), ((), ())), preferred_element_type=jnp.float32
-        ).astype(out_ref.dtype)
+        out_ref[i] = turn_by(mixer, jnp.concatenate([high, low, high], axis=0))
+
+
+def late_kernel(mixer_ref, early_ref, got_ref, out_ref):
+    modes, pairs = got_ref.shape[-2:]
+    mixer = mixer_ref[1:].reshape(-1, 2 * modes)
+    for i in range(got_ref.shape[1]):
+        got = got_ref[0, i].reshape(2 * modes, pairs)
+        turned = (early_ref[i] + turn_by(mixer, jnp.concatenate([got, got], axis=0))).astype(out_ref.dtype)
         out_ref[0, 0, i] = turned[:modes]
         out_ref[0, 1, i] = turned[modes:]
 
@@ -258,8 +267,8 @@
         rest_sums = rest_sums + wide(rest_other)
         first_got = swap(first_sums, last)
         width = spans - 1
-        beyond = [swap(rest_sums[d * width : (d + 1) * width], d) for d in range(1, last)]
-        among = [swap(rest_sums[last * width + d :][:1], d) for d in range(1, last)]
+        beyond = [swap(rest_sums[d * width : (d + 1) * width], d) for d in reversed(range(1, last))]
+        among = [swap(rest_sums[last * width + d :][:1], d) for d in reversed(range(1, last))]
         total = rest_sums[:width] + wide(first_got[:width])
         for got in beyond:
             total = total + wide(got)
@@ -270,15 +279,26 @@
             total = total[: half - 1] + wide(got[1:])
             among.append(got[:1])
             half = half // 2
-        among.append(swap(total, 1 << near))
-        return pl.pallas_call(
-            rotate_kernel,
-            out_shape=jax.ShapeDtypeStruct((1, 2, per_core, modes, pairs), jnp.bfloat16),
+        across = swap(total, 1 << near)
+        early = pl.pallas_call(
+            early_kernel,
+            out_shape=jax.ShapeDtypeStruct((per_core, 2 * modes, pairs), jnp.float32),
             in_specs=[vmem] * (2 + len(among)),
             out_specs=vmem,
             compiler_params=pltpu.CompilerParams(vmem_limit_bytes=4 * 2**20),
-            name="rotate_modes",
+            cost_estimate=pl.CostEstimate(
+                flops=2 * mixer.size * per_core * pairs, bytes_accessed=16 * per_core * modes * pairs, transcendentals=0
+            ),
+            name="rotate_early",
         )(mixer, own, *among)
+        return pl.pallas_call(
+            late_kernel,
+            out_shape=jax.ShapeDtypeStruct((1, 2, per_core, modes, pairs), jnp.bfloat16),
+            in_specs=[vmem] * 3,
+            out_specs=vmem,
+            compiler_params=pltpu.CompilerParams(vmem_limit_bytes=4 * 2**20),
+            name="rotate_last",
+        )(mixer, early, across)
 
     return shards
 

time: 20.3 us -> 20.2 us (level)
  waiting for transfers between devices: 3.4 us -> 2.94 us
    ppermute x8, waiting for transfers between devices: 3.4 us -> 2.94 us  [swap(): return lax.ppermute(blocks.astype(jnp.bfloat16), axis, ends)]
    pallas_call x1 -> x2, Pallas kernels: 0.84 us -> 1.02 us  [the longest x1 0.81 us: shards(): pl.pallas_call(late_kernel, out_shape=jax.ShapeDtypeStruct((1, 2, per_cor...]
  transfers between devices with their start and end apart: 8 -> 8, of which waited for: 3 -> 4; matrix products, arithmetic and copies ran while one was open for 1% -> 1% of each run, Pallas kernels for 2% -> 3%
where the time goes in v6:
time: 20.2 us; the launch traced here: 20 us
  starting transfers between devices  11.5 us (57%)
  Pallas kernels  5.42 us (27%)
  waiting for transfers between devices  2.94 us (15%)
    ppermute x8, starting transfers between devices, swap(): return lax.ppermute(blocks.astype(jnp.bfloat16), axis, ends)  11.5 us
    pallas_call x1, Pallas kernels, shards(): pl.pallas_call(lambda *refs: phase_kernel(bits, *refs), out_shape=(jax.Sh...  3.92 us
    ppermute x8, waiting for transfers between devices, swap(): return lax.ppermute(blocks.astype(jnp.bfloat16), axis, ends)  2.94 us
    pallas_call x1, Pallas kernels, shards(): pl.pallas_call(late_kernel, out_shape=jax.ShapeDtypeStruct((1, 2, per_cor...  0.81 us
    pallas_call x1, Pallas kernels, shards(): pl.pallas_call(keep_kernel, out_shape=[jax.ShapeDtypeStruct(shape, jnp.fl...  0.48 us
  transfers between devices with their start and end apart: 8, of which 4 were waited for; matrix products, arithmetic and copies ran while one was open for 1% of the time, Pallas kernels for 3%

profile of v6, /device:TPU:0, one launch (start us, length us, event | category | flops | bytes accessed | tf_op | source)
XLA Modules:
  0.0 20.0 jit_solution(14019315750145384172)
XLA Ops:
  0.0 3.9 %phase_sums.1 = (f32[3,4,256,256]{3,2,1,0:T(8,128)S(1)}, bf16[2,1,2,48,256]{4,3,2,1,0:T(8,128)(2,1)S(1)}, bf16[6,1,2,48,256]{4,3,2,1,0:T(8,128)(2,1)S(1)}, f32[2,2,4]{2,1,0:T(2,128)S(1)}, bf16[3,96,96]{2,1,0:T(8,128)(2,1)S(1)}) custom-call(s32[3,8]{1,0:T(4,128)} %refs_0_.1, s32[2,3]{1,0:T(2,128)} %bitcast.1, s32[3,8]{1,0:T(4,128)} %refs_2_.1, ...), custom_call_target="tpu_custom_call" | custom-call | tf_op jit(solution)/shard_map/phase_sums/pallas_call | solution.py:221
  3.9 0.5 %collective-permute-start.1 = (bf16[2,1,2,48,256]{4,3,2,1,0:T(8,128)(2,1)S(1)}, bf16[2,1,2,48,256]{4,3,2,1,0:T(8,128)(2,1)S(1)}, u32[]{:S(2)}, u32[]{:S(2)}) collective-permute-start(bf16[2,1,2,48,256]{4,3,2,1,0:T(8,128)(2,1)S(1)} %get-tuple-element.18), channel_id=1, source_target_pairs={{0,1},{1,0},{2,3},{3,2},{4,5},{5,4},{6,7},{7,6},{8,9},{9,8},{10,11... | collective-permute-start | bytes 294920 | tf_op jit(solution)/shard_map/ppermute | solution.py:258
  4.4 0.1 collective-permute-start
  4.5 0.5 %own_k_sums.1 = (f32[2,1,2,48,256]{4,3,2,1,0:T(8,128)S(1)}, f32[6,1,2,48,256]{4,3,2,1,0:T(8,128)S(1)}) custom-call(f32[3,4,256,256]{3,2,1,0:T(8,128)S(1)} %get-tuple-element.13.prod_ref, f32[2,2,4]{2,1,0:T(2,128)S(1)} %get-tuple-element.14.turn_ref), custom_call_target="tpu_custom_call" | custom-call | flops 6291456 | bytes 3145728 | tf_op jit(solution)/shard_map/own_k_sums/pallas_call | solution.py:245
  5.0 0.4 %collective-permute-done.1 = bf16[2,1,2,48,256]{4,3,2,1,0:T(8,128)(2,1)S(1)} collective-permute-done((bf16[2,1,2,48,256]{4,3,2,1,0:T(8,128)(2,1)S(1)}, bf16[2,1,2,48,256]{4,3,2,1,0:T(8,128)(2,1)S(1)}, u32[]{:S(2)}, u32[]{:S(2)}) %collective-permute-start.1) | collective-permute-done | bytes 98336 | tf_op jit(solution)/shard_map/ppermute | solution.py:258
  5.4 3.9 %collective-permute-start.2 = (bf16[2,1,2,48,256]{4,3,2,1,0:T(8,128)(2,1)S(1)}, bf16[2,1,2,48,256]{4,3,2,1,0:T(8,128)(2,1)S(1)}, u32[]{:S(2)}, u32[]{:S(2)}) collective-permute-start(bf16[2,1,2,48,256]{4,3,2,1,0:T(8,128)(2,1)S(1)} %add_convert_fusion), channel_id=1, source_target_pairs={{0,6},{2,4},{4,2},{6,0},{8,14},{10,12},{12,10},{14,8},{1,7},{3,5},... | collective-permute-start | bytes 294920 | tf_op jit(solution)/shard_map/ppermute | solution.py:258
  9.4 0.0 collective-permute-done
  9.4 0.1 fusion.3
  9.5 0.5 %collective-permute-start.5 = (bf16[1,1,2,48,256]{4,3,2,1,0:T(8,128)(2,1)S(1)}, bf16[1,1,2,48,256]{4,3,2,1,0:T(8,128)(2,1)S(1)}, u32[]{:S(2)}, u32[]{:S(2)}) collective-permute-start(bf16[1,1,2,48,256]{4,3,2,1,0:T(8,128)(2,1)S(1)} %get-tuple-element.23), channel_id=1, source_target_pairs={{0,4},{2,6},{4,0},{6,2},{8,12},{10,14},{12,8},{14,10},{1,5},{3,7},... | collective-permute-start | bytes 147464 | tf_op jit(solution)/shard_map/ppermute | solution.py:258
  10.0 0.5 %collective-permute-start.6 = (bf16[1,1,2,48,256]{4,3,2,1,0:T(8,128)(2,1)S(1)}, bf16[1,1,2,48,256]{4,3,2,1,0:T(8,128)(2,1)S(1)}, u32[]{:S(2)}, u32[]{:S(2)}) collective-permute-start(bf16[1,1,2,48,256]{4,3,2,1,0:T(8,128)(2,1)S(1)} %get-tuple-element.24), channel_id=1, source_target_pairs={{0,2},{2,0},{4,6},{6,4},{8,10},{10,8},{12,14},{14,12},{1,3},{3,1},... | collective-permute-start | bytes 147464 | tf_op jit(solution)/shard_map/ppermute | solution.py:258
  10.5 1.6 %collective-permute-start.4 = (bf16[1,1,2,48,256]{4,3,2,1,0:T(8,128)(2,1)S(1)}, bf16[1,1,2,48,256]{4,3,2,1,0:T(8,128)(2,1)S(1)}, u32[]{:S(2)}, u32[]{:S(2)}) collective-permute-start(bf16[1,1,2,48,256]{4,3,2,1,0:T(8,128)(2,1)S(1)} %get-tuple-element.25), channel_id=1, source_target_pairs={{0,2},{2,0},{4,6},{6,4},{8,10},{10,8},{12,14},{14,12},{1,3},{3,1},... | collective-permute-start | bytes 147464 | tf_op jit(solution)/shard_map/ppermute | solution.py:258
  12.0 1.6 %collective-permute-start.3 = (bf16[1,1,2,48,256]{4,3,2,1,0:T(8,128)(2,1)S(1)}, bf16[1,1,2,48,256]{4,3,2,1,0:T(8,128)(2,1)S(1)}, u32[]{:S(2)}, u32[]{:S(2)}) collective-permute-start(bf16[1,1,2,48,256]{4,3,2,1,0:T(8,128)(2,1)S(1)} %get-tuple-element.26), channel_id=1, source_target_pairs={{0,4},{2,6},{4,0},{6,2},{8,12},{10,14},{12,8},{14,10},{1,5},{3,7},... | collective-permute-start | bytes 147464 | tf_op jit(solution)/shard_map/ppermute | solution.py:258
  13.6 0.0 collective-permute-done.2
  13.6 0.1 collective-permute-done.5
  13.7 0.5 %collective-permute-done.6 = bf16[1,1,2,48,256]{4,3,2,1,0:T(8,128)(2,1)S(1)} collective-permute-done((bf16[1,1,2,48,256]{4,3,2,1,0:T(8,128)(2,1)S(1)}, bf16[1,1,2,48,256]{4,3,2,1,0:T(8,128)(2,1)S(1)}, u32[]{:S(2)}, u32[]{:S(2)}) %collective-permute-start.6) | collective-permute-done | bytes 49184 | tf_op jit(solution)/shard_map/ppermute | solution.py:258
  14.2 2.8 %collective-permute-start.7 = (bf16[1,1,2,48,256]{4,3,2,1,0:T(8,128)(2,1)S(1)}, bf16[1,1,2,48,256]{4,3,2,1,0:T(8,128)(2,1)S(1)}, u32[]{:S(2)}, u32[]{:S(2)}) collective-permute-start(bf16[1,1,2,48,256]{4,3,2,1,0:T(8,128)(2,1)S(1)} %get-tuple-element.21), channel_id=1, source_target_pairs={{0,8},{2,10},{4,12},{6,14},{8,0},{10,2},{12,4},{14,6},{1,9},{3,11}... | collective-permute-start | bytes 147464 | tf_op jit(solution)/shard_map/ppermute | solution.py:258
  17.0 0.0 collective-permute-done.4.refs_1_
  17.0 0.0 collective-permute-done.3.refs_0_
  17.0 0.2 %rotate_early.1.early_ref = f32[1,96,256]{2,1,0:T(8,128)S(1)} custom-call(bf16[3,96,96]{2,1,0:T(8,128)(2,1)S(1)} %get-tuple-element.12.mixer_ref, f32[1,1,2,48,256]{4,3,2,1,0:T(8,128)S(1)} %get-tuple-element.22.mine_ref, bf16[1,1,2,48,256]{4,3,2,1,0:T(8,128)(2,1)S(1)} %collective-permute-done.3.refs_0_, ...), custom_call_target="tpu_custom_call" | custom-call | flops 14155776 | bytes 196608 | tf_op jit(solution)/shard_map/rotate_early/pallas_call | solution.py:283
  17.2 2.0 %collective-permute-done.7.got_ref = bf16[1,1,2,48,256]{4,3,2,1,0:T(8,128)(2,1)S(1)} collective-permute-done((bf16[1,1,2,48,256]{4,3,2,1,0:T(8,128)(2,1)S(1)}, bf16[1,1,2,48,256]{4,3,2,1,0:T(8,128)(2,1)S(1)}, u32[]{:S(2)}, u32[]{:S(2)}) %collective-permute-start.7) | collective-permute-done | bytes 49184 | tf_op jit(solution)/shard_map/ppermute | solution.py:258
  19.2 0.8 %rotate_last.1 = bf16[1,2,1,48,256]{4,3,2,1,0:T(8,128)(2,1)} custom-call(bf16[3,96,96]{2,1,0:T(8,128)(2,1)S(1)} %get-tuple-element.12.mixer_ref, f32[1,96,256]{2,1,0:T(8,128)S(1)} %rotate_early.1.early_ref, bf16[1,1,2,48,256]{4,3,2,1,0:T(8,128)(2,1)S(1)} %collective-permute-done.7.got_ref), custom_call_target="tpu_custom_call" | custom-call | tf_op jit(solution)/shard_map/rotate_last/pallas_call | solution.py:294
  (3 shorter events, 0.1 us)
Async XLA Ops:
  3.9 1.5 %collective-permute-start.1 = (bf16[2,1,2,48,256]{4,3,2,1,0:T(8,128)(2,1)S(1)}, bf16[2,1,2,48,256]{4,3,2,1,0:T(8,128)(2,1)S(1)}, u32[]{:S(2)}, u32[]{:S(2)}) collective-permute-start(bf16[2,1,2,48,256]{4,3,2,1,0:T(8,128)(2,1)S(1)} %get-tuple-element.18), channel_id=1, source_target_pairs={{0,1},{1,0},{2,3},{3,2},{4,5},{5,4},{6,7},{7,6},{8,9},{9,8},{10,11... | collective-permute-start | bytes 294920 | tf_op jit(solution)/shard_map/ppermute | solution.py:258
  4.4 4.9 %collective-permute-start = (bf16[6,1,2,48,256]{4,3,2,1,0:T(8,128)(2,1)S(1)}, bf16[6,1,2,48,256]{4,3,2,1,0:T(8,128)(2,1)S(1)}, u32[]{:S(2)}, u32[]{:S(2)}) collective-permute-start(bf16[6,1,2,48,256]{4,3,2,1,0:T(8,128)(2,1)S(1)} %get-tuple-element.16), channel_id=1, source_target_pairs={{0,1},{1,0},{2,3},{3,2},{4,5},{5,4},{6,7},{7,6},{8,9},{9,8},{10,11... | collective-permute-start | bytes 884744 | tf_op jit(solution)/shard_map/ppermute | solution.py:258
  5.4 8.2 %collective-permute-start.2 = (bf16[2,1,2,48,256]{4,3,2,1,0:T(8,128)(2,1)S(1)}, bf16[2,1,2,48,256]{4,3,2,1,0:T(8,128)(2,1)S(1)}, u32[]{:S(2)}, u32[]{:S(2)}) collective-permute-start(bf16[2,1,2,48,256]{4,3,2,1,0:T(8,128)(2,1)S(1)} %add_convert_fusion), channel_id=1, source_target_pairs={{0,6},{2,4},{4,2},{6,0},{8,14},{10,12},{12,10},{14,8},{1,7},{3,5},... | collective-permute-start | bytes 294920 | tf_op jit(solution)/shard_map/ppermute | solution.py:258
  9.5 4.2 %collective-permute-start.5 = (bf16[1,1,2,48,256]{4,3,2,1,0:T(8,128)(2,1)S(1)}, bf16[1,1,2,48,256]{4,3,2,1,0:T(8,128)(2,1)S(1)}, u32[]{:S(2)}, u32[]{:S(2)}) collective-permute-start(bf16[1,1,2,48,256]{4,3,2,1,0:T(8,128)(2,1)S(1)} %get-tuple-element.23), channel_id=1, source_target_pairs={{0,4},{2,6},{4,0},{6,2},{8,12},{10,14},{12,8},{14,10},{1,5},{3,7},... | collective-permute-start | bytes 147464 | tf_op jit(solution)/shard_map/ppermute | solution.py:258
  10.0 4.1 %collective-permute-start.6 = (bf16[1,1,2,48,256]{4,3,2,1,0:T(8,128)(2,1)S(1)}, bf16[1,1,2,48,256]{4,3,2,1,0:T(8,128)(2,1)S(1)}, u32[]{:S(2)}, u32[]{:S(2)}) collective-permute-start(bf16[1,1,2,48,256]{4,3,2,1,0:T(8,128)(2,1)S(1)} %get-tuple-element.24), channel_id=1, source_target_pairs={{0,2},{2,0},{4,6},{6,4},{8,10},{10,8},{12,14},{14,12},{1,3},{3,1},... | collective-permute-start | bytes 147464 | tf_op jit(solution)/shard_map/ppermute | solution.py:258
  10.5 6.5 %collective-permute-start.4 = (bf16[1,1,2,48,256]{4,3,2,1,0:T(8,128)(2,1)S(1)}, bf16[1,1,2,48,256]{4,3,2,1,0:T(8,128)(2,1)S(1)}, u32[]{:S(2)}, u32[]{:S(2)}) collective-permute-start(bf16[1,1,2,48,256]{4,3,2,1,0:T(8,128)(2,1)S(1)} %get-tuple-element.25), channel_id=1, source_target_pairs={{0,2},{2,0},{4,6},{6,4},{8,10},{10,8},{12,14},{14,12},{1,3},{3,1},... | collective-permute-start | bytes 147464 | tf_op jit(solution)/shard_map/ppermute | solution.py:258
  12.0 5.0 %collective-permute-start.3 = (bf16[1,1,2,48,256]{4,3,2,1,0:T(8,128)(2,1)S(1)}, bf16[1,1,2,48,256]{4,3,2,1,0:T(8,128)(2,1)S(1)}, u32[]{:S(2)}, u32[]{:S(2)}) collective-permute-start(bf16[1,1,2,48,256]{4,3,2,1,0:T(8,128)(2,1)S(1)} %get-tuple-element.26), channel_id=1, source_target_pairs={{0,4},{2,6},{4,0},{6,2},{8,12},{10,14},{12,8},{14,10},{1,5},{3,7},... | collective-permute-start | bytes 147464 | tf_op jit(solution)/shard_map/ppermute | solution.py:258
  14.2 5.1 %collective-permute-start.7 = (bf16[1,1,2,48,256]{4,3,2,1,0:T(8,128)(2,1)S(1)}, bf16[1,1,2,48,256]{4,3,2,1,0:T(8,128)(2,1)S(1)}, u32[]{:S(2)}, u32[]{:S(2)}) collective-permute-start(bf16[1,1,2,48,256]{4,3,2,1,0:T(8,128)(2,1)S(1)} %get-tuple-element.21), channel_id=1, source_target_pairs={{0,8},{2,10},{4,12},{6,14},{8,0},{10,2},{12,4},{14,6},{1,9},{3,11}... | collective-permute-start | bytes 147464 | tf_op jit(solution)/shard_map/ppermute | solution.py:258

commit v7 on v6

--- a/solution.py
+++ b/solution.py
@@ -127,10 +127,10 @@
     rotation = jnp.concatenate(
         [jnp.concatenate([real_vec, imag_vec], axis=1), jnp.concatenate([-imag_vec, real_vec], axis=1)], axis=0
     )
-    high = rotation.astype(jnp.bfloat16)
-    mixer_ref[0] = high
-    mixer_ref[1] = high
-    mixer_ref[2] = (rotation - high.astype(jnp.float32)).astype(jnp.bfloat16)
+    turned = rotation.T
+    high = turned.astype(jnp.bfloat16)
+    low = (turned - high.astype(jnp.float32)).astype(jnp.bfloat16)
+    mixer_ref[...] = jnp.concatenate([high, low, high], axis=1)
 
     def send_sum(c):
         for slot in range(slots):
@@ -170,14 +170,10 @@
                         rest_ref[(slot - first_slots, *place)] = sums[part]
 
 
-def turn_by(mixer, source):
-    return lax.dot_general(mixer, source, (((0,), (0,)), ((), ())), preferred_element_type=jnp.float32)
-
-
 def early_kernel(mixer_ref, mine_ref, *refs):
     *got_refs, out_ref = refs
     modes, pairs = mine_ref.shape[-2:]
-    mixer = mixer_ref[...].reshape(-1, 2 * modes)
+    mixer = mixer_ref[...]
     for i in range(mine_ref.shape[1]):
         source = mine_ref[0, i]
         for got_ref in got_refs:
@@ -185,15 +181,17 @@
         source = source.reshape(2 * modes, pairs)
         high = source.astype(jnp.bfloat16)
         low = (source - high.astype(jnp.float32)).astype(jnp.bfloat16)
-        out_ref[i] = turn_by(mixer, jnp.concatenate([high, low, high], axis=0))
+        stacked = jnp.concatenate([high, high, low], axis=0)
+        out_ref[i] = jnp.dot(mixer, stacked, preferred_element_type=jnp.float32)
 
 
 def late_kernel(mixer_ref, early_ref, got_ref, out_ref):
     modes, pairs = got_ref.shape[-2:]
-    mixer = mixer_ref[1:].reshape(-1, 2 * modes)
+    mixer = mixer_ref[:, : 4 * modes]
     for i in range(got_ref.shape[1]):
         got = got_ref[0, i].reshape(2 * modes, pairs)
-        turned = (early_ref[i] + turn_by(mixer, jnp.concatenate([got, got], axis=0))).astype(out_ref.dtype)
+        turned = jnp.dot(mixer, jnp.concatenate([got, got], axis=0), preferred_element_type=jnp.float32)
+        turned = (early_ref[i] + turned).astype(out_ref.dtype)
         out_ref[0, 0, i] = turned[:modes]
         out_ref[0, 1, i] = turned[modes:]
 
@@ -224,7 +222,7 @@
                 jax.ShapeDtypeStruct((chunks, slab, lines, pairs), jnp.float32),
                 *[jax.ShapeDtypeStruct(shape, jnp.bfloat16) for shape in shapes],
                 jax.ShapeDtypeStruct((2, 2 * per_core, slab), jnp.float32),
-                jax.ShapeDtypeStruct((3, 2 * modes, 2 * modes), jnp.bfloat16),
+                jax.ShapeDtypeStruct((2 * modes, 6 * modes), jnp.bfloat16),
             ),
             in_specs=[hbm] * 6,
             out_specs=(vmem,) * 5,

time: 20.2 us -> 20.2 us (level)
  no operation moved by 1% of the time
where the time goes in v7:
time: 20.2 us; the launch traced here: 20 us
  starting transfers between devices  11.5 us (57%)
  Pallas kernels  5.35 us (26%)
  waiting for transfers between devices  2.98 us (15%)
    ppermute x8, starting transfers between devices, swap(): return lax.ppermute(blocks.astype(jnp.bfloat16), axis, ends)  11.5 us
    pallas_call x1, Pallas kernels, shards(): pl.pallas_call(lambda *refs: phase_kernel(bits, *refs), out_shape=(jax.Sh...  3.92 us
    ppermute x8, waiting for transfers between devices, swap(): return lax.ppermute(blocks.astype(jnp.bfloat16), axis, ends)  2.98 us
    pallas_call x1, Pallas kernels, shards(): pl.pallas_call(late_kernel, out_shape=jax.ShapeDtypeStruct((1, 2, per_cor...  0.77 us
    pallas_call x1, Pallas kernels, shards(): pl.pallas_call(keep_kernel, out_shape=[jax.ShapeDtypeStruct(shape, jnp.fl...  0.48 us
  transfers between devices with their start and end apart: 8, of which 4 were waited for; matrix products, arithmetic and copies ran while one was open for 1% of the time, Pallas kernels for 3%

profile of v7, /device:TPU:0, one launch (start us, length us, event | category | flops | bytes accessed | tf_op | source)
XLA Modules:
  0.0 20.0 jit_solution(16237423832721839203)
XLA Ops:
  0.0 3.9 %phase_sums.1 = (f32[3,4,256,256]{3,2,1,0:T(8,128)S(1)}, bf16[2,1,2,48,256]{4,3,2,1,0:T(8,128)(2,1)S(1)}, bf16[6,1,2,48,256]{4,3,2,1,0:T(8,128)(2,1)S(1)}, f32[2,2,4]{2,1,0:T(2,128)S(1)}, bf16[96,288]{1,0:T(8,128)(2,1)S(1)}) custom-call(s32[3,8]{1,0:T(4,128)} %refs_0_.1, s32[2,3]{1,0:T(2,128)} %bitcast.1, s32[3,8]{1,0:T(4,128)} %refs_2_.1, s32[3,32]{1,0:T(4,128)} %refs_3_.1, ...), custom_call_target="tpu_custom_call" | custom-call | tf_op jit(solution)/shard_map/phase_sums/pallas_call | solution.py:219
  3.9 0.5 %collective-permute-start.1 = (bf16[2,1,2,48,256]{4,3,2,1,0:T(8,128)(2,1)S(1)}, bf16[2,1,2,48,256]{4,3,2,1,0:T(8,128)(2,1)S(1)}, u32[]{:S(2)}, u32[]{:S(2)}) collective-permute-start(bf16[2,1,2,48,256]{4,3,2,1,0:T(8,128)(2,1)S(1)} %get-tuple-element.18), channel_id=1, source_target_pairs={{0,1},{1,0},{2,3},{3,2},{4,5},{5,4},{6,7},{7,6},{8,9},{9,8},{10,11... | collective-permute-start | bytes 294920 | tf_op jit(solution)/shard_map/ppermute | solution.py:256
  4.4 0.1 collective-permute-start
  4.5 0.5 %own_k_sums.1 = (f32[2,1,2,48,256]{4,3,2,1,0:T(8,128)S(1)}, f32[6,1,2,48,256]{4,3,2,1,0:T(8,128)S(1)}) custom-call(f32[3,4,256,256]{3,2,1,0:T(8,128)S(1)} %get-tuple-element.13.prod_ref, f32[2,2,4]{2,1,0:T(2,128)S(1)} %get-tuple-element.14.turn_ref), custom_call_target="tpu_custom_call" | custom-call | flops 6291456 | bytes 3145728 | tf_op jit(solution)/shard_map/own_k_sums/pallas_call | solution.py:243
  5.0 0.4 %collective-permute-done.1 = bf16[2,1,2,48,256]{4,3,2,1,0:T(8,128)(2,1)S(1)} collective-permute-done((bf16[2,1,2,48,256]{4,3,2,1,0:T(8,128)(2,1)S(1)}, bf16[2,1,2,48,256]{4,3,2,1,0:T(8,128)(2,1)S(1)}, u32[]{:S(2)}, u32[]{:S(2)}) %collective-permute-start.1) | collective-permute-done | bytes 98336 | tf_op jit(solution)/shard_map/ppermute | solution.py:256
  5.4 3.9 %collective-permute-start.2 = (bf16[2,1,2,48,256]{4,3,2,1,0:T(8,128)(2,1)S(1)}, bf16[2,1,2,48,256]{4,3,2,1,0:T(8,128)(2,1)S(1)}, u32[]{:S(2)}, u32[]{:S(2)}) collective-permute-start(bf16[2,1,2,48,256]{4,3,2,1,0:T(8,128)(2,1)S(1)} %add_convert_fusion), channel_id=1, source_target_pairs={{0,6},{2,4},{4,2},{6,0},{8,14},{10,12},{12,10},{14,8},{1,7},{3,5},... | collective-permute-start | bytes 294920 | tf_op jit(solution)/shard_map/ppermute | solution.py:256
  9.4 0.0 collective-permute-done
  9.4 0.1 fusion.3
  9.5 0.5 %collective-permute-start.5 = (bf16[1,1,2,48,256]{4,3,2,1,0:T(8,128)(2,1)S(1)}, bf16[1,1,2,48,256]{4,3,2,1,0:T(8,128)(2,1)S(1)}, u32[]{:S(2)}, u32[]{:S(2)}) collective-permute-start(bf16[1,1,2,48,256]{4,3,2,1,0:T(8,128)(2,1)S(1)} %get-tuple-element.23), channel_id=1, source_target_pairs={{0,4},{2,6},{4,0},{6,2},{8,12},{10,14},{12,8},{14,10},{1,5},{3,7},... | collective-permute-start | bytes 147464 | tf_op jit(solution)/shard_map/ppermute | solution.py:256
  10.0 0.5 %collective-permute-start.6 = (bf16[1,1,2,48,256]{4,3,2,1,0:T(8,128)(2,1)S(1)}, bf16[1,1,2,48,256]{4,3,2,1,0:T(8,128)(2,1)S(1)}, u32[]{:S(2)}, u32[]{:S(2)}) collective-permute-start(bf16[1,1,2,48,256]{4,3,2,1,0:T(8,128)(2,1)S(1)} %get-tuple-element.24), channel_id=1, source_target_pairs={{0,2},{2,0},{4,6},{6,4},{8,10},{10,8},{12,14},{14,12},{1,3},{3,1},... | collective-permute-start | bytes 147464 | tf_op jit(solution)/shard_map/ppermute | solution.py:256
  10.5 1.6 %collective-permute-start.4 = (bf16[1,1,2,48,256]{4,3,2,1,0:T(8,128)(2,1)S(1)}, bf16[1,1,2,48,256]{4,3,2,1,0:T(8,128)(2,1)S(1)}, u32[]{:S(2)}, u32[]{:S(2)}) collective-permute-start(bf16[1,1,2,48,256]{4,3,2,1,0:T(8,128)(2,1)S(1)} %get-tuple-element.25), channel_id=1, source_target_pairs={{0,2},{2,0},{4,6},{6,4},{8,10},{10,8},{12,14},{14,12},{1,3},{3,1},... | collective-permute-start | bytes 147464 | tf_op jit(solution)/shard_map/ppermute | solution.py:256
  12.0 1.6 %collective-permute-start.3 = (bf16[1,1,2,48,256]{4,3,2,1,0:T(8,128)(2,1)S(1)}, bf16[1,1,2,48,256]{4,3,2,1,0:T(8,128)(2,1)S(1)}, u32[]{:S(2)}, u32[]{:S(2)}) collective-permute-start(bf16[1,1,2,48,256]{4,3,2,1,0:T(8,128)(2,1)S(1)} %get-tuple-element.26), channel_id=1, source_target_pairs={{0,4},{2,6},{4,0},{6,2},{8,12},{10,14},{12,8},{14,10},{1,5},{3,7},... | collective-permute-start | bytes 147464 | tf_op jit(solution)/shard_map/ppermute | solution.py:256
  13.6 0.0 collective-permute-done.2
  13.6 0.1 collective-permute-done.5
  13.7 0.5 %collective-permute-done.6 = bf16[1,1,2,48,256]{4,3,2,1,0:T(8,128)(2,1)S(1)} collective-permute-done((bf16[1,1,2,48,256]{4,3,2,1,0:T(8,128)(2,1)S(1)}, bf16[1,1,2,48,256]{4,3,2,1,0:T(8,128)(2,1)S(1)}, u32[]{:S(2)}, u32[]{:S(2)}) %collective-permute-start.6) | collective-permute-done | bytes 49184 | tf_op jit(solution)/shard_map/ppermute | solution.py:256
  14.2 2.8 %collective-permute-start.7 = (bf16[1,1,2,48,256]{4,3,2,1,0:T(8,128)(2,1)S(1)}, bf16[1,1,2,48,256]{4,3,2,1,0:T(8,128)(2,1)S(1)}, u32[]{:S(2)}, u32[]{:S(2)}) collective-permute-start(bf16[1,1,2,48,256]{4,3,2,1,0:T(8,128)(2,1)S(1)} %get-tuple-element.21), channel_id=1, source_target_pairs={{0,8},{2,10},{4,12},{6,14},{8,0},{10,2},{12,4},{14,6},{1,9},{3,11}... | collective-permute-start | bytes 147464 | tf_op jit(solution)/shard_map/ppermute | solution.py:256
  17.0 0.0 collective-permute-done.4.refs_1_
  17.0 0.0 collective-permute-done.3.refs_0_
  17.0 0.2 rotate_early.1.early_ref
  17.2 2.1 %collective-permute-done.7.got_ref = bf16[1,1,2,48,256]{4,3,2,1,0:T(8,128)(2,1)S(1)} collective-permute-done((bf16[1,1,2,48,256]{4,3,2,1,0:T(8,128)(2,1)S(1)}, bf16[1,1,2,48,256]{4,3,2,1,0:T(8,128)(2,1)S(1)}, u32[]{:S(2)}, u32[]{:S(2)}) %collective-permute-start.7) | collective-permute-done | bytes 49184 | tf_op jit(solution)/shard_map/ppermute | solution.py:256
  19.2 0.8 %rotate_last.1 = bf16[1,2,1,48,256]{4,3,2,1,0:T(8,128)(2,1)} custom-call(bf16[96,288]{1,0:T(8,128)(2,1)S(1)} %get-tuple-element.12.mixer_ref, f32[1,96,256]{2,1,0:T(8,128)S(1)} %rotate_early.1.early_ref, bf16[1,1,2,48,256]{4,3,2,1,0:T(8,128)(2,1)S(1)} %collective-permute-done.7.got_ref), custom_call_target="tpu_custom_call" | custom-call | tf_op jit(solution)/shard_map/rotate_last/pallas_call | solution.py:292
  (3 shorter events, 0.1 us)
Async XLA Ops:
  3.9 1.5 %collective-permute-start.1 = (bf16[2,1,2,48,256]{4,3,2,1,0:T(8,128)(2,1)S(1)}, bf16[2,1,2,48,256]{4,3,2,1,0:T(8,128)(2,1)S(1)}, u32[]{:S(2)}, u32[]{:S(2)}) collective-permute-start(bf16[2,1,2,48,256]{4,3,2,1,0:T(8,128)(2,1)S(1)} %get-tuple-element.18), channel_id=1, source_target_pairs={{0,1},{1,0},{2,3},{3,2},{4,5},{5,4},{6,7},{7,6},{8,9},{9,8},{10,11... | collective-permute-start | bytes 294920 | tf_op jit(solution)/shard_map/ppermute | solution.py:256
  4.4 4.9 %collective-permute-start = (bf16[6,1,2,48,256]{4,3,2,1,0:T(8,128)(2,1)S(1)}, bf16[6,1,2,48,256]{4,3,2,1,0:T(8,128)(2,1)S(1)}, u32[]{:S(2)}, u32[]{:S(2)}) collective-permute-start(bf16[6,1,2,48,256]{4,3,2,1,0:T(8,128)(2,1)S(1)} %get-tuple-element.16), channel_id=1, source_target_pairs={{0,1},{1,0},{2,3},{3,2},{4,5},{5,4},{6,7},{7,6},{8,9},{9,8},{10,11... | collective-permute-start | bytes 884744 | tf_op jit(solution)/shard_map/ppermute | solution.py:256
  5.4 8.2 %collective-permute-start.2 = (bf16[2,1,2,48,256]{4,3,2,1,0:T(8,128)(2,1)S(1)}, bf16[2,1,2,48,256]{4,3,2,1,0:T(8,128)(2,1)S(1)}, u32[]{:S(2)}, u32[]{:S(2)}) collective-permute-start(bf16[2,1,2,48,256]{4,3,2,1,0:T(8,128)(2,1)S(1)} %add_convert_fusion), channel_id=1, source_target_pairs={{0,6},{2,4},{4,2},{6,0},{8,14},{10,12},{12,10},{14,8},{1,7},{3,5},... | collective-permute-start | bytes 294920 | tf_op jit(solution)/shard_map/ppermute | solution.py:256
  9.5 4.2 %collective-permute-start.5 = (bf16[1,1,2,48,256]{4,3,2,1,0:T(8,128)(2,1)S(1)}, bf16[1,1,2,48,256]{4,3,2,1,0:T(8,128)(2,1)S(1)}, u32[]{:S(2)}, u32[]{:S(2)}) collective-permute-start(bf16[1,1,2,48,256]{4,3,2,1,0:T(8,128)(2,1)S(1)} %get-tuple-element.23), channel_id=1, source_target_pairs={{0,4},{2,6},{4,0},{6,2},{8,12},{10,14},{12,8},{14,10},{1,5},{3,7},... | collective-permute-start | bytes 147464 | tf_op jit(solution)/shard_map/ppermute | solution.py:256
  10.0 4.1 %collective-permute-start.6 = (bf16[1,1,2,48,256]{4,3,2,1,0:T(8,128)(2,1)S(1)}, bf16[1,1,2,48,256]{4,3,2,1,0:T(8,128)(2,1)S(1)}, u32[]{:S(2)}, u32[]{:S(2)}) collective-permute-start(bf16[1,1,2,48,256]{4,3,2,1,0:T(8,128)(2,1)S(1)} %get-tuple-element.24), channel_id=1, source_target_pairs={{0,2},{2,0},{4,6},{6,4},{8,10},{10,8},{12,14},{14,12},{1,3},{3,1},... | collective-permute-start | bytes 147464 | tf_op jit(solution)/shard_map/ppermute | solution.py:256
  10.5 6.5 %collective-permute-start.4 = (bf16[1,1,2,48,256]{4,3,2,1,0:T(8,128)(2,1)S(1)}, bf16[1,1,2,48,256]{4,3,2,1,0:T(8,128)(2,1)S(1)}, u32[]{:S(2)}, u32[]{:S(2)}) collective-permute-start(bf16[1,1,2,48,256]{4,3,2,1,0:T(8,128)(2,1)S(1)} %get-tuple-element.25), channel_id=1, source_target_pairs={{0,2},{2,0},{4,6},{6,4},{8,10},{10,8},{12,14},{14,12},{1,3},{3,1},... | collective-permute-start | bytes 147464 | tf_op jit(solution)/shard_map/ppermute | solution.py:256
  12.0 5.0 %collective-permute-start.3 = (bf16[1,1,2,48,256]{4,3,2,1,0:T(8,128)(2,1)S(1)}, bf16[1,1,2,48,256]{4,3,2,1,0:T(8,128)(2,1)S(1)}, u32[]{:S(2)}, u32[]{:S(2)}) collective-permute-start(bf16[1,1,2,48,256]{4,3,2,1,0:T(8,128)(2,1)S(1)} %get-tuple-element.26), channel_id=1, source_target_pairs={{0,4},{2,6},{4,0},{6,2},{8,12},{10,14},{12,8},{14,10},{1,5},{3,7},... | collective-permute-start | bytes 147464 | tf_op jit(solution)/shard_map/ppermute | solution.py:256
  14.2 5.1 %collective-permute-start.7 = (bf16[1,1,2,48,256]{4,3,2,1,0:T(8,128)(2,1)S(1)}, bf16[1,1,2,48,256]{4,3,2,1,0:T(8,128)(2,1)S(1)}, u32[]{:S(2)}, u32[]{:S(2)}) collective-permute-start(bf16[1,1,2,48,256]{4,3,2,1,0:T(8,128)(2,1)S(1)} %get-tuple-element.21), channel_id=1, source_target_pairs={{0,8},{2,10},{4,12},{6,14},{8,0},{10,2},{12,4},{14,6},{1,9},{3,11}... | collective-permute-start | bytes 147464 | tf_op jit(solution)/shard_map/ppermute | solution.py:256

commit v8 on v7

--- a/solution.py
+++ b/solution.py
@@ -265,8 +265,8 @@
         rest_sums = rest_sums + wide(rest_other)
         first_got = swap(first_sums, last)
         width = spans - 1
-        beyond = [swap(rest_sums[d * width : (d + 1) * width], d) for d in reversed(range(1, last))]
-        among = [swap(rest_sums[last * width + d :][:1], d) for d in reversed(range(1, last))]
+        beyond = [swap(rest_sums[d * width : (d + 1) * width], d) for d in range(1, last)]
+        among = [swap(rest_sums[last * width + d :][:1], d) for d in range(1, last)]
         total = rest_sums[:width] + wide(first_got[:width])
         for got in beyond:
             total = total + wide(got)

time: 20.2 us -> 20.2 us (level)
  waiting for transfers between devices: 2.98 us -> 3.22 us
    ppermute x8, waiting for transfers between devices: 2.98 us -> 3.22 us  [swap(): return lax.ppermute(blocks.astype(jnp.bfloat16), axis, ends)]
  transfers between devices with their start and end apart: 8 -> 8, of which waited for: 4 -> 3; matrix products, arithmetic and copies ran while one was open for 1% -> 1% of each run, Pallas kernels for 3% -> 3%
where the time goes in v8:
time: 20.2 us; the launch traced here: 20.1 us
  starting transfers between devices  11.3 us (56%)
  Pallas kernels  5.35 us (26%)
  waiting for transfers between devices  3.22 us (16%)
    ppermute x8, starting transfers between devices, swap(): return lax.ppermute(blocks.astype(jnp.bfloat16), axis, ends)  11.3 us
    pallas_call x1, Pallas kernels, shards(): pl.pallas_call(lambda *refs: phase_kernel(bits, *refs), out_shape=(jax.Sh...  3.92 us
    ppermute x8, waiting for transfers between devices, swap(): return lax.ppermute(blocks.astype(jnp.bfloat16), axis, ends)  3.22 us
    pallas_call x1, Pallas kernels, shards(): pl.pallas_call(late_kernel, out_shape=jax.ShapeDtypeStruct((1, 2, per_cor...  0.77 us
    pallas_call x1, Pallas kernels, shards(): pl.pallas_call(keep_kernel, out_shape=[jax.ShapeDtypeStruct(shape, jnp.fl...  0.48 us
  transfers between devices with their start and end apart: 8, of which 3 were waited for; matrix products, arithmetic and copies ran while one was open for 1% of the time, Pallas kernels for 3%

profile of v8, /device:TPU:0, one launch (start us, length us, event | category | flops | bytes accessed | tf_op | source)
XLA Modules:
  0.0 20.1 jit_solution(11607269044895928246)
XLA Ops:
  0.0 3.9 %phase_sums.1 = (f32[3,4,256,256]{3,2,1,0:T(8,128)S(1)}, bf16[2,1,2,48,256]{4,3,2,1,0:T(8,128)(2,1)S(1)}, bf16[6,1,2,48,256]{4,3,2,1,0:T(8,128)(2,1)S(1)}, f32[2,2,4]{2,1,0:T(2,128)S(1)}, bf16[96,288]{1,0:T(8,128)(2,1)S(1)}) custom-call(s32[3,8]{1,0:T(4,128)} %refs_0_.1, s32[2,3]{1,0:T(2,128)} %bitcast.1, s32[3,8]{1,0:T(4,128)} %refs_2_.1, s32[3,32]{1,0:T(4,128)} %refs_3_.1, ...), custom_call_target="tpu_custom_call" | custom-call | tf_op jit(solution)/shard_map/phase_sums/pallas_call | solution.py:219
  3.9 0.5 %collective-permute-start.1 = (bf16[2,1,2,48,256]{4,3,2,1,0:T(8,128)(2,1)S(1)}, bf16[2,1,2,48,256]{4,3,2,1,0:T(8,128)(2,1)S(1)}, u32[]{:S(2)}, u32[]{:S(2)}) collective-permute-start(bf16[2,1,2,48,256]{4,3,2,1,0:T(8,128)(2,1)S(1)} %get-tuple-element.18), channel_id=1, source_target_pairs={{0,1},{1,0},{2,3},{3,2},{4,5},{5,4},{6,7},{7,6},{8,9},{9,8},{10,11... | collective-permute-start | bytes 294920 | tf_op jit(solution)/shard_map/ppermute | solution.py:256
  4.4 0.1 collective-permute-start
  4.5 0.5 %own_k_sums.1 = (f32[2,1,2,48,256]{4,3,2,1,0:T(8,128)S(1)}, f32[6,1,2,48,256]{4,3,2,1,0:T(8,128)S(1)}) custom-call(f32[3,4,256,256]{3,2,1,0:T(8,128)S(1)} %get-tuple-element.13.prod_ref, f32[2,2,4]{2,1,0:T(2,128)S(1)} %get-tuple-element.14.turn_ref), custom_call_target="tpu_custom_call" | custom-call | flops 6291456 | bytes 3145728 | tf_op jit(solution)/shard_map/own_k_sums/pallas_call | solution.py:243
  5.0 0.4 %collective-permute-done.1 = bf16[2,1,2,48,256]{4,3,2,1,0:T(8,128)(2,1)S(1)} collective-permute-done((bf16[2,1,2,48,256]{4,3,2,1,0:T(8,128)(2,1)S(1)}, bf16[2,1,2,48,256]{4,3,2,1,0:T(8,128)(2,1)S(1)}, u32[]{:S(2)}, u32[]{:S(2)}) %collective-permute-start.1) | collective-permute-done | bytes 98336 | tf_op jit(solution)/shard_map/ppermute | solution.py:256
  5.4 3.9 %collective-permute-start.2 = (bf16[2,1,2,48,256]{4,3,2,1,0:T(8,128)(2,1)S(1)}, bf16[2,1,2,48,256]{4,3,2,1,0:T(8,128)(2,1)S(1)}, u32[]{:S(2)}, u32[]{:S(2)}) collective-permute-start(bf16[2,1,2,48,256]{4,3,2,1,0:T(8,128)(2,1)S(1)} %add_convert_fusion), channel_id=1, source_target_pairs={{0,6},{2,4},{4,2},{6,0},{8,14},{10,12},{12,10},{14,8},{1,7},{3,5},... | collective-permute-start | bytes 294920 | tf_op jit(solution)/shard_map/ppermute | solution.py:256
  9.4 0.0 collective-permute-done
  9.4 0.1 fusion.3
  9.5 0.6 %collective-permute-start.5 = (bf16[1,1,2,48,256]{4,3,2,1,0:T(8,128)(2,1)S(1)}, bf16[1,1,2,48,256]{4,3,2,1,0:T(8,128)(2,1)S(1)}, u32[]{:S(2)}, u32[]{:S(2)}) collective-permute-start(bf16[1,1,2,48,256]{4,3,2,1,0:T(8,128)(2,1)S(1)} %get-tuple-element.23), channel_id=1, source_target_pairs={{0,2},{2,0},{4,6},{6,4},{8,10},{10,8},{12,14},{14,12},{1,3},{3,1},... | collective-permute-start | bytes 147464 | tf_op jit(solution)/shard_map/ppermute | solution.py:256
  10.1 0.4 %collective-permute-start.6 = (bf16[1,1,2,48,256]{4,3,2,1,0:T(8,128)(2,1)S(1)}, bf16[1,1,2,48,256]{4,3,2,1,0:T(8,128)(2,1)S(1)}, u32[]{:S(2)}, u32[]{:S(2)}) collective-permute-start(bf16[1,1,2,48,256]{4,3,2,1,0:T(8,128)(2,1)S(1)} %get-tuple-element.24), channel_id=1, source_target_pairs={{0,4},{2,6},{4,0},{6,2},{8,12},{10,14},{12,8},{14,10},{1,5},{3,7},... | collective-permute-start | bytes 147464 | tf_op jit(solution)/shard_map/ppermute | solution.py:256
  10.5 1.6 %collective-permute-start.4 = (bf16[1,1,2,48,256]{4,3,2,1,0:T(8,128)(2,1)S(1)}, bf16[1,1,2,48,256]{4,3,2,1,0:T(8,128)(2,1)S(1)}, u32[]{:S(2)}, u32[]{:S(2)}) collective-permute-start(bf16[1,1,2,48,256]{4,3,2,1,0:T(8,128)(2,1)S(1)} %get-tuple-element.25), channel_id=1, source_target_pairs={{0,4},{2,6},{4,0},{6,2},{8,12},{10,14},{12,8},{14,10},{1,5},{3,7},... | collective-permute-start | bytes 147464 | tf_op jit(solution)/shard_map/ppermute | solution.py:256
  12.1 1.5 %collective-permute-start.3 = (bf16[1,1,2,48,256]{4,3,2,1,0:T(8,128)(2,1)S(1)}, bf16[1,1,2,48,256]{4,3,2,1,0:T(8,128)(2,1)S(1)}, u32[]{:S(2)}, u32[]{:S(2)}) collective-permute-start(bf16[1,1,2,48,256]{4,3,2,1,0:T(8,128)(2,1)S(1)} %get-tuple-element.26), channel_id=1, source_target_pairs={{0,2},{2,0},{4,6},{6,4},{8,10},{10,8},{12,14},{14,12},{1,3},{3,1},... | collective-permute-start | bytes 147464 | tf_op jit(solution)/shard_map/ppermute | solution.py:256
  13.6 0.0 collective-permute-done.2
  13.6 0.0 collective-permute-done.5
  13.6 0.6 %collective-permute-done.6 = bf16[1,1,2,48,256]{4,3,2,1,0:T(8,128)(2,1)S(1)} collective-permute-done((bf16[1,1,2,48,256]{4,3,2,1,0:T(8,128)(2,1)S(1)}, bf16[1,1,2,48,256]{4,3,2,1,0:T(8,128)(2,1)S(1)}, u32[]{:S(2)}, u32[]{:S(2)}) %collective-permute-start.6) | collective-permute-done | bytes 49184 | tf_op jit(solution)/shard_map/ppermute | solution.py:256
  14.3 2.7 %collective-permute-start.7 = (bf16[1,1,2,48,256]{4,3,2,1,0:T(8,128)(2,1)S(1)}, bf16[1,1,2,48,256]{4,3,2,1,0:T(8,128)(2,1)S(1)}, u32[]{:S(2)}, u32[]{:S(2)}) collective-permute-start(bf16[1,1,2,48,256]{4,3,2,1,0:T(8,128)(2,1)S(1)} %get-tuple-element.21), channel_id=1, source_target_pairs={{0,8},{2,10},{4,12},{6,14},{8,0},{10,2},{12,4},{14,6},{1,9},{3,11}... | collective-permute-start | bytes 147464 | tf_op jit(solution)/shard_map/ppermute | solution.py:256
  16.9 0.0 collective-permute-done.4.refs_1_
  16.9 0.0 collective-permute-done.3.refs_0_
  16.9 0.2 rotate_early.1.early_ref
  17.1 2.2 %collective-permute-done.7.got_ref = bf16[1,1,2,48,256]{4,3,2,1,0:T(8,128)(2,1)S(1)} collective-permute-done((bf16[1,1,2,48,256]{4,3,2,1,0:T(8,128)(2,1)S(1)}, bf16[1,1,2,48,256]{4,3,2,1,0:T(8,128)(2,1)S(1)}, u32[]{:S(2)}, u32[]{:S(2)}) %collective-permute-start.7) | collective-permute-done | bytes 49184 | tf_op jit(solution)/shard_map/ppermute | solution.py:256
  19.3 0.8 %rotate_last.1 = bf16[1,2,1,48,256]{4,3,2,1,0:T(8,128)(2,1)} custom-call(bf16[96,288]{1,0:T(8,128)(2,1)S(1)} %get-tuple-element.12.mixer_ref, f32[1,96,256]{2,1,0:T(8,128)S(1)} %rotate_early.1.early_ref, bf16[1,1,2,48,256]{4,3,2,1,0:T(8,128)(2,1)S(1)} %collective-permute-done.7.got_ref), custom_call_target="tpu_custom_call" | custom-call | tf_op jit(solution)/shard_map/rotate_last/pallas_call | solution.py:292
  (3 shorter events, 0.1 us)
Async XLA Ops:
  3.9 1.5 %collective-permute-start.1 = (bf16[2,1,2,48,256]{4,3,2,1,0:T(8,128)(2,1)S(1)}, bf16[2,1,2,48,256]{4,3,2,1,0:T(8,128)(2,1)S(1)}, u32[]{:S(2)}, u32[]{:S(2)}) collective-permute-start(bf16[2,1,2,48,256]{4,3,2,1,0:T(8,128)(2,1)S(1)} %get-tuple-element.18), channel_id=1, source_target_pairs={{0,1},{1,0},{2,3},{3,2},{4,5},{5,4},{6,7},{7,6},{8,9},{9,8},{10,11... | collective-permute-start | bytes 294920 | tf_op jit(solution)/shard_map/ppermute | solution.py:256
  4.4 4.9 %collective-permute-start = (bf16[6,1,2,48,256]{4,3,2,1,0:T(8,128)(2,1)S(1)}, bf16[6,1,2,48,256]{4,3,2,1,0:T(8,128)(2,1)S(1)}, u32[]{:S(2)}, u32[]{:S(2)}) collective-permute-start(bf16[6,1,2,48,256]{4,3,2,1,0:T(8,128)(2,1)S(1)} %get-tuple-element.16), channel_id=1, source_target_pairs={{0,1},{1,0},{2,3},{3,2},{4,5},{5,4},{6,7},{7,6},{8,9},{9,8},{10,11... | collective-permute-start | bytes 884744 | tf_op jit(solution)/shard_map/ppermute | solution.py:256
  5.4 8.2 %collective-permute-start.2 = (bf16[2,1,2,48,256]{4,3,2,1,0:T(8,128)(2,1)S(1)}, bf16[2,1,2,48,256]{4,3,2,1,0:T(8,128)(2,1)S(1)}, u32[]{:S(2)}, u32[]{:S(2)}) collective-permute-start(bf16[2,1,2,48,256]{4,3,2,1,0:T(8,128)(2,1)S(1)} %add_convert_fusion), channel_id=1, source_target_pairs={{0,6},{2,4},{4,2},{6,0},{8,14},{10,12},{12,10},{14,8},{1,7},{3,5},... | collective-permute-start | bytes 294920 | tf_op jit(solution)/shard_map/ppermute | solution.py:256
  9.5 4.2 %collective-permute-start.5 = (bf16[1,1,2,48,256]{4,3,2,1,0:T(8,128)(2,1)S(1)}, bf16[1,1,2,48,256]{4,3,2,1,0:T(8,128)(2,1)S(1)}, u32[]{:S(2)}, u32[]{:S(2)}) collective-permute-start(bf16[1,1,2,48,256]{4,3,2,1,0:T(8,128)(2,1)S(1)} %get-tuple-element.23), channel_id=1, source_target_pairs={{0,2},{2,0},{4,6},{6,4},{8,10},{10,8},{12,14},{14,12},{1,3},{3,1},... | collective-permute-start | bytes 147464 | tf_op jit(solution)/shard_map/ppermute | solution.py:256
  10.1 4.2 %collective-permute-start.6 = (bf16[1,1,2,48,256]{4,3,2,1,0:T(8,128)(2,1)S(1)}, bf16[1,1,2,48,256]{4,3,2,1,0:T(8,128)(2,1)S(1)}, u32[]{:S(2)}, u32[]{:S(2)}) collective-permute-start(bf16[1,1,2,48,256]{4,3,2,1,0:T(8,128)(2,1)S(1)} %get-tuple-element.24), channel_id=1, source_target_pairs={{0,4},{2,6},{4,0},{6,2},{8,12},{10,14},{12,8},{14,10},{1,5},{3,7},... | collective-permute-start | bytes 147464 | tf_op jit(solution)/shard_map/ppermute | solution.py:256
  10.5 6.5 %collective-permute-start.4 = (bf16[1,1,2,48,256]{4,3,2,1,0:T(8,128)(2,1)S(1)}, bf16[1,1,2,48,256]{4,3,2,1,0:T(8,128)(2,1)S(1)}, u32[]{:S(2)}, u32[]{:S(2)}) collective-permute-start(bf16[1,1,2,48,256]{4,3,2,1,0:T(8,128)(2,1)S(1)} %get-tuple-element.25), channel_id=1, source_target_pairs={{0,4},{2,6},{4,0},{6,2},{8,12},{10,14},{12,8},{14,10},{1,5},{3,7},... | collective-permute-start | bytes 147464 | tf_op jit(solution)/shard_map/ppermute | solution.py:256
  12.1 4.8 %collective-permute-start.3 = (bf16[1,1,2,48,256]{4,3,2,1,0:T(8,128)(2,1)S(1)}, bf16[1,1,2,48,256]{4,3,2,1,0:T(8,128)(2,1)S(1)}, u32[]{:S(2)}, u32[]{:S(2)}) collective-permute-start(bf16[1,1,2,48,256]{4,3,2,1,0:T(8,128)(2,1)S(1)} %get-tuple-element.26), channel_id=1, source_target_pairs={{0,2},{2,0},{4,6},{6,4},{8,10},{10,8},{12,14},{14,12},{1,3},{3,1},... | collective-permute-start | bytes 147464 | tf_op jit(solution)/shard_map/ppermute | solution.py:256
  14.3 5.1 %collective-permute-start.7 = (bf16[1,1,2,48,256]{4,3,2,1,0:T(8,128)(2,1)S(1)}, bf16[1,1,2,48,256]{4,3,2,1,0:T(8,128)(2,1)S(1)}, u32[]{:S(2)}, u32[]{:S(2)}) collective-permute-start(bf16[1,1,2,48,256]{4,3,2,1,0:T(8,128)(2,1)S(1)} %get-tuple-element.21), channel_id=1, source_target_pairs={{0,8},{2,10},{4,12},{6,14},{8,0},{10,2},{12,4},{14,6},{1,9},{3,11}... | collective-permute-start | bytes 147464 | tf_op jit(solution)/shard_map/ppermute | solution.py:256

commit v9 on v7

--- a/solution.py
+++ b/solution.py
@@ -9,7 +9,7 @@
 
 NFINE = 48
 NEAR = 2
-PIECES = 2
+PIECES = 4
 ROWS = 16
 
 

time: 20.2 us -> 20.2 us (level)
  no operation moved by 1% of the time
where the time goes in v9:
time: 20.2 us; the launch traced here: 20 us
  starting transfers between devices  11.5 us (57%)
  Pallas kernels  5.38 us (27%)
  waiting for transfers between devices  2.98 us (15%)
    ppermute x8, starting transfers between devices, swap(): return lax.ppermute(blocks.astype(jnp.bfloat16), axis, ends)  11.5 us
    pallas_call x1, Pallas kernels, shards(): pl.pallas_call(lambda *refs: phase_kernel(bits, *refs), out_shape=(jax.Sh...  3.95 us
    ppermute x8, waiting for transfers between devices, swap(): return lax.ppermute(blocks.astype(jnp.bfloat16), axis, ends)  2.98 us
    pallas_call x1, Pallas kernels, shards(): pl.pallas_call(late_kernel, out_shape=jax.ShapeDtypeStruct((1, 2, per_cor...  0.77 us
    pallas_call x1, Pallas kernels, shards(): pl.pallas_call(keep_kernel, out_shape=[jax.ShapeDtypeStruct(shape, jnp.fl...  0.48 us
  transfers between devices with their start and end apart: 8, of which 4 were waited for; matrix products, arithmetic and copies ran while one was open for 1% of the time, Pallas kernels for 3%

profile of v9, /device:TPU:0, one launch (start us, length us, event | category | flops | bytes accessed | tf_op | source)
XLA Modules:
  0.0 20.0 jit_solution(9700253745327320243)
XLA Ops:
  0.0 3.9 %phase_sums.1 = (f32[3,4,256,256]{3,2,1,0:T(8,128)S(1)}, bf16[2,1,2,48,256]{4,3,2,1,0:T(8,128)(2,1)S(1)}, bf16[6,1,2,48,256]{4,3,2,1,0:T(8,128)(2,1)S(1)}, f32[2,2,4]{2,1,0:T(2,128)S(1)}, bf16[96,288]{1,0:T(8,128)(2,1)S(1)}) custom-call(s32[3,8]{1,0:T(4,128)} %refs_0_.1, s32[2,3]{1,0:T(2,128)} %bitcast.1, s32[3,8]{1,0:T(4,128)} %refs_2_.1, s32[3,32]{1,0:T(4,128)} %refs_3_.1, ...), custom_call_target="tpu_custom_call" | custom-call | tf_op jit(solution)/shard_map/phase_sums/pallas_call | solution.py:219
  4.0 0.5 %collective-permute-start.1 = (bf16[2,1,2,48,256]{4,3,2,1,0:T(8,128)(2,1)S(1)}, bf16[2,1,2,48,256]{4,3,2,1,0:T(8,128)(2,1)S(1)}, u32[]{:S(2)}, u32[]{:S(2)}) collective-permute-start(bf16[2,1,2,48,256]{4,3,2,1,0:T(8,128)(2,1)S(1)} %get-tuple-element.18), channel_id=1, source_target_pairs={{0,1},{1,0},{2,3},{3,2},{4,5},{5,4},{6,7},{7,6},{8,9},{9,8},{10,11... | collective-permute-start | bytes 294920 | tf_op jit(solution)/shard_map/ppermute | solution.py:256
  4.5 0.1 collective-permute-start
  4.6 0.5 %own_k_sums.1 = (f32[2,1,2,48,256]{4,3,2,1,0:T(8,128)S(1)}, f32[6,1,2,48,256]{4,3,2,1,0:T(8,128)S(1)}) custom-call(f32[3,4,256,256]{3,2,1,0:T(8,128)S(1)} %get-tuple-element.13.prod_ref, f32[2,2,4]{2,1,0:T(2,128)S(1)} %get-tuple-element.14.turn_ref), custom_call_target="tpu_custom_call" | custom-call | flops 6291456 | bytes 3145728 | tf_op jit(solution)/shard_map/own_k_sums/pallas_call | solution.py:243
  5.0 0.4 %collective-permute-done.1 = bf16[2,1,2,48,256]{4,3,2,1,0:T(8,128)(2,1)S(1)} collective-permute-done((bf16[2,1,2,48,256]{4,3,2,1,0:T(8,128)(2,1)S(1)}, bf16[2,1,2,48,256]{4,3,2,1,0:T(8,128)(2,1)S(1)}, u32[]{:S(2)}, u32[]{:S(2)}) %collective-permute-start.1) | collective-permute-done | bytes 98336 | tf_op jit(solution)/shard_map/ppermute | solution.py:256
  5.4 4.0 %collective-permute-start.2 = (bf16[2,1,2,48,256]{4,3,2,1,0:T(8,128)(2,1)S(1)}, bf16[2,1,2,48,256]{4,3,2,1,0:T(8,128)(2,1)S(1)}, u32[]{:S(2)}, u32[]{:S(2)}) collective-permute-start(bf16[2,1,2,48,256]{4,3,2,1,0:T(8,128)(2,1)S(1)} %add_convert_fusion), channel_id=1, source_target_pairs={{0,6},{2,4},{4,2},{6,0},{8,14},{10,12},{12,10},{14,8},{1,7},{3,5},... | collective-permute-start | bytes 294920 | tf_op jit(solution)/shard_map/ppermute | solution.py:256
  9.4 0.0 collective-permute-done
  9.4 0.1 fusion.3
  9.5 0.5 %collective-permute-start.5 = (bf16[1,1,2,48,256]{4,3,2,1,0:T(8,128)(2,1)S(1)}, bf16[1,1,2,48,256]{4,3,2,1,0:T(8,128)(2,1)S(1)}, u32[]{:S(2)}, u32[]{:S(2)}) collective-permute-start(bf16[1,1,2,48,256]{4,3,2,1,0:T(8,128)(2,1)S(1)} %get-tuple-element.23), channel_id=1, source_target_pairs={{0,4},{2,6},{4,0},{6,2},{8,12},{10,14},{12,8},{14,10},{1,5},{3,7},... | collective-permute-start | bytes 147464 | tf_op jit(solution)/shard_map/ppermute | solution.py:256
  10.0 0.5 %collective-permute-start.6 = (bf16[1,1,2,48,256]{4,3,2,1,0:T(8,128)(2,1)S(1)}, bf16[1,1,2,48,256]{4,3,2,1,0:T(8,128)(2,1)S(1)}, u32[]{:S(2)}, u32[]{:S(2)}) collective-permute-start(bf16[1,1,2,48,256]{4,3,2,1,0:T(8,128)(2,1)S(1)} %get-tuple-element.24), channel_id=1, source_target_pairs={{0,2},{2,0},{4,6},{6,4},{8,10},{10,8},{12,14},{14,12},{1,3},{3,1},... | collective-permute-start | bytes 147464 | tf_op jit(solution)/shard_map/ppermute | solution.py:256
  10.5 1.6 %collective-permute-start.4 = (bf16[1,1,2,48,256]{4,3,2,1,0:T(8,128)(2,1)S(1)}, bf16[1,1,2,48,256]{4,3,2,1,0:T(8,128)(2,1)S(1)}, u32[]{:S(2)}, u32[]{:S(2)}) collective-permute-start(bf16[1,1,2,48,256]{4,3,2,1,0:T(8,128)(2,1)S(1)} %get-tuple-element.25), channel_id=1, source_target_pairs={{0,2},{2,0},{4,6},{6,4},{8,10},{10,8},{12,14},{14,12},{1,3},{3,1},... | collective-permute-start | bytes 147464 | tf_op jit(solution)/shard_map/ppermute | solution.py:256
  12.1 1.6 %collective-permute-start.3 = (bf16[1,1,2,48,256]{4,3,2,1,0:T(8,128)(2,1)S(1)}, bf16[1,1,2,48,256]{4,3,2,1,0:T(8,128)(2,1)S(1)}, u32[]{:S(2)}, u32[]{:S(2)}) collective-permute-start(bf16[1,1,2,48,256]{4,3,2,1,0:T(8,128)(2,1)S(1)} %get-tuple-element.26), channel_id=1, source_target_pairs={{0,4},{2,6},{4,0},{6,2},{8,12},{10,14},{12,8},{14,10},{1,5},{3,7},... | collective-permute-start | bytes 147464 | tf_op jit(solution)/shard_map/ppermute | solution.py:256
  13.6 0.0 collective-permute-done.2
  13.6 0.1 collective-permute-done.5
  13.7 0.5 %collective-permute-done.6 = bf16[1,1,2,48,256]{4,3,2,1,0:T(8,128)(2,1)S(1)} collective-permute-done((bf16[1,1,2,48,256]{4,3,2,1,0:T(8,128)(2,1)S(1)}, bf16[1,1,2,48,256]{4,3,2,1,0:T(8,128)(2,1)S(1)}, u32[]{:S(2)}, u32[]{:S(2)}) %collective-permute-start.6) | collective-permute-done | bytes 49184 | tf_op jit(solution)/shard_map/ppermute | solution.py:256
  14.2 2.8 %collective-permute-start.7 = (bf16[1,1,2,48,256]{4,3,2,1,0:T(8,128)(2,1)S(1)}, bf16[1,1,2,48,256]{4,3,2,1,0:T(8,128)(2,1)S(1)}, u32[]{:S(2)}, u32[]{:S(2)}) collective-permute-start(bf16[1,1,2,48,256]{4,3,2,1,0:T(8,128)(2,1)S(1)} %get-tuple-element.21), channel_id=1, source_target_pairs={{0,8},{2,10},{4,12},{6,14},{8,0},{10,2},{12,4},{14,6},{1,9},{3,11}... | collective-permute-start | bytes 147464 | tf_op jit(solution)/shard_map/ppermute | solution.py:256
  17.0 0.0 collective-permute-done.4.refs_1_
  17.0 0.0 collective-permute-done.3.refs_0_
  17.0 0.2 rotate_early.1.early_ref
  17.2 2.0 %collective-permute-done.7.got_ref = bf16[1,1,2,48,256]{4,3,2,1,0:T(8,128)(2,1)S(1)} collective-permute-done((bf16[1,1,2,48,256]{4,3,2,1,0:T(8,128)(2,1)S(1)}, bf16[1,1,2,48,256]{4,3,2,1,0:T(8,128)(2,1)S(1)}, u32[]{:S(2)}, u32[]{:S(2)}) %collective-permute-start.7) | collective-permute-done | bytes 49184 | tf_op jit(solution)/shard_map/ppermute | solution.py:256
  19.3 0.8 %rotate_last.1 = bf16[1,2,1,48,256]{4,3,2,1,0:T(8,128)(2,1)} custom-call(bf16[96,288]{1,0:T(8,128)(2,1)S(1)} %get-tuple-element.12.mixer_ref, f32[1,96,256]{2,1,0:T(8,128)S(1)} %rotate_early.1.early_ref, bf16[1,1,2,48,256]{4,3,2,1,0:T(8,128)(2,1)S(1)} %collective-permute-done.7.got_ref), custom_call_target="tpu_custom_call" | custom-call | tf_op jit(solution)/shard_map/rotate_last/pallas_call | solution.py:292
  (3 shorter events, 0.1 us)
Async XLA Ops:
  4.0 1.5 %collective-permute-start.1 = (bf16[2,1,2,48,256]{4,3,2,1,0:T(8,128)(2,1)S(1)}, bf16[2,1,2,48,256]{4,3,2,1,0:T(8,128)(2,1)S(1)}, u32[]{:S(2)}, u32[]{:S(2)}) collective-permute-start(bf16[2,1,2,48,256]{4,3,2,1,0:T(8,128)(2,1)S(1)} %get-tuple-element.18), channel_id=1, source_target_pairs={{0,1},{1,0},{2,3},{3,2},{4,5},{5,4},{6,7},{7,6},{8,9},{9,8},{10,11... | collective-permute-start | bytes 294920 | tf_op jit(solution)/shard_map/ppermute | solution.py:256
  4.5 4.9 %collective-permute-start = (bf16[6,1,2,48,256]{4,3,2,1,0:T(8,128)(2,1)S(1)}, bf16[6,1,2,48,256]{4,3,2,1,0:T(8,128)(2,1)S(1)}, u32[]{:S(2)}, u32[]{:S(2)}) collective-permute-start(bf16[6,1,2,48,256]{4,3,2,1,0:T(8,128)(2,1)S(1)} %get-tuple-element.16), channel_id=1, source_target_pairs={{0,1},{1,0},{2,3},{3,2},{4,5},{5,4},{6,7},{7,6},{8,9},{9,8},{10,11... | collective-permute-start | bytes 884744 | tf_op jit(solution)/shard_map/ppermute | solution.py:256
  5.4 8.2 %collective-permute-start.2 = (bf16[2,1,2,48,256]{4,3,2,1,0:T(8,128)(2,1)S(1)}, bf16[2,1,2,48,256]{4,3,2,1,0:T(8,128)(2,1)S(1)}, u32[]{:S(2)}, u32[]{:S(2)}) collective-permute-start(bf16[2,1,2,48,256]{4,3,2,1,0:T(8,128)(2,1)S(1)} %add_convert_fusion), channel_id=1, source_target_pairs={{0,6},{2,4},{4,2},{6,0},{8,14},{10,12},{12,10},{14,8},{1,7},{3,5},... | collective-permute-start | bytes 294920 | tf_op jit(solution)/shard_map/ppermute | solution.py:256
  9.5 4.2 %collective-permute-start.5 = (bf16[1,1,2,48,256]{4,3,2,1,0:T(8,128)(2,1)S(1)}, bf16[1,1,2,48,256]{4,3,2,1,0:T(8,128)(2,1)S(1)}, u32[]{:S(2)}, u32[]{:S(2)}) collective-permute-start(bf16[1,1,2,48,256]{4,3,2,1,0:T(8,128)(2,1)S(1)} %get-tuple-element.23), channel_id=1, source_target_pairs={{0,4},{2,6},{4,0},{6,2},{8,12},{10,14},{12,8},{14,10},{1,5},{3,7},... | collective-permute-start | bytes 147464 | tf_op jit(solution)/shard_map/ppermute | solution.py:256
  10.0 4.1 %collective-permute-start.6 = (bf16[1,1,2,48,256]{4,3,2,1,0:T(8,128)(2,1)S(1)}, bf16[1,1,2,48,256]{4,3,2,1,0:T(8,128)(2,1)S(1)}, u32[]{:S(2)}, u32[]{:S(2)}) collective-permute-start(bf16[1,1,2,48,256]{4,3,2,1,0:T(8,128)(2,1)S(1)} %get-tuple-element.24), channel_id=1, source_target_pairs={{0,2},{2,0},{4,6},{6,4},{8,10},{10,8},{12,14},{14,12},{1,3},{3,1},... | collective-permute-start | bytes 147464 | tf_op jit(solution)/shard_map/ppermute | solution.py:256
  10.5 6.5 %collective-permute-start.4 = (bf16[1,1,2,48,256]{4,3,2,1,0:T(8,128)(2,1)S(1)}, bf16[1,1,2,48,256]{4,3,2,1,0:T(8,128)(2,1)S(1)}, u32[]{:S(2)}, u32[]{:S(2)}) collective-permute-start(bf16[1,1,2,48,256]{4,3,2,1,0:T(8,128)(2,1)S(1)} %get-tuple-element.25), channel_id=1, source_target_pairs={{0,2},{2,0},{4,6},{6,4},{8,10},{10,8},{12,14},{14,12},{1,3},{3,1},... | collective-permute-start | bytes 147464 | tf_op jit(solution)/shard_map/ppermute | solution.py:256
  12.1 5.0 %collective-permute-start.3 = (bf16[1,1,2,48,256]{4,3,2,1,0:T(8,128)(2,1)S(1)}, bf16[1,1,2,48,256]{4,3,2,1,0:T(8,128)(2,1)S(1)}, u32[]{:S(2)}, u32[]{:S(2)}) collective-permute-start(bf16[1,1,2,48,256]{4,3,2,1,0:T(8,128)(2,1)S(1)} %get-tuple-element.26), channel_id=1, source_target_pairs={{0,4},{2,6},{4,0},{6,2},{8,12},{10,14},{12,8},{14,10},{1,5},{3,7},... | collective-permute-start | bytes 147464 | tf_op jit(solution)/shard_map/ppermute | solution.py:256
  14.2 5.1 %collective-permute-start.7 = (bf16[1,1,2,48,256]{4,3,2,1,0:T(8,128)(2,1)S(1)}, bf16[1,1,2,48,256]{4,3,2,1,0:T(8,128)(2,1)S(1)}, u32[]{:S(2)}, u32[]{:S(2)}) collective-permute-start(bf16[1,1,2,48,256]{4,3,2,1,0:T(8,128)(2,1)S(1)} %get-tuple-element.21), channel_id=1, source_target_pairs={{0,8},{2,10},{4,12},{6,14},{8,0},{10,2},{12,4},{14,6},{1,9},{3,11}... | collective-permute-start | bytes 147464 | tf_op jit(solution)/shard_map/ppermute | solution.py:256
